TPU v7x, 32 devices: a whole 2x2x4 slice. The times are simulated.
32 devices in a mesh: wide: 8 (over z, y), narrow: 4 (over x, core).
Axes of the slice: x: 2, y: 2, z: 4, core: 2. Of those that a mesh axis runs over, the one named last changes fastest.
Arguments:
- layer_input_rows: bfloat16 [16384, 4096], P('wide', 'narrow'), may hold values from -6 to 6
- output_gradient_rows: bfloat16 [16384, 4096], P('wide', 'narrow'), may hold values from -60 to 60
- adapter_up_weight: bfloat16 [4096, 128], P('narrow'), may hold values from -0.09375 to 0.09375
- input_side_projection: bfloat16 [4096, 128], P('narrow'), may hold values from -0.09375 to 0.09375
- rank_side_projection: bfloat16 [128, 64], replicated, may hold values from -6 to 6
- lengths: int32 [512], P('wide'), may hold values from 1 to 32, 10240 in all
- program_output_index: int32 [512], replicated, may hold values from 0 to 511, each once
- targets: bfloat16 [16384, 8192], P('wide', 'narrow'), may hold values from -650 to 650
Outputs:
- scores: float32 [512, 16384], P('narrow', 'wide')
Inputs may be any that keep to these rules, and one draw needn't show every extreme that they name: Program s uses its first lengths[s] token rows; some program uses all 32. `program_output_index`: each output row is named by exactly one program.
All inputs are finite; a program needn't handle non-finite values. No bound on the sum of `lengths` on one device may be relied on, other than what follows from the above.
Results may differ from a plain program's by a relative error of at most 0.025.
Values may be sent and summed in bfloat16 or wider, within the bound.
No kernel may reach another device: no remote copies, remote signals or barrier semaphores. Data moves between devices by JAX's collectives and lax.ppermute only.
A program may use at most 128 MiB of HBM per device.

v0:
```python
import math

import jax
import jax.numpy as jnp
from jax import lax
from jax.sharding import PartitionSpec as P

epsilon = 1e-06


def program_features(out_side, in_side, lengths, length):
    programs = lengths.shape[0]
    positions = lax.broadcasted_iota(jnp.int32, (programs, length), 1)
    live_rows = (positions < lengths[:, None]).astype(jnp.float32)
    weighted = out_side.reshape(programs, length, -1) * live_rows[:, :, None]
    inputs = in_side.reshape(programs, length, -1)
    outer_sum = jnp.einsum("sla,slb->sab", weighted, inputs, precision=lax.Precision.HIGHEST)
    return outer_sum.reshape(programs, -1)


def normalize_rows(features, squares):
    return (features * lax.rsqrt(squares + epsilon)[:, None]).astype(jnp.bfloat16)


def shards(
    layer_input_rows,
    output_gradient_rows,
    adapter_up_weight,
    input_side_projection,
    rank_side_projection,
    lengths,
    program_output_index,
    targets,
):
    narrow_count = lax.axis_size("narrow")
    narrow_index = lax.axis_index("narrow")
    programs = lengths.shape[0]
    length = layer_input_rows.shape[0] // programs
    reduced_sums = jnp.dot(
        output_gradient_rows, adapter_up_weight, preferred_element_type=jnp.float32
    )
    out_part = jnp.dot(
        reduced_sums, rank_side_projection.astype(jnp.float32), precision=lax.Precision.HIGHEST
    )
    in_part = jnp.dot(layer_input_rows, input_side_projection, preferred_element_type=jnp.float32)
    target_wide = targets.astype(jnp.float32)
    target_squares = jnp.sum(target_wide * target_wide, axis=1)
    out_all, in_all = (
        lax.psum(out_part.astype(jnp.bfloat16), "narrow").astype(jnp.float32),
        lax.psum(in_part.astype(jnp.bfloat16), "narrow").astype(jnp.float32),
    )
    quarter_cols = out_all.shape[1] // narrow_count
    quarter = lax.dynamic_slice_in_dim(out_all, narrow_index * quarter_cols, quarter_cols, 1)
    features = program_features(quarter, in_all, lengths, length)
    squares = jnp.sum(features * features, axis=1)
    squares, target_squares = lax.psum((squares, target_squares), "narrow")
    unit_rows = normalize_rows(features, squares)
    target_unit = normalize_rows(target_wide, target_squares)
    row_order = jnp.argsort(program_output_index)
    contract = (((1,), (1,)), ((), ()))
    root_count = math.sqrt(float(targets.shape[1] * narrow_count))
    gathered = lax.all_gather(unit_rows, "wide", axis=0, tiled=True)
    permuted = jnp.take(gathered, row_order, axis=0)
    summed = lax.psum_scatter(
        lax.dot_general(permuted, target_unit, contract, preferred_element_type=jnp.float32).astype(
            jnp.bfloat16
        ),
        "narrow",
        scatter_dimension=0,
        tiled=True,
    ).astype(jnp.float32)
    return summed * root_count


def solution(mesh):
    return jax.shard_map(
        shards,
        mesh=mesh,
        in_specs=(
            P("wide", "narrow"),
            P("wide", "narrow"),
            P("narrow", None),
            P("narrow", None),
            P(),
            P("wide"),
            P(),
            P("wide", "narrow"),
        ),
        out_specs=P("narrow", "wide"),
        check_vma=False,
    )
```

profile of v0, /device:TPU:0, one launch (start us, length us, event | category | flops | bytes accessed | tf_op | source)
XLA Modules:
  0.0 166.4 jit_solution(2211801514592933268)
XLA Ops:
  6.5 0.0 copy-start
  6.5 0.0 copy-start.2
  6.5 0.0 all-reduce.4.cloned.1.call-start
  6.5 0.9 copy-done
  7.5 0.0 copy-start.1
  7.5 4.4 %convolution_convert_fusion = bf16[2048,128]{1,0:T(8,128)(2,1)} fusion(bf16[2048,1024]{1,0:T(8,128)(2,1)} %param.8, bf16[1024,128]{1,0:T(8,128)(2,1)S(1)} %copy-done), kind=kOutput, calls=%fused_computation.8 | convolution fusion | flops 537133056 | bytes 4980736 | tf_op jit(solution)/shard_map/dot_general | solution.py:45
  11.9 0.0 copy-done.2
  11.9 0.0 copy-done.1
  11.9 0.0 copy-start.3
  11.9 1.3 fusion.16
  13.1 0.0 copy-done.3
  13.1 1.5 convolution_convert_fusion.1
  14.6 0.0 all-reduce.4.cloned.1.call-update
  14.6 0.0 copy-start.5
  14.6 0.0 all-gather.2.cloned.1.call-start
  14.7 5.1 %fusion = f32[2048]{0:T(1024)S(1)} fusion(bf16[2048,2048]{1,0:T(8,128)(2,1)} %param.15), kind=kLoop, calls=%fused_computation.3 | loop fusion | flops 12580864 | bytes 8396800 | tf_op jit(solution)/shard_map/reduce_sum | solution.py:47
  19.8 0.0 copy-start.4
  19.8 0.0 copy-done.5
  19.8 0.1 fusion.14
  19.9 32.3 %all-reduce.4.cloned.1.call-done = (bf16[64,32,128]{2,1,0:T(8,128)(2,1)}, bf16[2048,64]{0,1:T(8,128)(2,1)}) async-done(((bf16[64,32,128]{2,1,0:T(8,128)(2,1)}, bf16[2048,64]{0,1:T(8,128)(2,1)}), (bf16[64,32,128]{2,1,0:T(8,128)(2,1)}, bf16[2048,64]{0,1:T(8,128)(2,1)})) %all-reduce.4.cloned.1.call-update) | async-done | bytes 786448 | tf_op jit(solution)/shard_map/psum | solution.py:50
  52.1 0.8 dynamic-slice_convert_fusion
  53.0 0.2 reshape.36
  53.2 2.3 %multiply_reduce_fusion = (f32[64]{0:T(128)S(1)}, f32[64,16,128]{2,1,0:T(8,128)S(1)}) fusion(bf16[64,32,128]{2,1,0:T(8,128)(2,1)} %get-tuple-element.9, f32[64,32,16]{1,0,2:T(8,128)S(1)} %broadcast_multiply_fusion), kind=kOutput, calls=%fused_computation.18 | convolution fusion | flops 50593728 | bytes 1179904 | tf_op jit(solution)/shard_map/sla,slb->sab/dot_general | solution.py:17
  55.5 6.0 %all-reduce = (f32[2048]{0:T(1024)S(1)}, f32[64]{0:T(128)S(1)}) all-reduce(f32[2048]{0:T(1024)S(1)} %fusion, f32[64]{0:T(128)S(1)} %get-tuple-element.11), channel_id=1, replica_groups=mesh['wide'=8,'narrow'=4] {'narrow'}, use_global_device_ids=true, to_apply=%region_6.0 | all-reduce | flops 2112 | bytes 16896 | tf_op jit(solution)/shard_map/psum | solution.py:56
  61.6 0.9 fusion.11
  62.4 0.0 all-gather.2.cloned.1.call-update
  62.5 0.2 reduce-scatter.2.cloned.1.call-start
  62.7 0.0 copy-done.4
  62.7 3.8 %sort.17 = (s32[512]{0:T(512)}, s32[512]{0:T(512)S(1)}) sort(s32[512]{0:T(512)S(1)} %copy-done.4, s32[512]{0:T(512)S(1)} %iota.11), dimensions={0}, to_apply=%region_0.0 | sort | flops 4608 | bytes 8192 | tf_op jit(solution)/shard_map/jit(argsort)/sort | solution.py:59
  66.5 45.4 %all-gather.2.cloned.1.call-done = bf16[512,2048]{1,0:T(8,128)(2,1)} async-done(((bf16[64,2048]{1,0:T(8,128)(2,1)}), bf16[512,2048]{1,0:T(8,128)(2,1)}) %all-gather.2.cloned.1.call-update) | async-done | bytes 2097168 | tf_op jit(solution)/shard_map/all_gather | solution.py:62
  111.9 6.3 %gather_fusion = bf16[512,2048]{1,0:T(8,128)(2,1)S(1)} fusion(bf16[512,2048]{1,0:T(8,128)(2,1)} %all-gather.2.cloned.1.call-done, s32[1024]{0:T(1024)S(1)} %pad_clamp_fusion), kind=kCustom, calls=%fused_computation | custom fusion | bytes 4196352 | tf_op jit(solution)/shard_map/jit(_take)/gather | solution.py:63
  118.2 9.4 %fusion.5 = bf16[512,2048]{1,0:T(8,128)(2,1)} fusion(bf16[2048,2048]{1,0:T(8,128)(2,1)} %param.15, f32[2048]{0:T(1024)S(1)} %add_rsqrt_fusion, bf16[512,2048]{1,0:T(8,128)(2,1)S(1)} %gather_fusion, pred[512]{0:T(512)(128)(4,1)S(1)} %compare_and_fusion), kind=kOutput, calls=%fused_computation.7 | convolution fusion | flops 4309647360 | bytes 12591616 | tf_op jit(solution)/shard_map/dot_general | solution.py:65
  127.6 0.0 reduce-scatter.2.cloned.1.call-update
  127.7 30.1 %reduce-scatter.2.cloned.1.call-done = bf16[128,2048]{1,0:T(8,128)(2,1)} async-done(((bf16[512,2048]{1,0:T(8,128)(2,1)}), bf16[128,2048]{1,0:T(8,128)(2,1)}) %reduce-scatter.2.cloned.1.call-update) | async-done | bytes 524304 | tf_op jit(solution)/shard_map/reduce_scatter | solution.py:64
  157.7 2.1 %convert_multiply_fusion.2 = f32[128,2048]{1,0:T(8,128)} fusion(bf16[128,2048]{1,0:T(8,128)(2,1)} %reduce-scatter.2.cloned.1.call-done), kind=kLoop, calls=%fused_computation.12 | loop fusion | flops 524288 | bytes 1572864 | tf_op jit(solution)/shard_map/mul | solution.py:72
  (7 shorter events, 0.1 us)
Async XLA Ops:
  6.5 1.0 copy-start
  6.5 5.3 %copy-start.2 = (bf16[1024,128]{1,0:T(8,128)(2,1)S(1)}, bf16[1024,128]{1,0:T(8,128)(2,1)}, u32[]{:S(2)}) copy-start(bf16[1024,128]{1,0:T(8,128)(2,1)} %param.10) | copy-start | bytes 786436
  6.5 45.6 %all-reduce.4.cloned.1.call-start = ((), (), s32[]{:S(2)}) async-start(), calls=%async_computation.3 | async-start | bytes 1572864 | tf_op jit(solution)/shard_map/psum | solution.py:50
  7.5 4.4 %copy-start.1 = (bf16[2048,1024]{1,0:T(8,128)(2,1)S(1)}, bf16[2048,1024]{1,0:T(8,128)(2,1)}, u32[]{:S(2)}) copy-start(bf16[2048,1024]{1,0:T(8,128)(2,1)} %param.9) | copy-start | bytes 12582916
  11.9 1.3 copy-start.3
  14.6 5.2 %copy-start.5 = (s32[64]{0:T(128)S(1)}, s32[64]{0:T(128)}, u32[]{:S(2)}) copy-start(s32[64]{0:T(128)} %param.13) | copy-start | bytes 772
  14.6 97.3 %all-gather.2.cloned.1.call-start = ((), (), s32[]{:S(2)}) async-start(), calls=%async_computation.1 | async-start | bytes 2359296 | tf_op jit(solution)/shard_map/all_gather | solution.py:62
  19.8 42.9 %copy-start.4 = (s32[512]{0:T(512)S(1)}, s32[512]{0:T(512)}, u32[]{:S(2)}) copy-start(s32[512]{0:T(512)} %param.14) | copy-start | bytes 6148
  62.5 95.3 %reduce-scatter.2.cloned.1.call-start = ((), (), s32[]{:S(2)}) async-start(), calls=%async_computation.2 | async-start | bytes 2621440 | tf_op jit(solution)/shard_map/reduce_scatter | solution.py:64
Sparse Core Ops, SparseCore 0:
  14.8 37.3 all-reduce.3
  62.6 49.2 all-gather.1
  127.8 29.8 reduce-scatter.1
where the time goes:
time: 167 us; the launch traced here: 166 us
  waiting for transfers between devices  108 us (65%)
  matrix products  18.8 us (11%)
  between operations  13.2 us (8%)
  other arithmetic  12.9 us (8%)
  local copies, waits for them, and re-layouts  7.4 us (4%)
  blocking collectives  6.04 us (4%)
    all_gather x1, waiting for transfers between devices, shards(): gathered = lax.all_gather(unit_rows, 'wide', axis=0, tiled=True)  45.4 us
    psum x1, waiting for transfers between devices, shards(): lax.psum(in_part.astype(jnp.bfloat16), 'narrow').astype(jnp.float32)  32.3 us
    reduce_scatter x1, waiting for transfers between devices, shards(): lax.psum_scatter(lax.dot_general(permuted, target_unit, contract, preferr...  30.1 us
    dot_general x1, matrix products, shards(): lax.dot_general(permuted, target_unit, contract, preferred_element_type=j...  9.45 us
    gather x1, local copies, waits for them, and re-layouts, shards(): permuted = jnp.take(gathered, row_order, axis=0)  6.27 us
    psum x1, blocking collectives, shards(): squares, target_squares = lax.psum((squares, target_squares), 'narrow')  6.04 us
    reduce_sum x1, other arithmetic, shards(): target_squares = jnp.sum(target_wide * target_wide, axis=1)  5.08 us
    dot_general x1, matrix products, shards(): jnp.dot(layer_input_rows, input_side_projection, preferred_element_type=j...  4.38 us
  transfers between devices with their start and end apart: 3, of which 3 were waited for; matrix products, arithmetic and copies ran while one was open for 5% of the time, Pallas kernels for 0%

commit v1 on v0

v1 whole, which is shorter than its diff:
```python
import math

import jax
import jax.numpy as jnp
from jax import lax
from jax.sharding import PartitionSpec as P

epsilon = 1e-06


def exchange(array, axis, bit):
    count = lax.axis_size(axis)
    return lax.ppermute(array, axis, [(i, i ^ bit) for i in range(count)])


def pick(array, index):
    return lax.dynamic_index_in_dim(array, index, 0, keepdims=False)


def gather_blocks(block):
    count = lax.axis_size("wide")
    held = {0: block}
    bit = count // 2
    while bit:
        for k in list(held):
            held[k | bit] = exchange(held[k], "wide", bit)
        bit //= 2
    return [held[k] for k in range(count)]


def shards(
    layer_input_rows,
    output_gradient_rows,
    adapter_up_weight,
    input_side_projection,
    rank_side_projection,
    lengths,
    program_output_index,
    targets,
):
    f32, bf16 = jnp.float32, jnp.bfloat16
    wide_count, narrow_count = lax.axis_size("wide"), lax.axis_size("narrow")
    w, n = lax.axis_index("wide"), lax.axis_index("narrow")
    core, x = n % 2, n // 2
    programs = lengths.shape[0]
    length = layer_input_rows.shape[0] // programs
    in_width = input_side_projection.shape[1]
    out_width = rank_side_projection.shape[1]
    quarter = out_width // narrow_count
    half = programs // 2

    reduced = jnp.dot(output_gradient_rows, adapter_up_weight, preferred_element_type=f32)
    out_part = jnp.dot(reduced, rank_side_projection.astype(f32), precision=lax.Precision.HIGHEST)
    in_part = jnp.dot(layer_input_rows, input_side_projection, preferred_element_type=f32)
    both = jnp.concatenate([in_part, out_part], axis=1).astype(bf16)
    both = both.reshape(2, half * length, in_width + out_width)

    chip = pick(both, core).astype(f32) + exchange(pick(both, 1 - core), "narrow", 1).astype(f32)
    chip_in = chip[:, :in_width]
    chip_out = chip[:, in_width:].reshape(-1, 2, 2 * quarter).transpose(1, 0, 2)
    sent = jnp.concatenate([chip_in, pick(chip_out, 1 - x)], axis=1).astype(bf16)
    came = exchange(sent, "narrow", 2).astype(f32)
    in_sum = chip_in + came[:, :in_width]
    out_sum = pick(chip_out, x) + came[:, in_width:]

    half_lengths = pick(lengths.reshape(2, half), core)
    live = lax.broadcasted_iota(jnp.int32, (half, length), 1) < half_lengths[:, None]
    weighted = out_sum.reshape(half, length, -1) * live[:, :, None].astype(f32)
    features = jnp.einsum(
        "sla,slb->sab", weighted, in_sum.reshape(half, length, -1), precision=lax.Precision.HIGHEST
    )
    features = features.reshape(half, 2, -1).transpose(1, 0, 2).astype(bf16)
    other = exchange(pick(features, 1 - core), "narrow", 1)
    mine = pick(features, core)
    block = jnp.concatenate([jnp.where(core == 0, mine, other), jnp.where(core == 0, other, mine)], 0)

    wide_targets = targets.astype(f32)
    target_squares = jnp.sum(wide_targets * wide_targets, axis=1)
    target_squares = target_squares + exchange(target_squares, "narrow", 1)
    target_squares = target_squares + exchange(target_squares, "narrow", 2)

    gathered = jnp.concatenate(gather_blocks(block), axis=0)
    order = program_output_index.reshape(wide_count, programs)
    order = jnp.take(order, w ^ jnp.arange(wide_count), axis=0).reshape(-1)
    rows = order.shape[0] // narrow_count
    contract = (((1,), (1,)), ((), ()))

    def partial(x_index, core_index):
        first = (x_index * 2 + core_index) * rows
        chosen = (lax.broadcasted_iota(jnp.int32, (rows, order.shape[0]), 0) + first == order[None, :])
        ordered = jnp.dot(chosen.astype(bf16), gathered, preferred_element_type=f32)
        squares = jnp.sum(ordered * ordered, axis=1)
        return lax.dot_general(
            ordered.astype(bf16), targets, contract, preferred_element_type=f32
        ), squares

    far_send, far_send_sq = partial(1 - x, 1 - core)
    far_keep, far_keep_sq = partial(1 - x, core)
    far = far_keep + exchange(far_send.astype(bf16), "narrow", 1).astype(f32)
    far_sq = far_keep_sq + exchange(far_send_sq, "narrow", 1)
    near_send, near_send_sq = partial(x, 1 - core)
    near_keep, near_keep_sq = partial(x, core)
    near = near_keep + exchange(near_send.astype(bf16), "narrow", 1).astype(f32)
    near_sq = near_keep_sq + exchange(near_send_sq, "narrow", 1)
    total = near + exchange(far.astype(bf16), "narrow", 2).astype(f32)
    squares = near_sq + exchange(far_sq, "narrow", 2)
    root_count = math.sqrt(float(targets.shape[1] * narrow_count))
    row_scale = lax.rsqrt(squares + epsilon) * root_count
    return total * row_scale[:, None] * lax.rsqrt(target_squares + epsilon)[None, :]


def solution(mesh):
    return jax.shard_map(
        shards,
        mesh=mesh,
        in_specs=(
            P("wide", "narrow"),
            P("wide", "narrow"),
            P("narrow", None),
            P("narrow", None),
            P(),
            P("wide"),
            P(),
            P("wide", "narrow"),
        ),
        out_specs=P("narrow", "wide"),
        check_vma=False,
    )
```

time: 167 us -> 94.9 us (0.57)
  waiting for transfers between devices: 108 us -> 41.3 us
  starting transfers between devices: 0.27 us -> 18.6 us
  between operations: 13.2 us -> 0.43 us
  blocking collectives: 6.04 us -> 0 us
  other arithmetic: 12.9 us -> 7.07 us
  matrix products: 18.8 us -> 24.1 us
  local copies, waits for them, and re-layouts: 7.4 us -> 3.27 us
    all_gather x1 -> x0, waiting for transfers between devices: 45.4 us -> none  [shards(): gathered = lax.all_gather(unit_rows, 'wide', axis=0, tiled=True)]
    ppermute x0 -> x18, waiting for transfers between devices: none -> 41.3 us  [exchange(): return lax.ppermute(array, axis, [(i, i ^ bit) for i in range(count)])]
    psum x1 -> x0, waiting for transfers between devices: 32.3 us -> none  [shards(): lax.psum(in_part.astype(jnp.bfloat16), 'narrow').astype(jnp.float32)]
    reduce_scatter x1 -> x0, waiting for transfers between devices: 30.1 us -> none  [shards(): lax.psum_scatter(lax.dot_general(permuted, target_unit, contract, preferr...]
    ppermute x0 -> x18, starting transfers between devices: none -> 18.6 us  [exchange(): return lax.ppermute(array, axis, [(i, i ^ bit) for i in range(count)])]
    psum x1 -> x0, blocking collectives: 6.04 us -> none  [shards(): squares, target_squares = lax.psum((squares, target_squares), 'narrow')]
    gather x1, local copies, waits for them, and re-layouts: 6.27 us -> 0.55 us  [shards(): order = jnp.take(order, w ^ jnp.arange(wide_count), axis=0).reshape(-1)]
    dot_general x5 -> x12, matrix products: 18.8 us -> 24.1 us  [the longest x4 15.2 us: partial(): lax.dot_general(ordered.astype(bf16), targets, contract, preferred_elemen...]
  transfers between devices with their start and end apart: 3 -> 18, of which waited for: 3 -> 6; matrix products, arithmetic and copies ran while one was open for 5% -> 27% of each run, Pallas kernels for 0% -> 0%
where the time goes in v1:
time: 94.9 us; the launch traced here: 94.8 us
  waiting for transfers between devices  41.3 us (44%)
  matrix products  24.1 us (25%)
  starting transfers between devices  18.6 us (20%)
  other arithmetic  7.07 us (7%)
  local copies, waits for them, and re-layouts  3.27 us (3%)
    ppermute x18, waiting for transfers between devices, exchange(): return lax.ppermute(array, axis, [(i, i ^ bit) for i in range(count)])  41.3 us
    ppermute x18, starting transfers between devices, exchange(): return lax.ppermute(array, axis, [(i, i ^ bit) for i in range(count)])  18.6 us
    dot_general x4, matrix products, partial(): lax.dot_general(ordered.astype(bf16), targets, contract, preferred_elemen...  15.2 us
    reduce_sum x1, other arithmetic, shards(): target_squares = jnp.sum(wide_targets * wide_targets, axis=1)  5.08 us
    dot_general x1, matrix products, shards(): jnp.dot(output_gradient_rows, adapter_up_weight, preferred_element_type=f32)  3.61 us
    dot_general x4, matrix products, partial(): ordered = jnp.dot(chosen.astype(bf16), gathered, preferred_element_type=f32)  2.29 us
  transfers between devices with their start and end apart: 18, of which 6 were waited for; matrix products, arithmetic and copies ran while one was open for 27% of the time, Pallas kernels for 0%

profile of v1, /device:TPU:0, one launch (start us, length us, event | category | flops | bytes accessed | tf_op | source)
XLA Modules:
  0.0 94.8 jit_solution(15648672459716341576)
XLA Ops:
  0.0 0.9 %copy-done = bf16[1024,128]{1,0:T(8,128)(2,1)S(1)} copy-done((bf16[1024,128]{1,0:T(8,128)(2,1)S(1)}, bf16[1024,128]{1,0:T(8,128)(2,1)}, u32[]{:S(2)}) %copy-start) | copy-done | bytes 262168
  1.0 3.6 %fusion.33 = f32[2048,128]{1,0:T(8,128)S(1)} fusion(bf16[2048,1024]{1,0:T(8,128)(2,1)} %param.9, bf16[1024,128]{1,0:T(8,128)(2,1)S(1)} %copy-done), kind=kOutput, calls=%fused_computation.85 | convolution fusion | flops 536870912 | bytes 5505024 | tf_op jit(solution)/shard_map/dot_general | solution.py:52
  4.6 0.7 convolution_convert_fusion.3
  5.4 1.3 %convolution_convert_fusion.2 = bf16[2048,128]{1,0:T(8,128)(2,1)S(1)} fusion(bf16[2048,1024]{1,0:T(8,128)(2,1)S(1)} %copy-done.3, bf16[1024,128]{1,0:T(8,128)(2,1)S(1)} %copy-done.4), kind=kOutput, calls=%fused_computation.4 | convolution fusion | flops 537133056 | bytes 4980736 | tf_op jit(solution)/shard_map/dot_general | solution.py:54
  6.7 0.2 copy.16
  7.0 0.5 collective-permute-start
  7.5 5.1 %multiply_reduce_fusion = f32[2048]{0:T(1024)S(1)} fusion(bf16[2048,2048]{1,0:T(8,128)(2,1)} %param.15), kind=kLoop, calls=%fused_computation.1 | loop fusion | flops 12580864 | bytes 8396800 | tf_op jit(solution)/shard_map/reduce_sum | solution.py:78
  12.6 0.1 collective-permute-start.16
  12.7 0.1 reshape.96
  12.9 0.6 gather_fusion
  13.5 0.1 convert_add_fusion
  13.8 3.0 %collective-permute-start.1 = (bf16[1024,160]{0,1:T(8,128)(2,1)S(1)}, bf16[1024,160]{0,1:T(8,128)(2,1)S(1)}, u32[]{:S(2)}, u32[]{:S(2)}) collective-permute-start(bf16[1024,160]{0,1:T(8,128)(2,1)S(1)} %pad_maximum_fusion), channel_id=1, source_target_pairs={{0,2},{1,3},{2,0},{3,1},{4,6},{5,7},{6,4},{7,5},{8,10},{9,11},{10,... | collective-permute-start | bytes 983048 | tf_op jit(solution)/shard_map/ppermute | solution.py:13
  16.9 7.9 %collective-permute-done.1 = bf16[1024,160]{0,1:T(8,128)(2,1)S(1)} collective-permute-done((bf16[1024,160]{0,1:T(8,128)(2,1)S(1)}, bf16[1024,160]{0,1:T(8,128)(2,1)S(1)}, u32[]{:S(2)}, u32[]{:S(2)}) %collective-permute-start.1) | collective-permute-done | bytes 327712 | tf_op jit(solution)/shard_map/ppermute | solution.py:13
  24.8 0.1 slice_add_fusion
  24.9 0.2 reshape.95
  25.1 0.2 copy.18
  25.3 0.9 convolution_convert_fusion.4
  26.3 0.5 constant_dynamic-slice_fusion.1
  26.9 0.1 copy.37
  27.1 1.8 %collective-permute-start.17 = (f32[2048]{0:T(1024)S(1)}, f32[2048]{0:T(1024)S(1)}, u32[]{:S(2)}, u32[]{:S(2)}) collective-permute-start(f32[2048]{0:T(1024)S(1)} %add.156), channel_id=1, source_target_pairs={{0,2},{1,3},{2,0},{3,1},{4,6},{5,7},{6,4},{7,5},{8,10},{9,11},{10,... | collective-permute-start | bytes 24584 | tf_op jit(solution)/shard_map/ppermute | solution.py:13
  28.9 0.1 constant_dynamic-update-slice_fusion.8
  29.0 0.1 constant_dynamic-update-slice_fusion.7
  29.1 1.6 %collective-permute-start.3 = (bf16[64,2048]{1,0:T(8,128)(2,1)S(1)}, bf16[64,2048]{1,0:T(8,128)(2,1)S(1)}, u32[]{:S(2)}, u32[]{:S(2)}) collective-permute-start(bf16[64,2048]{1,0:T(8,128)(2,1)S(1)} %pad_maximum_fusion.1), channel_id=1, source_target_pairs={{0,4},{4,0},{8,12},{12,8},{16,20},{20,16},{24,28},{28,24},{1,5},{5... | collective-permute-start | bytes 786440 | tf_op jit(solution)/shard_map/ppermute | solution.py:13
  30.7 1.6 %collective-permute-start.4 = (bf16[64,2048]{1,0:T(8,128)(2,1)S(1)}, bf16[64,2048]{1,0:T(8,128)(2,1)S(1)}, u32[]{:S(2)}, u32[]{:S(2)}) collective-permute-start(bf16[64,2048]{1,0:T(8,128)(2,1)S(1)} %pad_maximum_fusion.1), channel_id=1, source_target_pairs={{0,8},{4,12},{8,0},{12,4},{16,24},{20,28},{24,16},{28,20},{1,9},{5... | collective-permute-start | bytes 786440 | tf_op jit(solution)/shard_map/ppermute | solution.py:13
  32.3 2.6 %collective-permute-start.6 = (bf16[64,2048]{1,0:T(8,128)(2,1)S(1)}, bf16[64,2048]{1,0:T(8,128)(2,1)S(1)}, u32[]{:S(2)}, u32[]{:S(2)}) collective-permute-start(bf16[64,2048]{1,0:T(8,128)(2,1)S(1)} %pad_maximum_fusion.1), channel_id=1, source_target_pairs={{0,16},{4,20},{8,24},{12,28},{16,0},{20,4},{24,8},{28,12},{1,17},{... | collective-permute-start | bytes 786440 | tf_op jit(solution)/shard_map/ppermute | solution.py:13
  35.0 11.7 %collective-permute-done.6 = bf16[64,2048]{1,0:T(8,128)(2,1)S(1)} collective-permute-done((bf16[64,2048]{1,0:T(8,128)(2,1)S(1)}, bf16[64,2048]{1,0:T(8,128)(2,1)S(1)}, u32[]{:S(2)}, u32[]{:S(2)}) %collective-permute-start.6) | collective-permute-done | bytes 262176 | tf_op jit(solution)/shard_map/ppermute | solution.py:13
  46.7 0.5 collective-permute-start.7
  47.2 0.4 collective-permute-start.8
  47.6 1.5 %collective-permute-start.5 = (bf16[64,2048]{1,0:T(8,128)(2,1)S(1)}, bf16[64,2048]{1,0:T(8,128)(2,1)S(1)}, u32[]{:S(2)}, u32[]{:S(2)}) collective-permute-start(bf16[64,2048]{1,0:T(8,128)(2,1)S(1)} %collective-permute-done.4), channel_id=1, source_target_pairs={{0,4},{4,0},{8,12},{12,8},{16,20},{20,16},{24,28},{28,24},{1,5},{5... | collective-permute-start | bytes 786440 | tf_op jit(solution)/shard_map/ppermute | solution.py:13
  49.2 4.4 %collective-permute-done.8 = bf16[64,2048]{1,0:T(8,128)(2,1)S(1)} collective-permute-done((bf16[64,2048]{1,0:T(8,128)(2,1)S(1)}, bf16[64,2048]{1,0:T(8,128)(2,1)S(1)}, u32[]{:S(2)}, u32[]{:S(2)}) %collective-permute-start.8) | collective-permute-done | bytes 262176 | tf_op jit(solution)/shard_map/ppermute | solution.py:13
  53.6 1.5 %collective-permute-start.9 = (bf16[64,2048]{1,0:T(8,128)(2,1)S(1)}, bf16[64,2048]{1,0:T(8,128)(2,1)S(1)}, u32[]{:S(2)}, u32[]{:S(2)}) collective-permute-start(bf16[64,2048]{1,0:T(8,128)(2,1)S(1)} %collective-permute-done.8), channel_id=1, source_target_pairs={{0,4},{4,0},{8,12},{12,8},{16,20},{20,16},{24,28},{28,24},{1,5},{5... | collective-permute-start | bytes 786440 | tf_op jit(solution)/shard_map/ppermute | solution.py:13
  55.1 4.8 %collective-permute-done.5 = bf16[64,2048]{1,0:T(8,128)(2,1)S(1)} collective-permute-done((bf16[64,2048]{1,0:T(8,128)(2,1)S(1)}, bf16[64,2048]{1,0:T(8,128)(2,1)S(1)}, u32[]{:S(2)}, u32[]{:S(2)}) %collective-permute-start.5) | collective-permute-done | bytes 262176 | tf_op jit(solution)/shard_map/ppermute | solution.py:13
  60.0 2.7 %collective-permute-done.9 = bf16[64,2048]{1,0:T(8,128)(2,1)S(1)} collective-permute-done((bf16[64,2048]{1,0:T(8,128)(2,1)S(1)}, bf16[64,2048]{1,0:T(8,128)(2,1)S(1)}, u32[]{:S(2)}, u32[]{:S(2)}) %collective-permute-start.9) | collective-permute-done | bytes 262176 | tf_op jit(solution)/shard_map/ppermute | solution.py:13
  62.7 0.6 multiply_reduce_fusion.1
  63.4 0.6 multiply_reduce_fusion.3
  63.9 0.6 collective-permute-start.13
  64.5 6.4 %convolution_convert_fusion = bf16[128,2048]{1,0:T(8,128)(2,1)S(1)} fusion(bf16[2048,2048]{1,0:T(8,128)(2,1)} %param.15, bf16[128,2048]{1,0:T(8,128)(2,1)S(1)} %get-tuple-element.14), kind=kOutput, calls=%fused_computation.2 | convolution fusion | flops 1074003968 | bytes 9437184 | tf_op jit(solution)/shard_map/dot_general | solution.py:93
  70.9 0.1 collective-permute-start.11
  71.0 3.1 %convolution_convert_fusion.1 = bf16[128,2048]{1,0:T(8,128)(2,1)S(1)} fusion(bf16[2048,2048]{1,0:T(8,128)(2,1)S(1)} %bitcast.55, bf16[128,2048]{1,0:T(8,128)(2,1)S(1)} %get-tuple-element.18), kind=kOutput, calls=%fused_computation.3 | convolution fusion | flops 1074003968 | bytes 9437184 | tf_op jit(solution)/shard_map/dot_general | solution.py:93
  74.1 0.6 multiply_reduce_fusion.2
  74.7 0.6 multiply_reduce_fusion.4
  75.3 0.5 collective-permute-start.10
  75.8 1.2 %collective-permute-start.15 = (f32[128]{0:T(128)S(1)}, f32[128]{0:T(128)S(1)}, u32[]{:S(2)}, u32[]{:S(2)}) collective-permute-start(f32[128]{0:T(128)S(1)} %add.152), channel_id=1, source_target_pairs={{0,2},{1,3},{2,0},{3,1},{4,6},{5,7},{6,4},{7,5},{8,10},{9,11},{10,... | collective-permute-start | bytes 1544 | tf_op jit(solution)/shard_map/ppermute | solution.py:13
  77.0 2.9 %add_convert_fusion = bf16[128,2048]{1,0:T(8,128)(2,1)S(1)} fusion(bf16[128,2048]{1,0:T(8,128)(2,1)S(1)} %collective-permute-done.11, bf16[2048,2048]{1,0:T(8,128)(2,1)S(1)} %bitcast.55, bf16[128,2048]{1,0:T(8,128)(2,1)S(1)} %get-tuple-element.12), kind=kOutput, calls=%fused_computation.12 | convolution fusion | flops 1074528256 | bytes 9961472 | tf_op jit(solution)/shard_map/dot_general | solution.py:93
  79.8 0.9 collective-permute-start.12
  80.8 2.9 %fusion.7 = f32[128,2048]{1,0:T(8,128)S(1)} fusion(bf16[2048,2048]{1,0:T(8,128)(2,1)S(1)} %bitcast.55, bf16[128,2048]{1,0:T(8,128)(2,1)S(1)} %get-tuple-element.16), kind=kOutput, calls=%fused_computation.24 | convolution fusion | flops 1073741824 | bytes 9961472 | tf_op jit(solution)/shard_map/dot_general | solution.py:93
  83.7 9.8 %collective-permute-done.12 = bf16[128,2048]{1,0:T(8,128)(2,1)S(1)} collective-permute-done((bf16[128,2048]{1,0:T(8,128)(2,1)S(1)}, bf16[128,2048]{1,0:T(8,128)(2,1)S(1)}, u32[]{:S(2)}, u32[]{:S(2)}) %collective-permute-start.12) | collective-permute-done | bytes 524320 | tf_op jit(solution)/shard_map/ppermute | solution.py:13
  93.5 1.2 %multiply_multiply_fusion = f32[128,2048]{1,0:T(8,128)} fusion(bf16[128,2048]{1,0:T(8,128)(2,1)S(1)} %collective-permute-done.12, f32[128,2048]{1,0:T(8,128)S(1)} %fusion.7, bf16[128,2048]{1,0:T(8,128)(2,1)S(1)} %collective-permute-done.10, f32[2048]{0:T(1024)S(1)} %add_rsqrt_fusion, f32[128]{0:T(128)S(1)} %rsqrt_multiply_fusion), kind=kLoop, calls=%fused_computation.7 | loop fusion | flops 1572864 | bytes 3154432 | tf_op jit(solution)/shard_map/mul | solution.py:109
  (64 shorter events, 1.1 us)
Async XLA Ops:
  0.0 1.0 %copy-start = (bf16[1024,128]{1,0:T(8,128)(2,1)S(1)}, bf16[1024,128]{1,0:T(8,128)(2,1)}, u32[]{:S(2)}) copy-start(bf16[1024,128]{1,0:T(8,128)(2,1)} %param.10) | copy-start | bytes 786436
  1.0 3.6 %copy-start.1 = (bf16[128,64]{0,1:T(8,128)(2,1)S(1)}, bf16[128,64]{0,1:T(8,128)(2,1)}, u32[]{:S(2)}) copy-start(bf16[128,64]{0,1:T(8,128)(2,1)} %param.12) | copy-start | bytes 49156
  1.0 4.4 %copy-start.3 = (bf16[2048,1024]{1,0:T(8,128)(2,1)S(1)}, bf16[2048,1024]{1,0:T(8,128)(2,1)}, u32[]{:S(2)}) copy-start(bf16[2048,1024]{1,0:T(8,128)(2,1)} %param.8) | copy-start | bytes 12582916
  1.0 4.4 %copy-start.4 = (bf16[1024,128]{1,0:T(8,128)(2,1)S(1)}, bf16[1024,128]{1,0:T(8,128)(2,1)}, u32[]{:S(2)}) copy-start(bf16[1024,128]{1,0:T(8,128)(2,1)} %param.11) | copy-start | bytes 786436
  6.9 5.7 %copy-start.5 = (s32[64]{0:T(128)S(1)}, s32[64]{0:T(128)}, u32[]{:S(2)}) copy-start(s32[64]{0:T(128)} %param.13) | copy-start | bytes 772
  7.0 5.8 %copy-start.2 = (s32[512]{0:T(512)S(1)}, s32[512]{0:T(512)}, u32[]{:S(2)}) copy-start(s32[512]{0:T(512)} %param.14) | copy-start | bytes 6148
  7.0 6.6 %collective-permute-start = (bf16[1024,192]{0,1:T(8,128)(2,1)S(1)}, bf16[1024,192]{0,1:T(8,128)(2,1)S(1)}, u32[]{:S(2)}, u32[]{:S(2)}) collective-permute-start(bf16[1024,192]{0,1:T(8,128)(2,1)S(1)} %fusion.10), channel_id=1, source_target_pairs={{0,1},{1,0},{2,3},{3,2},{4,5},{5,4},{6,7},{7,6},{8,9},{9,8},{10,11... | collective-permute-start | bytes 1179656 | tf_op jit(solution)/shard_map/ppermute | solution.py:13
  12.6 14.5 %collective-permute-start.16 = (f32[2048]{0:T(1024)S(1)}, f32[2048]{0:T(1024)S(1)}, u32[]{:S(2)}, u32[]{:S(2)}) collective-permute-start(f32[2048]{0:T(1024)S(1)} %multiply_reduce_fusion), channel_id=1, source_target_pairs={{0,1},{1,0},{2,3},{3,2},{4,5},{5,4},{6,7},{7,6},{8,9},{9,8},{10,11... | collective-permute-start | bytes 24584 | tf_op jit(solution)/shard_map/ppermute | solution.py:13
  13.8 10.9 %collective-permute-start.1 = (bf16[1024,160]{0,1:T(8,128)(2,1)S(1)}, bf16[1024,160]{0,1:T(8,128)(2,1)S(1)}, u32[]{:S(2)}, u32[]{:S(2)}) collective-permute-start(bf16[1024,160]{0,1:T(8,128)(2,1)S(1)} %pad_maximum_fusion), channel_id=1, source_target_pairs={{0,2},{1,3},{2,0},{3,1},{4,6},{5,7},{6,4},{7,5},{8,10},{9,11},{10,... | collective-permute-start | bytes 983048 | tf_op jit(solution)/shard_map/ppermute | solution.py:13
  26.9 2.0 %collective-permute-start.2 = (bf16[32,2048]{1,0:T(8,128)(2,1)S(1)}, bf16[32,2048]{1,0:T(8,128)(2,1)S(1)}, u32[]{:S(2)}, u32[]{:S(2)}) collective-permute-start(bf16[32,2048]{1,0:T(8,128)(2,1)S(1)} %bitcast.63), channel_id=1, source_target_pairs={{0,1},{1,0},{2,3},{3,2},{4,5},{5,4},{6,7},{7,6},{8,9},{9,8},{10,11... | collective-permute-start | bytes 393224 | tf_op jit(solution)/shard_map/ppermute | solution.py:13
  27.1 7.9 %collective-permute-start.17 = (f32[2048]{0:T(1024)S(1)}, f32[2048]{0:T(1024)S(1)}, u32[]{:S(2)}, u32[]{:S(2)}) collective-permute-start(f32[2048]{0:T(1024)S(1)} %add.156), channel_id=1, source_target_pairs={{0,2},{1,3},{2,0},{3,1},{4,6},{5,7},{6,4},{7,5},{8,10},{9,11},{10,... | collective-permute-start | bytes 24584 | tf_op jit(solution)/shard_map/ppermute | solution.py:13
  29.1 20.0 %collective-permute-start.3 = (bf16[64,2048]{1,0:T(8,128)(2,1)S(1)}, bf16[64,2048]{1,0:T(8,128)(2,1)S(1)}, u32[]{:S(2)}, u32[]{:S(2)}) collective-permute-start(bf16[64,2048]{1,0:T(8,128)(2,1)S(1)} %pad_maximum_fusion.1), channel_id=1, source_target_pairs={{0,4},{4,0},{8,12},{12,8},{16,20},{20,16},{24,28},{28,24},{1,5},{5... | collective-permute-start | bytes 786440 | tf_op jit(solution)/shard_map/ppermute | solution.py:13
  30.7 16.9 %collective-permute-start.4 = (bf16[64,2048]{1,0:T(8,128)(2,1)S(1)}, bf16[64,2048]{1,0:T(8,128)(2,1)S(1)}, u32[]{:S(2)}, u32[]{:S(2)}) collective-permute-start(bf16[64,2048]{1,0:T(8,128)(2,1)S(1)} %pad_maximum_fusion.1), channel_id=1, source_target_pairs={{0,8},{4,12},{8,0},{12,4},{16,24},{20,28},{24,16},{28,20},{1,9},{5... | collective-permute-start | bytes 786440 | tf_op jit(solution)/shard_map/ppermute | solution.py:13
  32.3 14.4 %collective-permute-start.6 = (bf16[64,2048]{1,0:T(8,128)(2,1)S(1)}, bf16[64,2048]{1,0:T(8,128)(2,1)S(1)}, u32[]{:S(2)}, u32[]{:S(2)}) collective-permute-start(bf16[64,2048]{1,0:T(8,128)(2,1)S(1)} %pad_maximum_fusion.1), channel_id=1, source_target_pairs={{0,16},{4,20},{8,24},{12,28},{16,0},{20,4},{24,8},{28,12},{1,17},{... | collective-permute-start | bytes 786440 | tf_op jit(solution)/shard_map/ppermute | solution.py:13
  46.7 13.3 %collective-permute-start.7 = (bf16[64,2048]{1,0:T(8,128)(2,1)S(1)}, bf16[64,2048]{1,0:T(8,128)(2,1)S(1)}, u32[]{:S(2)}, u32[]{:S(2)}) collective-permute-start(bf16[64,2048]{1,0:T(8,128)(2,1)S(1)} %collective-permute-done.6), channel_id=1, source_target_pairs={{0,4},{4,0},{8,12},{12,8},{16,20},{20,16},{24,28},{28,24},{1,5},{5... | collective-permute-start | bytes 786440 | tf_op jit(solution)/shard_map/ppermute | solution.py:13
  47.2 6.4 %collective-permute-start.8 = (bf16[64,2048]{1,0:T(8,128)(2,1)S(1)}, bf16[64,2048]{1,0:T(8,128)(2,1)S(1)}, u32[]{:S(2)}, u32[]{:S(2)}) collective-permute-start(bf16[64,2048]{1,0:T(8,128)(2,1)S(1)} %collective-permute-done.6), channel_id=1, source_target_pairs={{0,8},{4,12},{8,0},{12,4},{16,24},{20,28},{24,16},{28,20},{1,9},{5... | collective-permute-start | bytes 786440 | tf_op jit(solution)/shard_map/ppermute | solution.py:13
  47.6 12.2 %collective-permute-start.5 = (bf16[64,2048]{1,0:T(8,128)(2,1)S(1)}, bf16[64,2048]{1,0:T(8,128)(2,1)S(1)}, u32[]{:S(2)}, u32[]{:S(2)}) collective-permute-start(bf16[64,2048]{1,0:T(8,128)(2,1)S(1)} %collective-permute-done.4), channel_id=1, source_target_pairs={{0,4},{4,0},{8,12},{12,8},{16,20},{20,16},{24,28},{28,24},{1,5},{5... | collective-permute-start | bytes 786440 | tf_op jit(solution)/shard_map/ppermute | solution.py:13
  53.6 9.1 %collective-permute-start.9 = (bf16[64,2048]{1,0:T(8,128)(2,1)S(1)}, bf16[64,2048]{1,0:T(8,128)(2,1)S(1)}, u32[]{:S(2)}, u32[]{:S(2)}) collective-permute-start(bf16[64,2048]{1,0:T(8,128)(2,1)S(1)} %collective-permute-done.8), channel_id=1, source_target_pairs={{0,4},{4,0},{8,12},{12,8},{16,20},{20,16},{24,28},{28,24},{1,5},{5... | collective-permute-start | bytes 786440 | tf_op jit(solution)/shard_map/ppermute | solution.py:13
  60.0 11.1 %slice-start = ((s8[8388608]{0:T(1024)(128)(4,1)}), s8[4194304]{0:T(1024)(128)(4,1)S(1)}, s32[]{:S(2)}) async-start(s8[8388608]{0:T(1024)(128)(4,1)} %bitcast.54), calls=%async_computation | async-start | bytes 8388608
  63.3 12.5 %collective-permute-start.14 = (f32[128]{0:T(128)S(1)}, f32[128]{0:T(128)S(1)}, u32[]{:S(2)}, u32[]{:S(2)}) collective-permute-start(f32[128]{0:T(128)S(1)} %get-tuple-element.13), channel_id=1, source_target_pairs={{0,1},{1,0},{2,3},{3,2},{4,5},{5,4},{6,7},{7,6},{8,9},{9,8},{10,11... | collective-permute-start | bytes 1544 | tf_op jit(solution)/shard_map/ppermute | solution.py:13
  63.9 19.7 %collective-permute-start.13 = (f32[128]{0:T(128)S(1)}, f32[128]{0:T(128)S(1)}, u32[]{:S(2)}, u32[]{:S(2)}) collective-permute-start(f32[128]{0:T(128)S(1)} %get-tuple-element.17), channel_id=1, source_target_pairs={{0,1},{1,0},{2,3},{3,2},{4,5},{5,4},{6,7},{7,6},{8,9},{9,8},{10,11... | collective-permute-start | bytes 1544 | tf_op jit(solution)/shard_map/ppermute | solution.py:13
  64.5 6.5 %slice-start.1 = ((s8[8388608]{0:T(1024)(128)(4,1)}), s8[4194304]{0:T(1024)(128)(4,1)S(1)}, s32[]{:S(2)}) async-start(s8[8388608]{0:T(1024)(128)(4,1)} %bitcast.54), calls=%async_computation.1 | async-start | bytes 8388608
  70.9 6.0 %collective-permute-start.11 = (bf16[128,2048]{1,0:T(8,128)(2,1)S(1)}, bf16[128,2048]{1,0:T(8,128)(2,1)S(1)}, u32[]{:S(2)}, u32[]{:S(2)}) collective-permute-start(bf16[128,2048]{1,0:T(8,128)(2,1)S(1)} %convolution_convert_fusion), channel_id=1, source_target_pairs={{0,1},{1,0},{2,3},{3,2},{4,5},{5,4},{6,7},{7,6},{8,9},{9,8},{10,11... | collective-permute-start | bytes 1572872 | tf_op jit(solution)/shard_map/ppermute | solution.py:13
  75.3 8.5 %collective-permute-start.10 = (bf16[128,2048]{1,0:T(8,128)(2,1)S(1)}, bf16[128,2048]{1,0:T(8,128)(2,1)S(1)}, u32[]{:S(2)}, u32[]{:S(2)}) collective-permute-start(bf16[128,2048]{1,0:T(8,128)(2,1)S(1)} %convolution_convert_fusion.1), channel_id=1, source_target_pairs={{0,1},{1,0},{2,3},{3,2},{4,5},{5,4},{6,7},{7,6},{8,9},{9,8},{10,11... | collective-permute-start | bytes 1572872 | tf_op jit(solution)/shard_map/ppermute | solution.py:13
  75.8 7.9 %collective-permute-start.15 = (f32[128]{0:T(128)S(1)}, f32[128]{0:T(128)S(1)}, u32[]{:S(2)}, u32[]{:S(2)}) collective-permute-start(f32[128]{0:T(128)S(1)} %add.152), channel_id=1, source_target_pairs={{0,2},{1,3},{2,0},{3,1},{4,6},{5,7},{6,4},{7,5},{8,10},{9,11},{10,... | collective-permute-start | bytes 1544 | tf_op jit(solution)/shard_map/ppermute | solution.py:13
  79.8 13.7 %collective-permute-start.12 = (bf16[128,2048]{1,0:T(8,128)(2,1)S(1)}, bf16[128,2048]{1,0:T(8,128)(2,1)S(1)}, u32[]{:S(2)}, u32[]{:S(2)}) collective-permute-start(bf16[128,2048]{1,0:T(8,128)(2,1)S(1)} %add_convert_fusion), channel_id=1, source_target_pairs={{0,2},{1,3},{2,0},{3,1},{4,6},{5,7},{6,4},{7,5},{8,10},{9,11},{10,... | collective-permute-start | bytes 1572872 | tf_op jit(solution)/shard_map/ppermute | solution.py:13

commit v2 on v1

v2 whole, which is shorter than its diff:
```python
import functools
import math

import jax
import jax.numpy as jnp
from jax import lax
from jax.experimental import pallas as pl
from jax.experimental.pallas import tpu as pltpu
from jax.sharding import PartitionSpec as P

epsilon = 1e-06
chunks = 2
lanes = 128
f32, bf16 = jnp.float32, jnp.bfloat16
nt = (((1,), (1,)), ((), ()))


def params():
    return pltpu.CompilerParams(vmem_limit_bytes=40 * 1024 * 1024)


def cost(flops, moved):
    return pl.CostEstimate(flops=flops, bytes_accessed=moved, transcendentals=0)


def exchange(array, axis, bit):
    count = lax.axis_size(axis)
    return lax.ppermute(array, axis, [(i, i ^ bit) for i in range(count)])


def gather_blocks(block):
    count = lax.axis_size("wide")
    held = {0: block}
    bit = count // 2
    while bit:
        for k in list(held):
            held[k | bit] = exchange(held[k], "wide", bit)
        bit //= 2
    return [held[k] for k in range(count)]


def project_kernel(place, x_ref, g_ref, w_ref, up_ref, rank_ref, send_ref, keep_ref):
    half, step = pl.program_id(0), pl.program_id(1)
    sub = x_ref.shape[0]
    tokens = pl.num_programs(1) * sub
    out_width = rank_ref.shape[0] // 2
    stack = tokens // lanes * out_width
    in_part = jnp.dot(x_ref[...], w_ref[...], preferred_element_type=f32)
    reduced = jnp.dot(g_ref[...], up_ref[...], preferred_element_type=f32)
    out_part = lax.dot_general(
        rank_ref[...], reduced, nt, preferred_element_type=f32, precision=lax.Precision.HIGHEST
    )

    def store(ref):
        ref[pl.ds(step * sub, sub), :] = in_part.astype(ref.dtype)
        for x in range(2):
            for piece in range(sub // lanes):
                row = tokens + x * stack + (step * (sub // lanes) + piece) * out_width
                ref[pl.ds(pl.multiple_of(row, out_width), out_width), :] = out_part[
                    x * out_width : (x + 1) * out_width, piece * lanes : (piece + 1) * lanes
                ].astype(ref.dtype)

    @pl.when(half == 0)
    def _():
        store(send_ref)

    @pl.when(half == 1)
    def _():
        store(keep_ref)


def project(chunk, place, x, g, w, up, rank):
    tokens = x.shape[0] // chunks // 2
    sub = min(256, tokens)
    steps = tokens // sub
    depth = x.shape[1]
    rows = tokens + 2 * (tokens // lanes) * (rank.shape[0] // 2)

    def block(half, step, place):
        mine = place[0] + (1 - half) * (1 - 2 * place[0])
        return ((chunk * 2 + mine) * steps + step, 0)

    def whole(half, step, place):
        return (0, 0)

    return pl.pallas_call(
        project_kernel,
        grid_spec=pltpu.PrefetchScalarGridSpec(
            num_scalar_prefetch=1,
            grid=(2, steps),
            in_specs=[
                pl.BlockSpec((sub, depth), block),
                pl.BlockSpec((sub, depth), block),
                pl.BlockSpec(w.shape, whole),
                pl.BlockSpec(up.shape, whole),
                pl.BlockSpec(rank.shape, whole),
            ],
            out_specs=[pl.BlockSpec((rows, lanes), whole), pl.BlockSpec((rows, lanes), whole)],
        ),
        out_shape=[
            jax.ShapeDtypeStruct((rows, lanes), bf16),
            jax.ShapeDtypeStruct((rows, lanes), f32),
        ],
        compiler_params=params(),
        cost_estimate=cost(8 * tokens * depth * lanes, 8 * tokens * depth),
        name="project",
    )(place, x, g, w, up, rank)


def core_sum_kernel(place, keep_ref, came_ref, send_ref, left_ref):
    rows = keep_ref.shape[0]
    final = send_ref.shape[0]
    stack = rows - final
    tokens = final - stack
    x = place[1]
    total = keep_ref[:tokens, :] + came_ref[:tokens, :].astype(f32)
    send_ref[:tokens, :] = total.astype(bf16)
    left_ref[:tokens, :] = total
    far = pl.ds(pl.multiple_of(tokens + (1 - x) * stack, stack), stack)
    near = pl.ds(pl.multiple_of(tokens + x * stack, stack), stack)
    send_ref[tokens:, :] = (keep_ref[far, :] + came_ref[far, :].astype(f32)).astype(bf16)
    left_ref[tokens:, :] = keep_ref[near, :] + came_ref[near, :].astype(f32)


def core_sum(place, keep, came, tokens):
    rows = keep.shape[0]
    final = tokens + (rows - tokens) // 2
    vmem = pl.BlockSpec(memory_space=pltpu.VMEM)
    return pl.pallas_call(
        core_sum_kernel,
        in_specs=[pl.BlockSpec(memory_space=pltpu.SMEM), vmem, vmem],
        out_specs=[vmem, vmem],
        out_shape=[
            jax.ShapeDtypeStruct((final, lanes), bf16),
            jax.ShapeDtypeStruct((final, lanes), f32),
        ],
        compiler_params=params(),
        cost_estimate=cost(rows * lanes, 12 * rows * lanes),
        name="core_sum",
    )(place, keep, came)


def feature_kernel(first, programs, place, lengths, left_ref, came_ref, mine_ref, other_ref, held):
    core = place[0]
    quarter = mine_ref.shape[0]
    out_width = 2 * quarter
    final = left_ref.shape[0]
    tokens = final * lanes // (lanes + out_width)
    length = tokens // programs
    in_sum = (left_ref[:tokens, :] + came_ref[:tokens, :].astype(f32)).astype(bf16)
    out_sum = left_ref[tokens:, :] + came_ref[tokens:, :].astype(f32)
    out_rows = jnp.concatenate(
        [out_sum[i * out_width : (i + 1) * out_width, :] for i in range(tokens // lanes)], axis=1
    )
    program = lax.broadcasted_iota(jnp.int32, (programs, tokens), 0)
    token = lax.broadcasted_iota(jnp.int32, (programs, tokens), 1) - program * length
    limit = jnp.zeros((programs, tokens), jnp.int32)
    for s in range(programs):
        limit = jnp.where(program == s, lengths[first + core * programs + s], limit)
    live = ((token >= 0) & (token < limit)).astype(f32)
    spread = (out_rows[:, None, :] * live[None, :, :]).reshape(out_width * programs, tokens)
    made = jnp.dot(spread.astype(bf16), in_sum, preferred_element_type=f32)
    held[...] = made.reshape(out_width, programs, lanes)
    mine_ref[...] = held[pl.ds(core * quarter, quarter), :, :].astype(bf16)
    other_ref[...] = held[pl.ds((1 - core) * quarter, quarter), :, :].astype(bf16)


def make_features(first, programs, quarter, place, lengths, left, came):
    vmem = pl.BlockSpec(memory_space=pltpu.VMEM)
    smem = pl.BlockSpec(memory_space=pltpu.SMEM)
    shape = jax.ShapeDtypeStruct((quarter, programs, lanes), bf16)
    return pl.pallas_call(
        functools.partial(feature_kernel, first, programs),
        in_specs=[smem, smem, vmem, vmem],
        out_specs=[vmem, vmem],
        out_shape=[shape, shape],
        scratch_shapes=[pltpu.VMEM((2 * quarter, programs, lanes), f32)],
        compiler_params=params(),
        cost_estimate=cost(10**8, 8 * left.size),
        name="features",
    )(place, lengths, left, came)


def score_kernel(count, squares_too, place, order_ref, *refs):
    pieces, refs = refs[:count], refs[count:]
    targets_ref, send_ref, keep_ref, squares_ref = refs[:4]
    ordered = refs[-1]
    rows = send_ref.shape[0]
    core, x = place[0], place[2]

    @pl.when(pl.program_id(0) == 0)
    def _():
        position_rows = order_ref[...]
        quarter = pieces[0].shape[1]
        row = lax.broadcasted_iota(jnp.int32, (2 * rows, position_rows.shape[1]), 0)
        first = jnp.where(row < rows, (x * 2 + 1 - core) * rows, (x * 2 + core) * rows - rows)
        chosen = (row + first == position_rows).astype(bf16)
        totals = jnp.zeros((2 * rows, lanes), f32)
        for a in range(0, quarter, 2):
            block = jnp.concatenate(
                [
                    jnp.concatenate([piece[i, a + d] for piece in pieces for i in range(2)], axis=0)
                    for d in range(2)
                ],
                axis=1,
            )
            found = jnp.dot(chosen, block, preferred_element_type=f32)
            ordered[:, a * lanes : (a + 2) * lanes] = found.astype(bf16)
            totals += found[:, :lanes] * found[:, :lanes] + found[:, lanes:] * found[:, lanes:]
        squares_ref[...] = jnp.sum(totals.T, axis=0, keepdims=True)

    block = targets_ref[...]
    scores = lax.dot_general(ordered[...], block, nt, preferred_element_type=f32).astype(bf16)
    send_ref[...] = scores[:rows, :]
    keep_ref[...] = scores[rows:, :]
    if squares_too:
        wide = block.astype(f32)
        wide = wide * wide
        totals = wide[:, :lanes]
        for k in range(1, wide.shape[1] // lanes):
            totals += wide[:, k * lanes : (k + 1) * lanes]
        refs[4][...] = jnp.sum(totals.T, axis=0, keepdims=True)


def partial_scores(squares_too, place, order, pieces, targets, rows):
    columns, depth = targets.shape
    tile = min(512, columns)
    whole = lambda *shape: pl.BlockSpec(shape, lambda j, place: (0,) * len(shape))
    strip = lambda height: pl.BlockSpec((height, tile), lambda j, place: (0, j))
    out_specs = [strip(rows), strip(rows), whole(1, 2 * rows)]
    out_shape = [
        jax.ShapeDtypeStruct((rows, columns), bf16),
        jax.ShapeDtypeStruct((rows, columns), bf16),
        jax.ShapeDtypeStruct((1, 2 * rows), f32),
    ]
    if squares_too:
        out_specs.append(strip(1))
        out_shape.append(jax.ShapeDtypeStruct((1, columns), f32))
    return pl.pallas_call(
        functools.partial(score_kernel, len(pieces), squares_too),
        grid_spec=pltpu.PrefetchScalarGridSpec(
            num_scalar_prefetch=1,
            grid=(columns // tile,),
            in_specs=[whole(*order.shape)]
            + [whole(*piece.shape) for piece in pieces]
            + [pl.BlockSpec((tile, depth), lambda j, place: (j, 0))],
            out_specs=out_specs,
            scratch_shapes=[pltpu.VMEM((2 * rows, depth), bf16)],
        ),
        out_shape=out_shape,
        compiler_params=params(),
        cost_estimate=cost(4 * rows * columns * depth, 2 * columns * depth),
        name="scores",
    )(place, order, *pieces, targets)


def shards(
    layer_input_rows,
    output_gradient_rows,
    adapter_up_weight,
    input_side_projection,
    rank_side_projection,
    lengths,
    program_output_index,
    targets,
):
    wide_count, narrow_count = lax.axis_size("wide"), lax.axis_size("narrow")
    w, n = lax.axis_index("wide"), lax.axis_index("narrow")
    core, x = n % 2, n // 2
    programs = lengths.shape[0]
    length = layer_input_rows.shape[0] // programs
    quarter = rank_side_projection.shape[1] // narrow_count
    share = programs // chunks // 2
    tokens = share * length
    place = jnp.stack([core, x]).astype(jnp.int32)
    rank = rank_side_projection.astype(f32).T

    pieces = []
    for chunk in range(chunks):
        send, keep = project(
            chunk,
            place,
            layer_input_rows,
            output_gradient_rows,
            input_side_projection,
            adapter_up_weight,
            rank,
        )
        send, left = core_sum(place, keep, exchange(send, "narrow", 1), tokens)
        came = exchange(send, "narrow", 2)
        mine, other = make_features(
            chunk * 2 * share, share, quarter, place, lengths, left, came
        )
        block = jnp.stack([mine, exchange(other, "narrow", 1)])
        pieces.append(gather_blocks(block))

    order = program_output_index.reshape(wide_count, chunks, 2, share)
    order = jnp.take(order, w ^ jnp.arange(wide_count), axis=0)
    order = jnp.take(order, core ^ jnp.arange(2), axis=2)
    order = order.transpose(1, 0, 2, 3).reshape(1, -1)
    pieces = [piece for chunk in pieces for piece in chunk]
    rows = order.shape[1] // narrow_count

    def scores(squares_too, x_index):
        where = jnp.stack([core, x, x_index]).astype(jnp.int32)
        return partial_scores(squares_too, where, order, pieces, targets, rows)

    far_send, far_keep, far_squares = scores(False, 1 - x)
    far = (far_keep.astype(f32) + exchange(far_send, "narrow", 1).astype(f32)).astype(bf16)
    far = exchange(far, "narrow", 2)
    near_send, near_keep, near_squares, target_squares = scores(True, x)
    near = near_keep.astype(f32) + exchange(near_send, "narrow", 1).astype(f32)

    far_squares = far_squares.reshape(2, rows)
    near_squares = near_squares.reshape(2, rows)
    groups = jnp.stack([far_squares, near_squares])
    groups = jnp.where(x == 1, groups, groups[::-1])
    groups = jnp.where(core == 1, groups, groups[:, ::-1])
    squares = jnp.concatenate([groups.reshape(-1), target_squares.reshape(-1)])
    squares = squares + exchange(squares, "narrow", 1)
    squares = squares + exchange(squares, "narrow", 2)
    row_squares = lax.dynamic_slice_in_dim(squares, n * rows, rows, 0)
    target_squares = squares[narrow_count * rows :]
    root_count = math.sqrt(float(targets.shape[1] * narrow_count))
    row_scale = lax.rsqrt(row_squares + epsilon) * root_count
    column_scale = lax.rsqrt(target_squares + epsilon)
    return (near + far.astype(f32)) * row_scale[:, None] * column_scale[None, :]


def solution(mesh):
    return jax.shard_map(
        shards,
        mesh=mesh,
        in_specs=(
            P("wide", "narrow"),
            P("wide", "narrow"),
            P("narrow", None),
            P("narrow", None),
            P(),
            P("wide"),
            P(),
            P("wide", "narrow"),
        ),
        out_specs=P("narrow", "wide"),
        check_vma=False,
    )
```

time: 94.9 us -> 94.5 us (level)
  matrix products: 24.1 us -> 0 us
  Pallas kernels: 0 us -> 20.7 us
  local copies, waits for them, and re-layouts: 3.27 us -> 11 us
  other arithmetic: 7.07 us -> 3.63 us
  waiting for transfers between devices: 41.3 us -> 39.7 us
    dot_general x12 -> x0, matrix products: 24.1 us -> none  [the longest x4 15.2 us: partial(): lax.dot_general(ordered.astype(bf16), targets, contract, preferred_elemen...]
    pallas_call x0 -> x8, Pallas kernels: none -> 20.7 us  [the longest x2 10.4 us: partial_scores(): pl.pallas_call(functools.partial(score_kernel, len(pieces), squares_too),...]
    unnamed x23 -> x16, local copies, waits for them, and re-layouts: 1.18 us -> 9.67 us
    reduce_sum x1 -> x0, other arithmetic: 5.08 us -> none  [shards(): target_squares = jnp.sum(wide_targets * wide_targets, axis=1)]
    ppermute x18 -> x25, waiting for transfers between devices: 41.3 us -> 39.7 us  [exchange(): return lax.ppermute(array, axis, [(i, i ^ bit) for i in range(count)])]
    convert_element_type x2 -> x1, other arithmetic: 0.13 us -> 1.17 us  [shards(): (far_keep.astype(f32) + exchange(far_send, 'narrow', 1).astype(f32)).asty...]
    ppermute x18 -> x25, starting transfers between devices: 18.6 us -> 18.9 us  [exchange(): return lax.ppermute(array, axis, [(i, i ^ bit) for i in range(count)])]
  transfers between devices with their start and end apart: 18 -> 25, of which waited for: 6 -> 12; matrix products, arithmetic and copies ran while one was open for 27% -> 3% of each run, Pallas kernels for 0% -> 13%
where the time goes in v2:
time: 94.5 us; the launch traced here: 94.1 us
  waiting for transfers between devices  39.7 us (42%)
  Pallas kernels  20.7 us (22%)
  starting transfers between devices  18.9 us (20%)
  local copies, waits for them, and re-layouts  11 us (12%)
  other arithmetic  3.63 us (4%)
    ppermute x25, waiting for transfers between devices, exchange(): return lax.ppermute(array, axis, [(i, i ^ bit) for i in range(count)])  39.7 us
    ppermute x25, starting transfers between devices, exchange(): return lax.ppermute(array, axis, [(i, i ^ bit) for i in range(count)])  18.9 us
    pallas_call x2, Pallas kernels, partial_scores(): pl.pallas_call(functools.partial(score_kernel, len(pieces), squares_too),...  10.4 us
    unnamed x16, local copies, waits for them, and re-layouts  9.67 us
    pallas_call x2, Pallas kernels, project(): pl.pallas_call(project_kernel, grid_spec=pltpu.PrefetchScalarGridSpec(num...  7.4 us
  transfers between devices with their start and end apart: 25, of which 12 were waited for; matrix products, arithmetic and copies ran while one was open for 3% of the time, Pallas kernels for 13%

profile of v2, /device:TPU:0, one launch (start us, length us, event | category | flops | bytes accessed | tf_op | source)
XLA Modules:
  0.0 94.1 jit_solution(6807546818790906046)
XLA Ops:
  0.0 0.7 convert_bitcast_fusion.rank_ref
  0.8 2.2 %copy-done.2 = bf16[2048,1024]{1,0:T(8,128)(2,1)S(1)} copy-done((bf16[2048,1024]{1,0:T(8,128)(2,1)S(1)}, bf16[2048,1024]{1,0:T(8,128)(2,1)}, u32[]{:S(2)}) %copy-start.2) | copy-done | bytes 4194328
  3.0 2.2 %copy-done.3 = bf16[2048,1024]{1,0:T(8,128)(2,1)S(1)} copy-done((bf16[2048,1024]{1,0:T(8,128)(2,1)S(1)}, bf16[2048,1024]{1,0:T(8,128)(2,1)}, u32[]{:S(2)}) %copy-start.3) | copy-done | bytes 4194328
  5.2 0.9 %copy-done.4 = bf16[1024,128]{1,0:T(8,128)(2,1)S(1)} copy-done((bf16[1024,128]{1,0:T(8,128)(2,1)S(1)}, bf16[1024,128]{1,0:T(8,128)(2,1)}, u32[]{:S(2)}) %copy-start.4) | copy-done | bytes 262168
  6.1 0.9 %copy-done.5 = bf16[1024,128]{1,0:T(8,128)(2,1)S(1)} copy-done((bf16[1024,128]{1,0:T(8,128)(2,1)S(1)}, bf16[1024,128]{1,0:T(8,128)(2,1)}, u32[]{:S(2)}) %copy-start.5) | copy-done | bytes 262168
  7.1 3.7 %project.2 = (bf16[768,128]{1,0:T(8,128)(2,1)S(1)}, f32[768,128]{1,0:T(8,128)S(1)}) custom-call(s32[2]{0:T(128)S(1)} %pad_add_fusion.2.place, bf16[2048,1024]{1,0:T(8,128)(2,1)S(1)} %copy-done.2, bf16[2048,1024]{1,0:T(8,128)(2,1)S(1)} %copy-done.3, bf16[1024,128]{1,0:T(8,128)(2,1)S(1)} %copy-done.4, bf16[1024,128]{1,0:T(8,128)(2,1)S(1)} %copy-done.5, ...), custom_call_target="tpu_custom_call" | custom-call | flops 536870912 | bytes 4194304 | tf_op jit(solution)/shard_map/project/pallas_call | solution.py:86
  10.8 0.5 collective-permute-start
  11.3 3.7 %project.3 = (bf16[768,128]{1,0:T(8,128)(2,1)S(1)}, f32[768,128]{1,0:T(8,128)S(1)}) custom-call(s32[2]{0:T(128)S(1)} %pad_add_fusion.2.place, bf16[2048,1024]{1,0:T(8,128)(2,1)S(1)} %copy-done.2, bf16[2048,1024]{1,0:T(8,128)(2,1)S(1)} %copy-done.3, bf16[1024,128]{1,0:T(8,128)(2,1)S(1)} %copy-done.4, bf16[1024,128]{1,0:T(8,128)(2,1)S(1)} %copy-done.5, ...), custom_call_target="tpu_custom_call" | custom-call | flops 536870912 | bytes 4194304 | tf_op jit(solution)/shard_map/project/pallas_call | solution.py:86
  15.0 0.1 collective-permute-start.10
  15.2 0.6 core_sum.2
  15.7 3.0 %collective-permute-start.1 = (bf16[640,128]{1,0:T(8,128)(2,1)S(1)}, bf16[640,128]{1,0:T(8,128)(2,1)S(1)}, u32[]{:S(2)}, u32[]{:S(2)}) collective-permute-start(bf16[640,128]{1,0:T(8,128)(2,1)S(1)} %get-tuple-element.27), channel_id=1, source_target_pairs={{0,2},{1,3},{2,0},{3,1},{4,6},{5,7},{6,4},{7,5},{8,10},{9,11},{10,... | collective-permute-start | bytes 491528 | tf_op jit(solution)/shard_map/ppermute | solution.py:28
  18.8 0.6 core_sum.3
  19.3 0.5 collective-permute-start.11
  19.8 3.9 %collective-permute-done.1.came_ref = bf16[640,128]{1,0:T(8,128)(2,1)S(1)} collective-permute-done((bf16[640,128]{1,0:T(8,128)(2,1)S(1)}, bf16[640,128]{1,0:T(8,128)(2,1)S(1)}, u32[]{:S(2)}, u32[]{:S(2)}) %collective-permute-start.1) | collective-permute-done | bytes 163872 | tf_op jit(solution)/shard_map/ppermute | solution.py:28
  23.7 0.9 features.2
  24.8 0.6 gather_fusion
  25.4 1.2 %collective-permute-done.11.came_ref = bf16[640,128]{1,0:T(8,128)(2,1)S(1)} collective-permute-done((bf16[640,128]{1,0:T(8,128)(2,1)S(1)}, bf16[640,128]{1,0:T(8,128)(2,1)S(1)}, u32[]{:S(2)}, u32[]{:S(2)}) %collective-permute-start.11) | collective-permute-done | bytes 163872 | tf_op jit(solution)/shard_map/ppermute | solution.py:28
  26.6 0.9 features.3
  27.6 1.8 %collective-permute-start.3 = (bf16[2,16,16,128]{3,2,1,0:T(8,128)(2,1)S(1)}, bf16[2,16,16,128]{3,2,1,0:T(8,128)(2,1)S(1)}, u32[]{:S(2)}, u32[]{:S(2)}) collective-permute-start(bf16[2,16,16,128]{3,2,1,0:T(8,128)(2,1)S(1)} %pad_maximum_fusion.refs_0_), channel_id=1, source_target_pairs={{0,4},{4,0},{8,12},{12,8},{16,20},{20,16},{24,28},{28,24},{1,5},{5... | collective-permute-start | bytes 393224 | tf_op jit(solution)/shard_map/ppermute | solution.py:28
  29.5 1.6 %collective-permute-start.4 = (bf16[2,16,16,128]{3,2,1,0:T(8,128)(2,1)S(1)}, bf16[2,16,16,128]{3,2,1,0:T(8,128)(2,1)S(1)}, u32[]{:S(2)}, u32[]{:S(2)}) collective-permute-start(bf16[2,16,16,128]{3,2,1,0:T(8,128)(2,1)S(1)} %pad_maximum_fusion.refs_0_), channel_id=1, source_target_pairs={{0,8},{4,12},{8,0},{12,4},{16,24},{20,28},{24,16},{28,20},{1,9},{5... | collective-permute-start | bytes 393224 | tf_op jit(solution)/shard_map/ppermute | solution.py:28
  31.1 2.6 %collective-permute-start.6 = (bf16[2,16,16,128]{3,2,1,0:T(8,128)(2,1)S(1)}, bf16[2,16,16,128]{3,2,1,0:T(8,128)(2,1)S(1)}, u32[]{:S(2)}, u32[]{:S(2)}) collective-permute-start(bf16[2,16,16,128]{3,2,1,0:T(8,128)(2,1)S(1)} %pad_maximum_fusion.refs_0_), channel_id=1, source_target_pairs={{0,16},{4,20},{8,24},{12,28},{16,0},{20,4},{24,8},{28,12},{1,17},{... | collective-permute-start | bytes 393224 | tf_op jit(solution)/shard_map/ppermute | solution.py:28
  33.7 0.4 collective-permute-start.16
  34.2 0.6 collective-permute-start.13
  34.7 0.7 collective-permute-start.14
  35.4 2.8 %collective-permute-done.4.refs_2_ = bf16[2,16,16,128]{3,2,1,0:T(8,128)(2,1)S(1)} collective-permute-done((bf16[2,16,16,128]{3,2,1,0:T(8,128)(2,1)S(1)}, bf16[2,16,16,128]{3,2,1,0:T(8,128)(2,1)S(1)}, u32[]{:S(2)}, u32[]{:S(2)}) %collective-permute-start.4) | collective-permute-done | bytes 131104 | tf_op jit(solution)/shard_map/ppermute | solution.py:28
  38.2 5.4 %collective-permute-done.6.refs_4_ = bf16[2,16,16,128]{3,2,1,0:T(8,128)(2,1)S(1)} collective-permute-done((bf16[2,16,16,128]{3,2,1,0:T(8,128)(2,1)S(1)}, bf16[2,16,16,128]{3,2,1,0:T(8,128)(2,1)S(1)}, u32[]{:S(2)}, u32[]{:S(2)}) %collective-permute-start.6) | collective-permute-done | bytes 131104 | tf_op jit(solution)/shard_map/ppermute | solution.py:28
  43.6 2.1 %collective-permute-done.16.refs_12_ = bf16[2,16,16,128]{3,2,1,0:T(8,128)(2,1)S(1)} collective-permute-done((bf16[2,16,16,128]{3,2,1,0:T(8,128)(2,1)S(1)}, bf16[2,16,16,128]{3,2,1,0:T(8,128)(2,1)S(1)}, u32[]{:S(2)}, u32[]{:S(2)}) %collective-permute-start.16) | collective-permute-done | bytes 131104 | tf_op jit(solution)/shard_map/ppermute | solution.py:28
  45.8 0.5 gather_fusion.1
  46.4 0.6 collective-permute-start.7
  46.9 1.5 %collective-permute-start.17 = (bf16[2,16,16,128]{3,2,1,0:T(8,128)(2,1)S(1)}, bf16[2,16,16,128]{3,2,1,0:T(8,128)(2,1)S(1)}, u32[]{:S(2)}, u32[]{:S(2)}) collective-permute-start(bf16[2,16,16,128]{3,2,1,0:T(8,128)(2,1)S(1)} %collective-permute-done.16.refs_12_), channel_id=1, source_target_pairs={{0,4},{4,0},{8,12},{12,8},{16,20},{20,16},{24,28},{28,24},{1,5},{5... | collective-permute-start | bytes 393224 | tf_op jit(solution)/shard_map/ppermute | solution.py:28
  48.5 0.5 collective-permute-start.15
  49.0 0.4 collective-permute-done.8.refs_6_
  49.4 1.1 %collective-permute-start.9 = (bf16[2,16,16,128]{3,2,1,0:T(8,128)(2,1)S(1)}, bf16[2,16,16,128]{3,2,1,0:T(8,128)(2,1)S(1)}, u32[]{:S(2)}, u32[]{:S(2)}) collective-permute-start(bf16[2,16,16,128]{3,2,1,0:T(8,128)(2,1)S(1)} %collective-permute-done.8.refs_6_), channel_id=1, source_target_pairs={{0,4},{4,0},{8,12},{12,8},{16,20},{20,16},{24,28},{28,24},{1,5},{5... | collective-permute-start | bytes 393224 | tf_op jit(solution)/shard_map/ppermute | solution.py:28
  50.5 0.9 collective-permute-done.18.refs_14_
  51.4 0.5 collective-permute-start.19
  52.1 0.7 collective-permute-done.7.refs_5_
  52.9 5.6 %collective-permute-done.15.refs_11_ = bf16[2,16,16,128]{3,2,1,0:T(8,128)(2,1)S(1)} collective-permute-done((bf16[2,16,16,128]{3,2,1,0:T(8,128)(2,1)S(1)}, bf16[2,16,16,128]{3,2,1,0:T(8,128)(2,1)S(1)}, u32[]{:S(2)}, u32[]{:S(2)}) %collective-permute-start.15) | collective-permute-done | bytes 131104 | tf_op jit(solution)/shard_map/ppermute | solution.py:28
  58.5 2.6 %collective-permute-done.9.refs_7_ = bf16[2,16,16,128]{3,2,1,0:T(8,128)(2,1)S(1)} collective-permute-done((bf16[2,16,16,128]{3,2,1,0:T(8,128)(2,1)S(1)}, bf16[2,16,16,128]{3,2,1,0:T(8,128)(2,1)S(1)}, u32[]{:S(2)}, u32[]{:S(2)}) %collective-permute-start.9) | collective-permute-done | bytes 131104 | tf_op jit(solution)/shard_map/ppermute | solution.py:28
  61.1 1.4 %collective-permute-done.19.refs_15_ = bf16[2,16,16,128]{3,2,1,0:T(8,128)(2,1)S(1)} collective-permute-done((bf16[2,16,16,128]{3,2,1,0:T(8,128)(2,1)S(1)}, bf16[2,16,16,128]{3,2,1,0:T(8,128)(2,1)S(1)}, u32[]{:S(2)}, u32[]{:S(2)}) %collective-permute-start.19) | collective-permute-done | bytes 131104 | tf_op jit(solution)/shard_map/ppermute | solution.py:28
  62.5 3.4 %copy-done = bf16[2048,2048]{1,0:T(8,128)(2,1)S(1)} copy-done((bf16[2048,2048]{1,0:T(8,128)(2,1)S(1)}, bf16[2048,2048]{1,0:T(8,128)(2,1)}, u32[]{:S(2)}) %copy-start) | copy-done | bytes 8388632
  65.9 5.1 %scores.3 = (bf16[128,2048]{1,0:T(8,128)(2,1)}, bf16[128,2048]{1,0:T(8,128)(2,1)S(1)}, f32[1,256]{1,0:T(1,128)S(1)}) custom-call(s32[3]{0:T(128)S(1)} %get-tuple-element.44.place, s32[1,512]{1,0:T(1,128)S(1)} %reshape.57.order_ref, bf16[2,16,16,128]{3,2,1,0:T(8,128)(2,1)S(1)} %pad_maximum_fusion.refs_0_, ...), custom_call_target="tpu_custom_call" | custom-call | flops 2147483648 | bytes 8388608 | tf_op jit(solution)/shard_map/scores/pallas_call | solution.py:239
  71.0 5.3 %scores.2 = (bf16[128,2048]{1,0:T(8,128)(2,1)}, bf16[128,2048]{1,0:T(8,128)(2,1)S(1)}, f32[1,256]{1,0:T(1,128)S(1)}, f32[1,2048]{1,0:T(1,128)S(1)}) custom-call(s32[3]{0:T(128)S(1)} %get-tuple-element.43.place, s32[1,512]{1,0:T(1,128)S(1)} %reshape.57.order_ref, bf16[2,16,16,128]{3,2,1,0:T(8,128)(2,1)S(1)} %pad_maximum_fusion.refs_0_, ...), custom_call_target="tpu_custom_call" | custom-call | flops 2147483648 | bytes 8388608 | tf_op jit(solution)/shard_map/scores/pallas_call | solution.py:239
  76.3 0.5 collective-permute-start.20
  76.9 1.2 %add_convert_fusion = bf16[128,2048]{1,0:T(8,128)(2,1)S(1)} fusion(bf16[128,2048]{1,0:T(8,128)(2,1)} %collective-permute-done.21, bf16[128,2048]{1,0:T(8,128)(2,1)S(1)} %get-tuple-element.38), kind=kLoop, calls=%fused_computation.3 | loop fusion | flops 1048576 | bytes 1572864 | tf_op jit(solution)/shard_map/convert_element_type | solution.py:309
  78.1 1.6 %collective-permute-start.22 = (bf16[128,2048]{1,0:T(8,128)(2,1)S(1)}, bf16[128,2048]{1,0:T(8,128)(2,1)S(1)}, u32[]{:S(2)}, u32[]{:S(2)}) collective-permute-start(bf16[128,2048]{1,0:T(8,128)(2,1)S(1)} %add_convert_fusion), channel_id=1, source_target_pairs={{0,2},{1,3},{2,0},{3,1},{4,6},{5,7},{6,4},{7,5},{8,10},{9,11},{10,... | collective-permute-start | bytes 1572872 | tf_op jit(solution)/shard_map/ppermute | solution.py:28
  79.7 0.6 collective-permute-start.24
  80.3 12.5 %collective-permute-done.24 = f32[2560]{0:T(1024)S(1)} collective-permute-done((f32[2560]{0:T(1024)S(1)}, f32[2560]{0:T(1024)S(1)}, u32[]{:S(2)}, u32[]{:S(2)}) %collective-permute-start.24) | collective-permute-done | bytes 10272 | tf_op jit(solution)/shard_map/ppermute | solution.py:28
  92.9 1.3 %multiply_multiply_fusion = f32[128,2048]{1,0:T(8,128)} fusion(bf16[128,2048]{1,0:T(8,128)(2,1)S(1)} %collective-permute-done.22, bf16[128,2048]{1,0:T(8,128)(2,1)S(1)} %collective-permute-done.20, bf16[128,2048]{1,0:T(8,128)(2,1)S(1)} %get-tuple-element.36, f32[2048]{0:T(1024)S(1)} %fusion, f32[128]{0:T(128)S(1)} %rsqrt_multiply_fusion), kind=kLoop, calls=%fused_computation.2 | loop fusion | flops 1835008 | bytes 2630144 | tf_op jit(solution)/shard_map/mul | solution.py:327
  (56 shorter events, 1.0 us)
Async XLA Ops:
  0.8 2.2 %copy-start.2 = (bf16[2048,1024]{1,0:T(8,128)(2,1)S(1)}, bf16[2048,1024]{1,0:T(8,128)(2,1)}, u32[]{:S(2)}) copy-start(bf16[2048,1024]{1,0:T(8,128)(2,1)} %x_ref.3) | copy-start | bytes 12582916
  3.0 2.2 %copy-start.3 = (bf16[2048,1024]{1,0:T(8,128)(2,1)S(1)}, bf16[2048,1024]{1,0:T(8,128)(2,1)}, u32[]{:S(2)}) copy-start(bf16[2048,1024]{1,0:T(8,128)(2,1)} %g_ref.3) | copy-start | bytes 12582916
  5.2 0.9 %copy-start.4 = (bf16[1024,128]{1,0:T(8,128)(2,1)S(1)}, bf16[1024,128]{1,0:T(8,128)(2,1)}, u32[]{:S(2)}) copy-start(bf16[1024,128]{1,0:T(8,128)(2,1)} %w_ref.3) | copy-start | bytes 786436
  6.1 0.9 %copy-start.5 = (bf16[1024,128]{1,0:T(8,128)(2,1)S(1)}, bf16[1024,128]{1,0:T(8,128)(2,1)}, u32[]{:S(2)}) copy-start(bf16[1024,128]{1,0:T(8,128)(2,1)} %up_ref.3) | copy-start | bytes 786436
  10.8 13.0 %copy-start.6 = (s32[64]{0:T(128)S(1)}, s32[64]{0:T(128)}, u32[]{:S(2)}) copy-start(s32[64]{0:T(128)} %lengths.3) | copy-start | bytes 772
  10.8 13.9 %copy-start.7 = (s32[512]{0:T(512)S(1)}, s32[512]{0:T(512)}, u32[]{:S(2)}) copy-start(s32[512]{0:T(512)} %param.14) | copy-start | bytes 6148
  10.8 4.4 %collective-permute-start = (bf16[768,128]{1,0:T(8,128)(2,1)S(1)}, bf16[768,128]{1,0:T(8,128)(2,1)S(1)}, u32[]{:S(2)}, u32[]{:S(2)}) collective-permute-start(bf16[768,128]{1,0:T(8,128)(2,1)S(1)} %get-tuple-element.25), channel_id=1, source_target_pairs={{0,1},{1,0},{2,3},{3,2},{4,5},{5,4},{6,7},{7,6},{8,9},{9,8},{10,11... | collective-permute-start | bytes 589832 | tf_op jit(solution)/shard_map/ppermute | solution.py:28
  15.0 3.7 %collective-permute-start.10 = (bf16[768,128]{1,0:T(8,128)(2,1)S(1)}, bf16[768,128]{1,0:T(8,128)(2,1)S(1)}, u32[]{:S(2)}, u32[]{:S(2)}) collective-permute-start(bf16[768,128]{1,0:T(8,128)(2,1)S(1)} %get-tuple-element.31), channel_id=1, source_target_pairs={{0,1},{1,0},{2,3},{3,2},{4,5},{5,4},{6,7},{7,6},{8,9},{9,8},{10,11... | collective-permute-start | bytes 589832 | tf_op jit(solution)/shard_map/ppermute | solution.py:28
  15.7 8.0 %collective-permute-start.1 = (bf16[640,128]{1,0:T(8,128)(2,1)S(1)}, bf16[640,128]{1,0:T(8,128)(2,1)S(1)}, u32[]{:S(2)}, u32[]{:S(2)}) collective-permute-start(bf16[640,128]{1,0:T(8,128)(2,1)S(1)} %get-tuple-element.27), channel_id=1, source_target_pairs={{0,2},{1,3},{2,0},{3,1},{4,6},{5,7},{6,4},{7,5},{8,10},{9,11},{10,... | collective-permute-start | bytes 491528 | tf_op jit(solution)/shard_map/ppermute | solution.py:28
  19.3 7.3 %collective-permute-start.11 = (bf16[640,128]{1,0:T(8,128)(2,1)S(1)}, bf16[640,128]{1,0:T(8,128)(2,1)S(1)}, u32[]{:S(2)}, u32[]{:S(2)}) collective-permute-start(bf16[640,128]{1,0:T(8,128)(2,1)S(1)} %get-tuple-element.33), channel_id=1, source_target_pairs={{0,2},{1,3},{2,0},{3,1},{4,6},{5,7},{6,4},{7,5},{8,10},{9,11},{10,... | collective-permute-start | bytes 491528 | tf_op jit(solution)/shard_map/ppermute | solution.py:28
  24.6 3.0 %collective-permute-start.2 = (bf16[16,16,128]{2,1,0:T(8,128)(2,1)S(1)}, bf16[16,16,128]{2,1,0:T(8,128)(2,1)S(1)}, u32[]{:S(2)}, u32[]{:S(2)}) collective-permute-start(bf16[16,16,128]{2,1,0:T(8,128)(2,1)S(1)} %get-tuple-element.29), channel_id=1, source_target_pairs={{0,1},{1,0},{2,3},{3,2},{4,5},{5,4},{6,7},{7,6},{8,9},{9,8},{10,11... | collective-permute-start | bytes 196616 | tf_op jit(solution)/shard_map/ppermute | solution.py:28
  27.5 6.1 %collective-permute-start.12 = (bf16[16,16,128]{2,1,0:T(8,128)(2,1)S(1)}, bf16[16,16,128]{2,1,0:T(8,128)(2,1)S(1)}, u32[]{:S(2)}, u32[]{:S(2)}) collective-permute-start(bf16[16,16,128]{2,1,0:T(8,128)(2,1)S(1)} %get-tuple-element.35), channel_id=1, source_target_pairs={{0,1},{1,0},{2,3},{3,2},{4,5},{5,4},{6,7},{7,6},{8,9},{9,8},{10,11... | collective-permute-start | bytes 196616 | tf_op jit(solution)/shard_map/ppermute | solution.py:28
  27.6 7.1 %collective-permute-start.3 = (bf16[2,16,16,128]{3,2,1,0:T(8,128)(2,1)S(1)}, bf16[2,16,16,128]{3,2,1,0:T(8,128)(2,1)S(1)}, u32[]{:S(2)}, u32[]{:S(2)}) collective-permute-start(bf16[2,16,16,128]{3,2,1,0:T(8,128)(2,1)S(1)} %pad_maximum_fusion.refs_0_), channel_id=1, source_target_pairs={{0,4},{4,0},{8,12},{12,8},{16,20},{20,16},{24,28},{28,24},{1,5},{5... | collective-permute-start | bytes 393224 | tf_op jit(solution)/shard_map/ppermute | solution.py:28
  29.5 8.7 %collective-permute-start.4 = (bf16[2,16,16,128]{3,2,1,0:T(8,128)(2,1)S(1)}, bf16[2,16,16,128]{3,2,1,0:T(8,128)(2,1)S(1)}, u32[]{:S(2)}, u32[]{:S(2)}) collective-permute-start(bf16[2,16,16,128]{3,2,1,0:T(8,128)(2,1)S(1)} %pad_maximum_fusion.refs_0_), channel_id=1, source_target_pairs={{0,8},{4,12},{8,0},{12,4},{16,24},{20,28},{24,16},{28,20},{1,9},{5... | collective-permute-start | bytes 393224 | tf_op jit(solution)/shard_map/ppermute | solution.py:28
  31.1 12.5 %collective-permute-start.6 = (bf16[2,16,16,128]{3,2,1,0:T(8,128)(2,1)S(1)}, bf16[2,16,16,128]{3,2,1,0:T(8,128)(2,1)S(1)}, u32[]{:S(2)}, u32[]{:S(2)}) collective-permute-start(bf16[2,16,16,128]{3,2,1,0:T(8,128)(2,1)S(1)} %pad_maximum_fusion.refs_0_), channel_id=1, source_target_pairs={{0,16},{4,20},{8,24},{12,28},{16,0},{20,4},{24,8},{28,12},{1,17},{... | collective-permute-start | bytes 393224 | tf_op jit(solution)/shard_map/ppermute | solution.py:28
  33.7 12.1 %collective-permute-start.16 = (bf16[2,16,16,128]{3,2,1,0:T(8,128)(2,1)S(1)}, bf16[2,16,16,128]{3,2,1,0:T(8,128)(2,1)S(1)}, u32[]{:S(2)}, u32[]{:S(2)}) collective-permute-start(bf16[2,16,16,128]{3,2,1,0:T(8,128)(2,1)S(1)} %pad_maximum_fusion.1.refs_8_), channel_id=1, source_target_pairs={{0,16},{4,20},{8,24},{12,28},{16,0},{20,4},{24,8},{28,12},{1,17},{... | collective-permute-start | bytes 393224 | tf_op jit(solution)/shard_map/ppermute | solution.py:28
  34.2 12.2 %collective-permute-start.13 = (bf16[2,16,16,128]{3,2,1,0:T(8,128)(2,1)S(1)}, bf16[2,16,16,128]{3,2,1,0:T(8,128)(2,1)S(1)}, u32[]{:S(2)}, u32[]{:S(2)}) collective-permute-start(bf16[2,16,16,128]{3,2,1,0:T(8,128)(2,1)S(1)} %pad_maximum_fusion.1.refs_8_), channel_id=1, source_target_pairs={{0,4},{4,0},{8,12},{12,8},{16,20},{20,16},{24,28},{28,24},{1,5},{5... | collective-permute-start | bytes 393224 | tf_op jit(solution)/shard_map/ppermute | solution.py:28
  34.7 12.2 %collective-permute-start.14 = (bf16[2,16,16,128]{3,2,1,0:T(8,128)(2,1)S(1)}, bf16[2,16,16,128]{3,2,1,0:T(8,128)(2,1)S(1)}, u32[]{:S(2)}, u32[]{:S(2)}) collective-permute-start(bf16[2,16,16,128]{3,2,1,0:T(8,128)(2,1)S(1)} %pad_maximum_fusion.1.refs_8_), channel_id=1, source_target_pairs={{0,8},{4,12},{8,0},{12,4},{16,24},{20,28},{24,16},{28,20},{1,9},{5... | collective-permute-start | bytes 393224 | tf_op jit(solution)/shard_map/ppermute | solution.py:28
  38.2 10.2 %collective-permute-start.5 = (bf16[2,16,16,128]{3,2,1,0:T(8,128)(2,1)S(1)}, bf16[2,16,16,128]{3,2,1,0:T(8,128)(2,1)S(1)}, u32[]{:S(2)}, u32[]{:S(2)}) collective-permute-start(bf16[2,16,16,128]{3,2,1,0:T(8,128)(2,1)S(1)} %collective-permute-done.4.refs_2_), channel_id=1, source_target_pairs={{0,4},{4,0},{8,12},{12,8},{16,20},{20,16},{24,28},{28,24},{1,5},{5... | collective-permute-start | bytes 393224 | tf_op jit(solution)/shard_map/ppermute | solution.py:28
  43.6 5.8 %collective-permute-start.8 = (bf16[2,16,16,128]{3,2,1,0:T(8,128)(2,1)S(1)}, bf16[2,16,16,128]{3,2,1,0:T(8,128)(2,1)S(1)}, u32[]{:S(2)}, u32[]{:S(2)}) collective-permute-start(bf16[2,16,16,128]{3,2,1,0:T(8,128)(2,1)S(1)} %collective-permute-done.6.refs_4_), channel_id=1, source_target_pairs={{0,8},{4,12},{8,0},{12,4},{16,24},{20,28},{24,16},{28,20},{1,9},{5... | collective-permute-start | bytes 393224 | tf_op jit(solution)/shard_map/ppermute | solution.py:28
  45.8 5.6 %collective-permute-start.18 = (bf16[2,16,16,128]{3,2,1,0:T(8,128)(2,1)S(1)}, bf16[2,16,16,128]{3,2,1,0:T(8,128)(2,1)S(1)}, u32[]{:S(2)}, u32[]{:S(2)}) collective-permute-start(bf16[2,16,16,128]{3,2,1,0:T(8,128)(2,1)S(1)} %collective-permute-done.16.refs_12_), channel_id=1, source_target_pairs={{0,8},{4,12},{8,0},{12,4},{16,24},{20,28},{24,16},{28,20},{1,9},{5... | collective-permute-start | bytes 393224 | tf_op jit(solution)/shard_map/ppermute | solution.py:28
  46.4 6.5 %collective-permute-start.7 = (bf16[2,16,16,128]{3,2,1,0:T(8,128)(2,1)S(1)}, bf16[2,16,16,128]{3,2,1,0:T(8,128)(2,1)S(1)}, u32[]{:S(2)}, u32[]{:S(2)}) collective-permute-start(bf16[2,16,16,128]{3,2,1,0:T(8,128)(2,1)S(1)} %collective-permute-done.6.refs_4_), channel_id=1, source_target_pairs={{0,4},{4,0},{8,12},{12,8},{16,20},{20,16},{24,28},{28,24},{1,5},{5... | collective-permute-start | bytes 393224 | tf_op jit(solution)/shard_map/ppermute | solution.py:28
  46.9 11.5 %collective-permute-start.17 = (bf16[2,16,16,128]{3,2,1,0:T(8,128)(2,1)S(1)}, bf16[2,16,16,128]{3,2,1,0:T(8,128)(2,1)S(1)}, u32[]{:S(2)}, u32[]{:S(2)}) collective-permute-start(bf16[2,16,16,128]{3,2,1,0:T(8,128)(2,1)S(1)} %collective-permute-done.16.refs_12_), channel_id=1, source_target_pairs={{0,4},{4,0},{8,12},{12,8},{16,20},{20,16},{24,28},{28,24},{1,5},{5... | collective-permute-start | bytes 393224 | tf_op jit(solution)/shard_map/ppermute | solution.py:28
  48.5 10.0 %collective-permute-start.15 = (bf16[2,16,16,128]{3,2,1,0:T(8,128)(2,1)S(1)}, bf16[2,16,16,128]{3,2,1,0:T(8,128)(2,1)S(1)}, u32[]{:S(2)}, u32[]{:S(2)}) collective-permute-start(bf16[2,16,16,128]{3,2,1,0:T(8,128)(2,1)S(1)} %collective-permute-done.14.refs_10_), channel_id=1, source_target_pairs={{0,4},{4,0},{8,12},{12,8},{16,20},{20,16},{24,28},{28,24},{1,5},{5... | collective-permute-start | bytes 393224 | tf_op jit(solution)/shard_map/ppermute | solution.py:28
  49.4 11.7 %collective-permute-start.9 = (bf16[2,16,16,128]{3,2,1,0:T(8,128)(2,1)S(1)}, bf16[2,16,16,128]{3,2,1,0:T(8,128)(2,1)S(1)}, u32[]{:S(2)}, u32[]{:S(2)}) collective-permute-start(bf16[2,16,16,128]{3,2,1,0:T(8,128)(2,1)S(1)} %collective-permute-done.8.refs_6_), channel_id=1, source_target_pairs={{0,4},{4,0},{8,12},{12,8},{16,20},{20,16},{24,28},{28,24},{1,5},{5... | collective-permute-start | bytes 393224 | tf_op jit(solution)/shard_map/ppermute | solution.py:28
  51.4 11.1 %collective-permute-start.19 = (bf16[2,16,16,128]{3,2,1,0:T(8,128)(2,1)S(1)}, bf16[2,16,16,128]{3,2,1,0:T(8,128)(2,1)S(1)}, u32[]{:S(2)}, u32[]{:S(2)}) collective-permute-start(bf16[2,16,16,128]{3,2,1,0:T(8,128)(2,1)S(1)} %collective-permute-done.18.refs_14_), channel_id=1, source_target_pairs={{0,4},{4,0},{8,12},{12,8},{16,20},{20,16},{24,28},{28,24},{1,5},{5... | collective-permute-start | bytes 393224 | tf_op jit(solution)/shard_map/ppermute | solution.py:28
  62.5 3.4 %copy-start = (bf16[2048,2048]{1,0:T(8,128)(2,1)S(1)}, bf16[2048,2048]{1,0:T(8,128)(2,1)}, u32[]{:S(2)}) copy-start(bf16[2048,2048]{1,0:T(8,128)(2,1)} %refs_16_.3) | copy-start | bytes 25165828
  65.9 5.1 %copy-start.1 = (bf16[2048,2048]{1,0:T(8,128)(2,1)S(1)}, bf16[2048,2048]{1,0:T(8,128)(2,1)}, u32[]{:S(2)}) copy-start(bf16[2048,2048]{1,0:T(8,128)(2,1)} %refs_16_.3) | copy-start | bytes 25165828
  71.0 6.0 %collective-permute-start.21 = (bf16[128,2048]{1,0:T(8,128)(2,1)}, bf16[128,2048]{1,0:T(8,128)(2,1)}, u32[]{:S(2)}, u32[]{:S(2)}) collective-permute-start(bf16[128,2048]{1,0:T(8,128)(2,1)} %get-tuple-element.39), channel_id=1, source_target_pairs={{0,1},{1,0},{2,3},{3,2},{4,5},{5,4},{6,7},{7,6},{8,9},{9,8},{10,11... | collective-permute-start | bytes 1572872 | tf_op jit(solution)/shard_map/ppermute | solution.py:28
  76.3 16.6 %collective-permute-start.20 = (bf16[128,2048]{1,0:T(8,128)(2,1)}, bf16[128,2048]{1,0:T(8,128)(2,1)S(1)}, u32[]{:S(2)}, u32[]{:S(2)}) collective-permute-start(bf16[128,2048]{1,0:T(8,128)(2,1)} %get-tuple-element.37), channel_id=1, source_target_pairs={{0,1},{1,0},{2,3},{3,2},{4,5},{5,4},{6,7},{7,6},{8,9},{9,8},{10,11... | collective-permute-start | bytes 1572872 | tf_op jit(solution)/shard_map/ppermute | solution.py:28
  76.9 2.8 %collective-permute-start.23 = (f32[2560]{0:T(1024)S(1)}, f32[2560]{0:T(1024)S(1)}, u32[]{:S(2)}, u32[]{:S(2)}) collective-permute-start(f32[2560]{0:T(1024)S(1)} %pad_maximum_fusion.2), channel_id=1, source_target_pairs={{0,1},{1,0},{2,3},{3,2},{4,5},{5,4},{6,7},{7,6},{8,9},{9,8},{10,11... | collective-permute-start | bytes 30728 | tf_op jit(solution)/shard_map/ppermute | solution.py:28
  78.1 14.7 %collective-permute-start.22 = (bf16[128,2048]{1,0:T(8,128)(2,1)S(1)}, bf16[128,2048]{1,0:T(8,128)(2,1)S(1)}, u32[]{:S(2)}, u32[]{:S(2)}) collective-permute-start(bf16[128,2048]{1,0:T(8,128)(2,1)S(1)} %add_convert_fusion), channel_id=1, source_target_pairs={{0,2},{1,3},{2,0},{3,1},{4,6},{5,7},{6,4},{7,5},{8,10},{9,11},{10,... | collective-permute-start | bytes 1572872 | tf_op jit(solution)/shard_map/ppermute | solution.py:28
  79.7 13.1 %collective-permute-start.24 = (f32[2560]{0:T(1024)S(1)}, f32[2560]{0:T(1024)S(1)}, u32[]{:S(2)}, u32[]{:S(2)}) collective-permute-start(f32[2560]{0:T(1024)S(1)} %fusion.3), channel_id=1, source_target_pairs={{0,2},{1,3},{2,0},{3,1},{4,6},{5,7},{6,4},{7,5},{8,10},{9,11},{10,... | collective-permute-start | bytes 30728 | tf_op jit(solution)/shard_map/ppermute | solution.py:28

commit v3 on v0

v3 whole, which is shorter than its diff:
```python
import functools
import math

import jax
import jax.numpy as jnp
from jax import lax
from jax.experimental import pallas as pl
from jax.experimental.pallas import tpu as pltpu
from jax.sharding import PartitionSpec as P

epsilon = 1e-06
lanes = 128
f32, bf16 = jnp.float32, jnp.bfloat16
nt = (((1,), (1,)), ((), ()))


def params(mebibytes):
    return pltpu.CompilerParams(vmem_limit_bytes=int(mebibytes * 1024 * 1024))


def cost(flops, moved):
    return pl.CostEstimate(flops=flops, bytes_accessed=moved, transcendentals=0)


def exchange(array, axis, bit):
    count = lax.axis_size(axis)
    return lax.ppermute(array, axis, [(i, i ^ bit) for i in range(count)])


def after(array, *others):
    return lax.optimization_barrier((array,) + others)[0]


def gather_blocks(block):
    count = lax.axis_size("wide")
    held = {0: block, 1: exchange(block, "wide", 1)}
    bit = count // 2
    if count == 8:
        held[2], held[4] = exchange(block, "wide", 2), exchange(block, "wide", 4)
        held[6] = exchange(held[4], "wide", 2)
        held[5] = exchange(after(held[4], held[1], held[2]), "wide", 1)
        held[7] = exchange(held[6], "wide", 1)
        held[3] = exchange(after(held[1], held[6]), "wide", 2)
        return [held[k] for k in range(count)]
    while bit > 1:
        for k in [k for k in held if k % 2 == 0]:
            held[k | bit] = exchange(held[k], "wide", bit)
        bit //= 2
    for k in range(2, count, 2):
        held[k | 1] = exchange(held[k], "wide", 1)
    return [held[k] for k in range(count)]


def position():
    n = lax.axis_index("narrow")
    return n % 2, n // 2


def project_kernel(mine, x_hbm, g_hbm, w_hbm, up_hbm, rank_hbm, out_ref, x, g, w, up, rank, sems):
    core, _ = position()
    half = core if mine else 1 - core
    steps, sub = x.shape[:2]
    tokens = steps * sub
    out_width = rank.shape[0] // 2
    stack = tokens // lanes * out_width

    def copies(i):
        rows = pl.ds(pl.multiple_of((half * steps + i) * sub, sub), sub)
        return [
            pltpu.make_async_copy(x_hbm.at[rows, :], x.at[i], sems.at[2 * i]),
            pltpu.make_async_copy(g_hbm.at[rows, :], g.at[i], sems.at[2 * i + 1]),
        ]

    weights = [
        pltpu.make_async_copy(w_hbm, w, sems.at[2 * steps]),
        pltpu.make_async_copy(up_hbm, up, sems.at[2 * steps + 1]),
        pltpu.make_async_copy(rank_hbm, rank, sems.at[2 * steps + 2]),
    ]
    started = [copies(i) for i in range(steps)]
    for copy in weights + [copy for pair in started for copy in pair]:
        copy.start()
    for copy in weights:
        copy.wait()
    rank_twice = jnp.concatenate([rank[...], rank[...]], axis=1)
    for i in range(steps):
        for copy in started[i]:
            copy.wait()
        in_part = jnp.dot(x[i], w[...], preferred_element_type=f32)
        reduced = jnp.dot(g[i], up[...], preferred_element_type=f32)
        high = reduced.astype(bf16)
        low = (reduced - high.astype(f32)).astype(bf16)
        both = jnp.concatenate([high, low], axis=1)
        out_part = lax.dot_general(rank_twice, both, nt, preferred_element_type=f32)
        out_ref[i * sub : (i + 1) * sub, :] = in_part.astype(out_ref.dtype)
        for side in range(2):
            for piece in range(sub // lanes):
                row = tokens + side * stack + (i * (sub // lanes) + piece) * out_width
                out_ref[row : row + out_width, :] = out_part[
                    side * out_width : (side + 1) * out_width, piece * lanes : (piece + 1) * lanes
                ].astype(out_ref.dtype)


def project(mine, x, g, w, up, rank):
    tokens = x.shape[0] // 2
    sub = min(512, tokens)
    steps = tokens // sub
    depth = x.shape[1]
    rows = tokens + tokens // lanes * rank.shape[0]
    return pl.pallas_call(
        functools.partial(project_kernel, mine),
        in_specs=[pl.BlockSpec(memory_space=pltpu.HBM)] * 5,
        out_specs=pl.BlockSpec(memory_space=pltpu.VMEM),
        out_shape=jax.ShapeDtypeStruct((rows, lanes), f32 if mine else bf16),
        scratch_shapes=[
            pltpu.VMEM((steps, sub, depth), bf16),
            pltpu.VMEM((steps, sub, depth), bf16),
            pltpu.VMEM(w.shape, bf16),
            pltpu.VMEM(up.shape, bf16),
            pltpu.VMEM(rank.shape, bf16),
            pltpu.SemaphoreType.DMA((2 * steps + 3,)),
        ],
        compiler_params=params(16),
        cost_estimate=cost(4 * tokens * depth * lanes, 4 * tokens * depth),
        name="project",
    )(*(pltpu.with_memory_space_constraint(array, pltpu.HBM) for array in (x, g, w, up, rank)))


def square_kernel(targets_hbm, squares_ref, targets, sems):
    parts, rows, depth = targets.shape
    started = []
    for i in range(parts):
        part = pl.ds(i * rows, rows)
        started.append(pltpu.make_async_copy(targets_hbm.at[part, :], targets.at[i], sems.at[i]))
        started[-1].start()
    for i in range(parts):
        started[i].wait()
        totals = jnp.zeros((rows, lanes), f32)
        for k in range(depth // lanes):
            wide = targets[i, :, k * lanes : (k + 1) * lanes].astype(f32)
            totals += wide * wide
        squares_ref[:, i * rows : (i + 1) * rows] = jnp.sum(totals.T, axis=0, keepdims=True)


def row_squares(targets):
    columns, depth = targets.shape
    rows = min(256, columns)
    return pl.pallas_call(
        square_kernel,
        in_specs=[pl.BlockSpec(memory_space=pltpu.HBM)],
        out_specs=pl.BlockSpec(memory_space=pltpu.VMEM),
        out_shape=jax.ShapeDtypeStruct((1, columns), f32),
        scratch_shapes=[
            pltpu.VMEM((columns // rows, rows, depth), targets.dtype),
            pltpu.SemaphoreType.DMA((columns // rows,)),
        ],
        compiler_params=params(16),
        cost_estimate=cost(2 * columns * depth, 2 * columns * depth),
        name="squares",
    )(pltpu.with_memory_space_constraint(targets, pltpu.HBM))


def stage_kernel(targets_hbm, targets_ref, sem):
    copy = pltpu.make_async_copy(targets_hbm, targets_ref, sem)
    copy.start()
    copy.wait()


def stage(targets):
    return pl.pallas_call(
        stage_kernel,
        in_specs=[pl.BlockSpec(memory_space=pltpu.HBM)],
        out_specs=pl.BlockSpec(memory_space=pltpu.VMEM),
        out_shape=pltpu.VMEM(targets.shape, targets.dtype),
        scratch_shapes=[pltpu.SemaphoreType.DMA],
        compiler_params=params(12),
        cost_estimate=cost(0, 2 * targets.size),
        name="stage",
    )(pltpu.with_memory_space_constraint(targets, pltpu.HBM))


def core_sum_kernel(keep_ref, came_ref, send_ref, left_ref):
    rows = keep_ref.shape[0]
    final = send_ref.shape[0]
    stack = rows - final
    tokens = final - stack
    _, x = position()
    total = keep_ref[:tokens, :] + came_ref[:tokens, :].astype(f32)
    send_ref[:tokens, :] = total.astype(bf16)
    left_ref[:tokens, :] = total
    far = pl.ds(pl.multiple_of(tokens + (1 - x) * stack, stack), stack)
    near = pl.ds(pl.multiple_of(tokens + x * stack, stack), stack)
    send_ref[tokens:, :] = (keep_ref[far, :] + came_ref[far, :].astype(f32)).astype(bf16)
    left_ref[tokens:, :] = keep_ref[near, :] + came_ref[near, :].astype(f32)


def core_sum(keep, came, tokens):
    rows = keep.shape[0]
    final = tokens + (rows - tokens) // 2
    vmem = pl.BlockSpec(memory_space=pltpu.VMEM)
    return pl.pallas_call(
        core_sum_kernel,
        in_specs=[vmem, vmem],
        out_specs=[vmem, vmem],
        out_shape=[
            jax.ShapeDtypeStruct((final, lanes), bf16),
            jax.ShapeDtypeStruct((final, lanes), f32),
        ],
        compiler_params=params(8),
        cost_estimate=cost(rows * lanes, 12 * rows * lanes),
        name="core_sum",
    )(keep, came)


def feature_kernel(programs, lengths, left_ref, came_ref, mine_ref, other_ref, held):
    core, _ = position()
    quarter = mine_ref.shape[0]
    out_width = 2 * quarter
    final = left_ref.shape[0]
    tokens = final * lanes // (lanes + out_width)
    length = tokens // programs
    some = 8
    span = some * length
    program = lax.broadcasted_iota(jnp.int32, (some, span), 0)
    token = lax.broadcasted_iota(jnp.int32, (some, span), 1) - program * length
    for group in range(programs // some):
        rows = slice(group * span, (group + 1) * span)
        in_sum = (left_ref[rows, :] + came_ref[rows, :].astype(f32)).astype(bf16)
        first = tokens + group * (span // lanes) * out_width
        rows = slice(first, first + span // lanes * out_width)
        out_sum = left_ref[rows, :] + came_ref[rows, :].astype(f32)
        out_rows = jnp.concatenate(
            [out_sum[i * out_width : (i + 1) * out_width, :] for i in range(span // lanes)], axis=1
        )
        limit = jnp.zeros((some, span), jnp.int32)
        for s in range(some):
            limit = jnp.where(program == s, lengths[core * programs + group * some + s], limit)
        live = ((token >= 0) & (token < limit)).astype(f32)
        spread = (out_rows[:, None, :] * live[None, :, :]).reshape(out_width * some, span)
        made = jnp.dot(spread.astype(bf16), in_sum, preferred_element_type=f32)
        held[:, group * some : (group + 1) * some, :] = made.reshape(out_width, some, lanes)
    mine_ref[...] = held[pl.ds(core * quarter, quarter), :, :].astype(bf16)
    other_ref[...] = held[pl.ds((1 - core) * quarter, quarter), :, :].astype(bf16)


def make_features(programs, quarter, lengths, left, came):
    vmem = pl.BlockSpec(memory_space=pltpu.VMEM)
    shape = jax.ShapeDtypeStruct((quarter, programs, lanes), bf16)
    return pl.pallas_call(
        functools.partial(feature_kernel, programs),
        in_specs=[pl.BlockSpec(memory_space=pltpu.SMEM), vmem, vmem],
        out_specs=[vmem, vmem],
        out_shape=[shape, shape],
        scratch_shapes=[pltpu.VMEM((2 * quarter, programs, lanes), f32)],
        compiler_params=params(12),
        cost_estimate=cost(10**8, 8 * left.size),
        name="features",
    )(lengths, left, came)


def score_kernel(count, far, order_ref, targets_ref, *refs):
    pieces, sends, (keep_ref, ordered) = refs[:count], refs[count:-2], refs[-2:]
    columns, rows = targets_ref.shape[0], keep_ref.shape[0]

    def store(first, size, values):
        height = rows // len(sends)
        for i, ref in enumerate(sends):
            ref[:, first : first + size] = values[i * height : (i + 1) * height, :]
        keep_ref[:, first : first + size] = values[rows:, :]

    core, x = position()
    x = 1 - x if far else x
    position_rows = order_ref[...]
    row = lax.broadcasted_iota(jnp.int32, (2 * rows, position_rows.shape[1]), 0)
    first = jnp.where(row < rows, (x * 2 + 1 - core) * rows, (x * 2 + core) * rows - rows)
    chosen = (row + first == position_rows).astype(bf16)
    totals = jnp.zeros((2 * rows, lanes), f32)
    for a in range(0, pieces[0].shape[1], 2):
        block = jnp.concatenate(
            [
                jnp.concatenate([piece[i, a + d] for piece in pieces for i in range(2)], axis=0)
                for d in range(2)
            ],
            axis=1,
        )
        found = jnp.dot(chosen, block, preferred_element_type=f32)
        ordered[:, a * lanes : (a + 2) * lanes] = found.astype(bf16)
        totals += found[:, :lanes] * found[:, :lanes] + found[:, lanes:] * found[:, lanes:]
    store(columns, lanes, totals.astype(bf16))
    tile = min(512, columns)
    for j in range(0, columns, tile):
        scores = lax.dot_general(
            ordered[...], targets_ref[j : j + tile, :], nt, preferred_element_type=f32
        ).astype(bf16)
        store(j, tile, scores)


def partial_scores(far, order, pieces, targets, rows):
    columns, depth = targets.shape
    held = 2 * (4 * rows * depth + 4 * rows * columns + 8 * rows * order.size)
    limit = 6 + held // 1024**2
    vmem = pl.BlockSpec(memory_space=pltpu.VMEM)
    sends = 1 if far else 2
    shape = jax.ShapeDtypeStruct((rows // sends, columns + lanes), bf16)
    whole = jax.ShapeDtypeStruct((rows, columns + lanes), bf16)
    return pl.pallas_call(
        functools.partial(score_kernel, len(pieces), far),
        in_specs=[vmem] * (2 + len(pieces)),
        out_specs=[vmem] * (sends + 1),
        out_shape=[shape] * sends + [whole],
        scratch_shapes=[pltpu.VMEM((2 * rows, depth), bf16)],
        compiler_params=params(limit),
        cost_estimate=cost(4 * rows * columns * depth, 2 * columns * depth),
        name="scores_far" if far else "scores_near",
    )(order, pltpu.with_memory_space_constraint(targets, pltpu.VMEM), *pieces)


def join_kernel(keep_ref, came_ref, out_ref):
    out_ref[...] = (keep_ref[...].astype(f32) + came_ref[...].astype(f32)).astype(bf16)


def join(keep, came):
    vmem = pl.BlockSpec(memory_space=pltpu.VMEM)
    return pl.pallas_call(
        join_kernel,
        in_specs=[vmem, vmem],
        out_specs=vmem,
        out_shape=jax.ShapeDtypeStruct(keep.shape, bf16),
        compiler_params=params(16),
        cost_estimate=cost(keep.size, 6 * keep.size),
        name="join",
    )(keep, came)


def finish_kernel(root_count, keep_ref, low_ref, high_ref, far_ref, squares_ref, out_ref):
    columns = out_ref.shape[1]
    tile = min(512, columns)
    height = low_ref.shape[0]
    for i, near_ref in enumerate((low_ref, high_ref)):
        rows = slice(i * height, (i + 1) * height)

        def total(first, size):
            strip = slice(first, first + size)
            mine = keep_ref[rows, strip].astype(f32) + near_ref[:, strip].astype(f32)
            return mine + far_ref[rows, strip].astype(f32)

        squares = jnp.sum(total(columns, lanes), axis=1, keepdims=True)
        row_scale = lax.rsqrt(squares + epsilon) * root_count
        for j in range(0, columns, tile):
            column_scale = lax.rsqrt(squares_ref[:, j : j + tile] + epsilon)
            out_ref[rows, j : j + tile] = total(j, tile) * row_scale * column_scale


def finish(root_count, keep, low, high, far, squares):
    rows, columns = keep.shape[0], squares.shape[1]
    vmem = pl.BlockSpec(memory_space=pltpu.VMEM)
    return pl.pallas_call(
        functools.partial(finish_kernel, root_count),
        in_specs=[vmem] * 5,
        out_specs=vmem,
        out_shape=jax.ShapeDtypeStruct((rows, columns), f32),
        compiler_params=params(24),
        cost_estimate=cost(4 * rows * columns, 10 * rows * columns),
        name="finish",
    )(keep, low, high, far, squares)


def shards(
    layer_input_rows,
    output_gradient_rows,
    adapter_up_weight,
    input_side_projection,
    rank_side_projection,
    lengths,
    program_output_index,
    targets,
):
    wide_count, narrow_count = lax.axis_size("wide"), lax.axis_size("narrow")
    w, n = lax.axis_index("wide"), lax.axis_index("narrow")
    core, x = n % 2, n // 2
    programs = lengths.shape[0]
    length = layer_input_rows.shape[0] // programs
    quarter = rank_side_projection.shape[1] // narrow_count
    share = programs // 2
    tokens = share * length
    rank = rank_side_projection.T
    operands = (layer_input_rows, output_gradient_rows, input_side_projection, adapter_up_weight, rank)

    send = project(False, *operands)
    keep = project(True, *operands)
    send, left = core_sum(keep, exchange(send, "narrow", 1), tokens)
    squares = row_squares(after(targets, send))
    squares = squares + exchange(squares, "narrow", 1)
    squares = squares + exchange(squares, "narrow", 2)
    left, squares = lax.optimization_barrier((left, squares))
    came = exchange(send, "narrow", 2)
    mine, other = make_features(share, quarter, lengths, left, came)
    block = jnp.stack([mine, exchange(other, "narrow", 1)])
    pieces = gather_blocks(block)
    targets = stage(after(targets, pieces[-2]))

    order = program_output_index.reshape(wide_count, 2, share)
    order = jnp.take(order, w ^ jnp.arange(wide_count), axis=0)
    order = jnp.where(core == 1, order[:, ::-1], order).reshape(1, -1)
    rows = order.shape[1] // narrow_count

    far_send, far_keep = partial_scores(True, order, pieces, targets, rows)
    far = join(far_keep, exchange(far_send, "narrow", 1))
    order, far = lax.optimization_barrier((order, far))
    far = exchange(far, "narrow", 2)
    *near_sends, near_keep = partial_scores(False, order, pieces, targets, rows)
    near = [exchange(part, "narrow", 1) for part in near_sends]
    root_count = math.sqrt(float(targets.shape[1] * narrow_count))
    return finish(root_count, near_keep, *near, far, squares)


def solution(mesh):
    return jax.shard_map(
        shards,
        mesh=mesh,
        in_specs=(
            P("wide", "narrow"),
            P("wide", "narrow"),
            P("narrow", None),
            P("narrow", None),
            P(),
            P("wide"),
            P(),
            P("wide", "narrow"),
        ),
        out_specs=P("narrow", "wide"),
        check_vma=False,
    )
```

time: 167 us -> 73.6 us (0.44)
  waiting for transfers between devices: 108 us -> 33.1 us
  Pallas kernels: 0 us -> 22.4 us
  matrix products: 18.8 us -> 0 us
  starting transfers between devices: 0.27 us -> 16.8 us
  between operations: 13.2 us -> 0.19 us
  other arithmetic: 12.9 us -> 0.22 us
  local copies, waits for them, and re-layouts: 7.4 us -> 0.79 us
  blocking collectives: 6.04 us -> 0 us
    all_gather x1 -> x0, waiting for transfers between devices: 45.4 us -> none  [shards(): gathered = lax.all_gather(unit_rows, 'wide', axis=0, tiled=True)]
    ppermute x0 -> x16, waiting for transfers between devices: none -> 33.1 us  [exchange(): return lax.ppermute(array, axis, [(i, i ^ bit) for i in range(count)])]
    psum x1 -> x0, waiting for transfers between devices: 32.3 us -> none  [shards(): lax.psum(in_part.astype(jnp.bfloat16), 'narrow').astype(jnp.float32)]
    reduce_scatter x1 -> x0, waiting for transfers between devices: 30.1 us -> none  [shards(): lax.psum_scatter(lax.dot_general(permuted, target_unit, contract, preferr...]
    pallas_call x0 -> x10, Pallas kernels: none -> 22.4 us  [the longest x2 6.95 us: project(): pl.pallas_call(functools.partial(project_kernel, mine), in_specs=[pl.Bloc...]
    dot_general x5 -> x0, matrix products: 18.8 us -> none  [the longest x1 9.45 us: shards(): lax.dot_general(permuted, target_unit, contract, preferred_element_type=j...]
    ppermute x0 -> x16, starting transfers between devices: none -> 16.8 us  [exchange(): return lax.ppermute(array, axis, [(i, i ^ bit) for i in range(count)])]
    psum x1 -> x0, blocking collectives: 6.04 us -> none  [shards(): squares, target_squares = lax.psum((squares, target_squares), 'narrow')]
  transfers between devices with their start and end apart: 3 -> 16, of which waited for: 3 -> 11; matrix products, arithmetic and copies ran while one was open for 5% -> 1% of each run, Pallas kernels for 0% -> 18%
where the time goes in v3:
time: 73.6 us; the launch traced here: 73.5 us
  waiting for transfers between devices  33.1 us (45%)
  Pallas kernels  22.4 us (30%)
  starting transfers between devices  16.8 us (23%)
  local copies, waits for them, and re-layouts  0.79 us (1%)
    ppermute x16, waiting for transfers between devices, exchange(): return lax.ppermute(array, axis, [(i, i ^ bit) for i in range(count)])  33.1 us
    ppermute x16, starting transfers between devices, exchange(): return lax.ppermute(array, axis, [(i, i ^ bit) for i in range(count)])  16.8 us
    pallas_call x2, Pallas kernels, project(): pl.pallas_call(functools.partial(project_kernel, mine), in_specs=[pl.Bloc...  6.95 us
    pallas_call x2, Pallas kernels, partial_scores(): pl.pallas_call(functools.partial(score_kernel, len(pieces), far), in_spec...  5.82 us
    pallas_call x1, Pallas kernels, row_squares(): pl.pallas_call(square_kernel, in_specs=[pl.BlockSpec(memory_space=pltpu.H...  3.76 us
    pallas_call x1, Pallas kernels, stage(): pl.pallas_call(stage_kernel, in_specs=[pl.BlockSpec(memory_space=pltpu.HB...  3.4 us
  transfers between devices with their start and end apart: 16, of which 11 were waited for; matrix products, arithmetic and copies ran while one was open for 1% of the time, Pallas kernels for 18%

profile of v3, /device:TPU:0, one launch (start us, length us, event | category | flops | bytes accessed | tf_op | source)
XLA Modules:
  0.0 73.5 jit_solution(11319618556016101476)
XLA Ops:
  0.0 3.5 %project.3 = bf16[1536,128]{1,0:T(8,128)(2,1)S(1)} custom-call(bf16[2048,1024]{1,0:T(8,128)(2,1)} %x_hbm.3, bf16[2048,1024]{1,0:T(8,128)(2,1)} %g_hbm.3, bf16[1024,128]{1,0:T(8,128)(2,1)} %w_hbm.3, bf16[1024,128]{1,0:T(8,128)(2,1)} %up_hbm.3, bf16[64,128]{1,0:T(8,128)(2,1)} %bitcast.7), custom_call_target="tpu_custom_call" | custom-call | flops 536870912 | bytes 4194304 | tf_op jit(solution)/shard_map/project/pallas_call | solution.py:109
  3.5 0.0 copy-start
  3.5 0.0 copy-start.1
  3.5 0.5 collective-permute-start
  4.0 3.5 %project.2.keep_ref = f32[1536,128]{1,0:T(8,128)S(1)} custom-call(bf16[2048,1024]{1,0:T(8,128)(2,1)} %x_hbm.3, bf16[2048,1024]{1,0:T(8,128)(2,1)} %g_hbm.3, bf16[1024,128]{1,0:T(8,128)(2,1)} %w_hbm.3, bf16[1024,128]{1,0:T(8,128)(2,1)} %up_hbm.3, bf16[64,128]{1,0:T(8,128)(2,1)} %bitcast.8), custom_call_target="tpu_custom_call" | custom-call | flops 536870912 | bytes 4194304 | tf_op jit(solution)/shard_map/project/pallas_call | solution.py:109
  7.5 0.0 collective-permute-done.came_ref
  7.5 0.1 core_sum.1
  7.6 2.6 %collective-permute-start.3 = (bf16[1280,128]{1,0:T(8,128)(2,1)S(1)}, bf16[1280,128]{1,0:T(8,128)(2,1)S(1)}, u32[]{:S(2)}, u32[]{:S(2)}) collective-permute-start(bf16[1280,128]{1,0:T(8,128)(2,1)S(1)} %get-tuple-element.23), channel_id=1, source_target_pairs={{0,2},{1,3},{2,0},{3,1},{4,6},{5,7},{6,4},{7,5},{8,10},{9,11},{10,... | collective-permute-start | bytes 983048 | tf_op jit(solution)/shard_map/ppermute | solution.py:27
  10.2 3.8 %squares.1 = f32[1,2048]{1,0:T(1,128)S(1)} custom-call(bf16[2048,2048]{1,0:T(8,128)(2,1)} %targets_hbm.1), custom_call_target="tpu_custom_call" | custom-call | flops 8388608 | bytes 8388608 | tf_op jit(solution)/shard_map/squares/pallas_call | solution.py:147
  13.9 0.3 collective-permute-start.1
  14.2 1.0 %collective-permute-done.1 = f32[1,2048]{1,0:T(1,128)S(1)} collective-permute-done((f32[1,2048]{1,0:T(1,128)S(1)}, f32[1,2048]{1,0:T(1,128)S(1)}, u32[]{:S(2)}, u32[]{:S(2)}) %collective-permute-start.1) | collective-permute-done | bytes 8224 | tf_op jit(solution)/shard_map/ppermute | solution.py:27
  15.2 0.2 collective-permute-start.2
  15.4 3.5 %collective-permute-done.2 = f32[1,2048]{1,0:T(1,128)S(1)} collective-permute-done((f32[1,2048]{1,0:T(1,128)S(1)}, f32[1,2048]{1,0:T(1,128)S(1)}, u32[]{:S(2)}, u32[]{:S(2)}) %collective-permute-start.2) | collective-permute-done | bytes 8224 | tf_op jit(solution)/shard_map/ppermute | solution.py:27
  18.9 0.0 collective-permute-done.3.came_ref
  19.0 0.9 %features.1 = (bf16[16,32,128]{2,1,0:T(8,128)(2,1)S(1)}, bf16[16,32,128]{2,1,0:T(8,128)(2,1)S(1)}) custom-call(s32[64]{0:T(128)S(1)} %copy-done, f32[1280,128]{1,0:T(8,128)S(1)} %get-tuple-element.25.left_ref, bf16[1280,128]{1,0:T(8,128)(2,1)S(1)} %collective-permute-done.3.came_ref), custom_call_target="tpu_custom_call" | custom-call | flops 100000000 | bytes 1310720 | tf_op jit(solution)/shard_map/features/pallas_call | solution.py:248
  19.9 0.1 collective-permute-start.4
  20.0 1.3 %collective-permute-done.4 = bf16[16,32,128]{2,1,0:T(8,128)(2,1)S(1)} collective-permute-done((bf16[16,32,128]{2,1,0:T(8,128)(2,1)S(1)}, bf16[16,32,128]{2,1,0:T(8,128)(2,1)S(1)}, u32[]{:S(2)}, u32[]{:S(2)}) %collective-permute-start.4) | collective-permute-done | bytes 131104 | tf_op jit(solution)/shard_map/ppermute | solution.py:27
  21.3 2.7 %collective-permute-start.5 = (bf16[2,16,32,128]{3,2,1,0:T(8,128)(2,1)S(1)}, bf16[2,16,32,128]{3,2,1,0:T(8,128)(2,1)S(1)}, u32[]{:S(2)}, u32[]{:S(2)}) collective-permute-start(bf16[2,16,32,128]{3,2,1,0:T(8,128)(2,1)S(1)} %pad_maximum_fusion.refs_0_), channel_id=1, source_target_pairs={{0,16},{4,20},{8,24},{12,28},{16,0},{20,4},{24,8},{28,12},{1,17},{... | collective-permute-start | bytes 786440 | tf_op jit(solution)/shard_map/ppermute | solution.py:27
  24.0 1.6 %collective-permute-start.8 = (bf16[2,16,32,128]{3,2,1,0:T(8,128)(2,1)S(1)}, bf16[2,16,32,128]{3,2,1,0:T(8,128)(2,1)S(1)}, u32[]{:S(2)}, u32[]{:S(2)}) collective-permute-start(bf16[2,16,32,128]{3,2,1,0:T(8,128)(2,1)S(1)} %pad_maximum_fusion.refs_0_), channel_id=1, source_target_pairs={{0,8},{4,12},{8,0},{12,4},{16,24},{20,28},{24,16},{28,20},{1,9},{5... | collective-permute-start | bytes 786440 | tf_op jit(solution)/shard_map/ppermute | solution.py:27
  25.6 1.5 %collective-permute-start.7 = (bf16[2,16,32,128]{3,2,1,0:T(8,128)(2,1)S(1)}, bf16[2,16,32,128]{3,2,1,0:T(8,128)(2,1)S(1)}, u32[]{:S(2)}, u32[]{:S(2)}) collective-permute-start(bf16[2,16,32,128]{3,2,1,0:T(8,128)(2,1)S(1)} %pad_maximum_fusion.refs_0_), channel_id=1, source_target_pairs={{0,4},{4,0},{8,12},{12,8},{16,20},{20,16},{24,28},{28,24},{1,5},{5... | collective-permute-start | bytes 786440 | tf_op jit(solution)/shard_map/ppermute | solution.py:27
  27.1 9.3 %collective-permute-done.5.refs_4_ = bf16[2,16,32,128]{3,2,1,0:T(8,128)(2,1)S(1)} collective-permute-done((bf16[2,16,32,128]{3,2,1,0:T(8,128)(2,1)S(1)}, bf16[2,16,32,128]{3,2,1,0:T(8,128)(2,1)S(1)}, u32[]{:S(2)}, u32[]{:S(2)}) %collective-permute-start.5) | collective-permute-done | bytes 262176 | tf_op jit(solution)/shard_map/ppermute | solution.py:27
  36.4 0.6 collective-permute-start.6
  37.0 0.1 reshape.27
  37.1 0.6 gather_fusion
  37.7 0.0 collective-permute-done.8.refs_2_
  37.7 0.0 collective-permute-done.7.refs_1_
  37.7 1.6 %collective-permute-start.10 = (bf16[2,16,32,128]{3,2,1,0:T(8,128)(2,1)S(1)}, bf16[2,16,32,128]{3,2,1,0:T(8,128)(2,1)S(1)}, u32[]{:S(2)}, u32[]{:S(2)}) collective-permute-start(bf16[2,16,32,128]{3,2,1,0:T(8,128)(2,1)S(1)} %collective-permute-done.5.refs_4_), channel_id=1, source_target_pairs={{0,4},{4,0},{8,12},{12,8},{16,20},{20,16},{24,28},{28,24},{1,5},{5... | collective-permute-start | bytes 786440 | tf_op jit(solution)/shard_map/ppermute | solution.py:27
  39.3 4.5 %collective-permute-done.6.refs_6_ = bf16[2,16,32,128]{3,2,1,0:T(8,128)(2,1)S(1)} collective-permute-done((bf16[2,16,32,128]{3,2,1,0:T(8,128)(2,1)S(1)}, bf16[2,16,32,128]{3,2,1,0:T(8,128)(2,1)S(1)}, u32[]{:S(2)}, u32[]{:S(2)}) %collective-permute-start.6) | collective-permute-done | bytes 262176 | tf_op jit(solution)/shard_map/ppermute | solution.py:27
  43.8 1.4 %collective-permute-start.9 = (bf16[2,16,32,128]{3,2,1,0:T(8,128)(2,1)S(1)}, bf16[2,16,32,128]{3,2,1,0:T(8,128)(2,1)S(1)}, u32[]{:S(2)}, u32[]{:S(2)}) collective-permute-start(bf16[2,16,32,128]{3,2,1,0:T(8,128)(2,1)S(1)} %collective-permute-done.7.refs_1_), channel_id=1, source_target_pairs={{0,8},{4,12},{8,0},{12,4},{16,24},{20,28},{24,16},{28,20},{1,9},{5... | collective-permute-start | bytes 786440 | tf_op jit(solution)/shard_map/ppermute | solution.py:27
  45.2 1.5 %collective-permute-start.11 = (bf16[2,16,32,128]{3,2,1,0:T(8,128)(2,1)S(1)}, bf16[2,16,32,128]{3,2,1,0:T(8,128)(2,1)S(1)}, u32[]{:S(2)}, u32[]{:S(2)}) collective-permute-start(bf16[2,16,32,128]{3,2,1,0:T(8,128)(2,1)S(1)} %collective-permute-done.6.refs_6_), channel_id=1, source_target_pairs={{0,4},{4,0},{8,12},{12,8},{16,20},{20,16},{24,28},{28,24},{1,5},{5... | collective-permute-start | bytes 786440 | tf_op jit(solution)/shard_map/ppermute | solution.py:27
  46.8 0.1 broadcast_select_fusion
  46.9 0.1 broadcast_select_fusion.1
  46.9 0.1 reshape.28.order_ref
  47.0 3.4 %stage.1.targets_ref = bf16[2048,2048]{1,0:T(8,128)(2,1)S(1)} custom-call(bf16[2048,2048]{1,0:T(8,128)(2,1)} %targets_hbm.1), custom_call_target="tpu_custom_call" | custom-call | bytes 8388608 | tf_op jit(solution)/shard_map/stage/pallas_call | solution.py:169
  50.4 0.4 collective-permute-done.9.refs_3_
  50.9 1.5 %collective-permute-done.11.refs_7_ = bf16[2,16,32,128]{3,2,1,0:T(8,128)(2,1)S(1)} collective-permute-done((bf16[2,16,32,128]{3,2,1,0:T(8,128)(2,1)S(1)}, bf16[2,16,32,128]{3,2,1,0:T(8,128)(2,1)S(1)}, u32[]{:S(2)}, u32[]{:S(2)}) %collective-permute-start.11) | collective-permute-done | bytes 262176 | tf_op jit(solution)/shard_map/ppermute | solution.py:27
  52.3 2.9 %scores_far.1 = (bf16[128,2176]{1,0:T(8,128)(2,1)S(1)}, bf16[128,2176]{1,0:T(8,128)(2,1)S(1)}) custom-call(s32[1,512]{1,0:T(1,128)S(1)} %reshape.28.order_ref, bf16[2048,2048]{1,0:T(8,128)(2,1)S(1)} %stage.1.targets_ref, bf16[2,16,32,128]{3,2,1,0:T(8,128)(2,1)S(1)} %pad_maximum_fusion.refs_0_, bf16[2,16,32,128]{3,2,1,0:T(8,128)(2,1)S(1)} %collective-permute-done.7.refs_1_, ...), custom_call_target="tpu_custom_call" | custom-call | flops 2147483648 | bytes 8388608 | tf_op jit(solution)/shard_map/scores_far/pallas_call | solution.py:305
  55.3 0.1 collective-permute-start.12
  55.3 1.9 %collective-permute-done.12.came_ref = bf16[128,2176]{1,0:T(8,128)(2,1)S(1)} collective-permute-done((bf16[128,2176]{1,0:T(8,128)(2,1)S(1)}, bf16[128,2176]{1,0:T(8,128)(2,1)S(1)}, u32[]{:S(2)}, u32[]{:S(2)}) %collective-permute-start.12) | collective-permute-done | bytes 557088 | tf_op jit(solution)/shard_map/ppermute | solution.py:27
  57.3 0.1 join.1
  57.4 1.6 %collective-permute-start.15 = (bf16[128,2176]{1,0:T(8,128)(2,1)S(1)}, bf16[128,2176]{1,0:T(8,128)(2,1)S(1)}, u32[]{:S(2)}, u32[]{:S(2)}) collective-permute-start(bf16[128,2176]{1,0:T(8,128)(2,1)S(1)} %join.1), channel_id=1, source_target_pairs={{0,2},{1,3},{2,0},{3,1},{4,6},{5,7},{6,4},{7,5},{8,10},{9,11},{10,... | collective-permute-start | bytes 1671176 | tf_op jit(solution)/shard_map/ppermute | solution.py:27
  59.0 2.9 %scores_near.1 = (bf16[64,2176]{1,0:T(8,128)(2,1)S(1)}, bf16[64,2176]{1,0:T(8,128)(2,1)S(1)}, bf16[128,2176]{1,0:T(8,128)(2,1)S(1)}) custom-call(s32[1,512]{1,0:T(1,128)S(1)} %reshape.28.order_ref, bf16[2048,2048]{1,0:T(8,128)(2,1)S(1)} %stage.1.targets_ref, bf16[2,16,32,128]{3,2,1,0:T(8,128)(2,1)S(1)} %pad_maximum_fusion.refs_0_, ...), custom_call_target="tpu_custom_call" | custom-call | flops 2147483648 | bytes 8388608 | tf_op jit(solution)/shard_map/scores_near/pallas_call | solution.py:305
  61.9 0.1 collective-permute-start.13
  62.0 0.5 collective-permute-start.14
  62.5 1.0 %collective-permute-done.13.low_ref = bf16[64,2176]{1,0:T(8,128)(2,1)S(1)} collective-permute-done((bf16[64,2176]{1,0:T(8,128)(2,1)S(1)}, bf16[64,2176]{1,0:T(8,128)(2,1)S(1)}, u32[]{:S(2)}, u32[]{:S(2)}) %collective-permute-start.13) | collective-permute-done | bytes 278560 | tf_op jit(solution)/shard_map/ppermute | solution.py:27
  63.5 0.4 collective-permute-done.14.high_ref
  63.9 8.2 %collective-permute-done.15.far_ref = bf16[128,2176]{1,0:T(8,128)(2,1)S(1)} collective-permute-done((bf16[128,2176]{1,0:T(8,128)(2,1)S(1)}, bf16[128,2176]{1,0:T(8,128)(2,1)S(1)}, u32[]{:S(2)}, u32[]{:S(2)}) %collective-permute-start.15) | collective-permute-done | bytes 557088 | tf_op jit(solution)/shard_map/ppermute | solution.py:27
  72.1 1.3 %finish.1 = f32[128,2048]{1,0:T(8,128)} custom-call(bf16[128,2176]{1,0:T(8,128)(2,1)S(1)} %get-tuple-element.34.keep_ref, bf16[64,2176]{1,0:T(8,128)(2,1)S(1)} %collective-permute-done.13.low_ref, bf16[64,2176]{1,0:T(8,128)(2,1)S(1)} %collective-permute-done.14.high_ref, bf16[128,2176]{1,0:T(8,128)(2,1)S(1)} %collective-permute-done.15.far_ref, ...), custom_call_target="tpu_custom_call" | custom-call | flops 1048576 | bytes 2621440 | tf_op jit(solution)/shard_map/finish/pallas_call | solution.py:356
  (10 shorter events, 0.1 us)
Async XLA Ops:
  3.5 15.5 %copy-start = (s32[64]{0:T(128)S(1)}, s32[64]{0:T(128)}, u32[]{:S(2)}) copy-start(s32[64]{0:T(128)} %lengths.1) | copy-start | bytes 772
  3.5 33.5 %copy-start.1 = (s32[512]{0:T(512)S(1)}, s32[512]{0:T(512)}, u32[]{:S(2)}) copy-start(s32[512]{0:T(512)} %param.14) | copy-start | bytes 6148
  3.5 4.0 %collective-permute-start = (bf16[1536,128]{1,0:T(8,128)(2,1)S(1)}, bf16[1536,128]{1,0:T(8,128)(2,1)S(1)}, u32[]{:S(2)}, u32[]{:S(2)}) collective-permute-start(bf16[1536,128]{1,0:T(8,128)(2,1)S(1)} %project.3), channel_id=1, source_target_pairs={{0,1},{1,0},{2,3},{3,2},{4,5},{5,4},{6,7},{7,6},{8,9},{9,8},{10,11... | collective-permute-start | bytes 1179656 | tf_op jit(solution)/shard_map/ppermute | solution.py:27
  7.6 11.3 %collective-permute-start.3 = (bf16[1280,128]{1,0:T(8,128)(2,1)S(1)}, bf16[1280,128]{1,0:T(8,128)(2,1)S(1)}, u32[]{:S(2)}, u32[]{:S(2)}) collective-permute-start(bf16[1280,128]{1,0:T(8,128)(2,1)S(1)} %get-tuple-element.23), channel_id=1, source_target_pairs={{0,2},{1,3},{2,0},{3,1},{4,6},{5,7},{6,4},{7,5},{8,10},{9,11},{10,... | collective-permute-start | bytes 983048 | tf_op jit(solution)/shard_map/ppermute | solution.py:27
  13.9 1.2 %collective-permute-start.1 = (f32[1,2048]{1,0:T(1,128)S(1)}, f32[1,2048]{1,0:T(1,128)S(1)}, u32[]{:S(2)}, u32[]{:S(2)}) collective-permute-start(f32[1,2048]{1,0:T(1,128)S(1)} %squares.1), channel_id=1, source_target_pairs={{0,1},{1,0},{2,3},{3,2},{4,5},{5,4},{6,7},{7,6},{8,9},{9,8},{10,11... | collective-permute-start | bytes 24584 | tf_op jit(solution)/shard_map/ppermute | solution.py:27
  15.2 3.7 %collective-permute-start.2 = (f32[1,2048]{1,0:T(1,128)S(1)}, f32[1,2048]{1,0:T(1,128)S(1)}, u32[]{:S(2)}, u32[]{:S(2)}) collective-permute-start(f32[1,2048]{1,0:T(1,128)S(1)} %add.28), channel_id=1, source_target_pairs={{0,2},{1,3},{2,0},{3,1},{4,6},{5,7},{6,4},{7,5},{8,10},{9,11},{10,... | collective-permute-start | bytes 24584 | tf_op jit(solution)/shard_map/ppermute | solution.py:27
  19.9 1.4 %collective-permute-start.4 = (bf16[16,32,128]{2,1,0:T(8,128)(2,1)S(1)}, bf16[16,32,128]{2,1,0:T(8,128)(2,1)S(1)}, u32[]{:S(2)}, u32[]{:S(2)}) collective-permute-start(bf16[16,32,128]{2,1,0:T(8,128)(2,1)S(1)} %get-tuple-element.27), channel_id=1, source_target_pairs={{0,1},{1,0},{2,3},{3,2},{4,5},{5,4},{6,7},{7,6},{8,9},{9,8},{10,11... | collective-permute-start | bytes 393224 | tf_op jit(solution)/shard_map/ppermute | solution.py:27
  21.3 15.0 %collective-permute-start.5 = (bf16[2,16,32,128]{3,2,1,0:T(8,128)(2,1)S(1)}, bf16[2,16,32,128]{3,2,1,0:T(8,128)(2,1)S(1)}, u32[]{:S(2)}, u32[]{:S(2)}) collective-permute-start(bf16[2,16,32,128]{3,2,1,0:T(8,128)(2,1)S(1)} %pad_maximum_fusion.refs_0_), channel_id=1, source_target_pairs={{0,16},{4,20},{8,24},{12,28},{16,0},{20,4},{24,8},{28,12},{1,17},{... | collective-permute-start | bytes 786440 | tf_op jit(solution)/shard_map/ppermute | solution.py:27
  24.0 13.7 %collective-permute-start.8 = (bf16[2,16,32,128]{3,2,1,0:T(8,128)(2,1)S(1)}, bf16[2,16,32,128]{3,2,1,0:T(8,128)(2,1)S(1)}, u32[]{:S(2)}, u32[]{:S(2)}) collective-permute-start(bf16[2,16,32,128]{3,2,1,0:T(8,128)(2,1)S(1)} %pad_maximum_fusion.refs_0_), channel_id=1, source_target_pairs={{0,8},{4,12},{8,0},{12,4},{16,24},{20,28},{24,16},{28,20},{1,9},{5... | collective-permute-start | bytes 786440 | tf_op jit(solution)/shard_map/ppermute | solution.py:27
  25.6 12.1 %collective-permute-start.7 = (bf16[2,16,32,128]{3,2,1,0:T(8,128)(2,1)S(1)}, bf16[2,16,32,128]{3,2,1,0:T(8,128)(2,1)S(1)}, u32[]{:S(2)}, u32[]{:S(2)}) collective-permute-start(bf16[2,16,32,128]{3,2,1,0:T(8,128)(2,1)S(1)} %pad_maximum_fusion.refs_0_), channel_id=1, source_target_pairs={{0,4},{4,0},{8,12},{12,8},{16,20},{20,16},{24,28},{28,24},{1,5},{5... | collective-permute-start | bytes 786440 | tf_op jit(solution)/shard_map/ppermute | solution.py:27
  36.4 7.5 %collective-permute-start.6 = (bf16[2,16,32,128]{3,2,1,0:T(8,128)(2,1)S(1)}, bf16[2,16,32,128]{3,2,1,0:T(8,128)(2,1)S(1)}, u32[]{:S(2)}, u32[]{:S(2)}) collective-permute-start(bf16[2,16,32,128]{3,2,1,0:T(8,128)(2,1)S(1)} %collective-permute-done.5.refs_4_), channel_id=1, source_target_pairs={{0,8},{4,12},{8,0},{12,4},{16,24},{20,28},{24,16},{28,20},{1,9},{5... | collective-permute-start | bytes 786440 | tf_op jit(solution)/shard_map/ppermute | solution.py:27
  37.7 12.7 %collective-permute-start.10 = (bf16[2,16,32,128]{3,2,1,0:T(8,128)(2,1)S(1)}, bf16[2,16,32,128]{3,2,1,0:T(8,128)(2,1)S(1)}, u32[]{:S(2)}, u32[]{:S(2)}) collective-permute-start(bf16[2,16,32,128]{3,2,1,0:T(8,128)(2,1)S(1)} %collective-permute-done.5.refs_4_), channel_id=1, source_target_pairs={{0,4},{4,0},{8,12},{12,8},{16,20},{20,16},{24,28},{28,24},{1,5},{5... | collective-permute-start | bytes 786440 | tf_op jit(solution)/shard_map/ppermute | solution.py:27
  43.8 7.0 %collective-permute-start.9 = (bf16[2,16,32,128]{3,2,1,0:T(8,128)(2,1)S(1)}, bf16[2,16,32,128]{3,2,1,0:T(8,128)(2,1)S(1)}, u32[]{:S(2)}, u32[]{:S(2)}) collective-permute-start(bf16[2,16,32,128]{3,2,1,0:T(8,128)(2,1)S(1)} %collective-permute-done.7.refs_1_), channel_id=1, source_target_pairs={{0,8},{4,12},{8,0},{12,4},{16,24},{20,28},{24,16},{28,20},{1,9},{5... | collective-permute-start | bytes 786440 | tf_op jit(solution)/shard_map/ppermute | solution.py:27
  45.2 7.1 %collective-permute-start.11 = (bf16[2,16,32,128]{3,2,1,0:T(8,128)(2,1)S(1)}, bf16[2,16,32,128]{3,2,1,0:T(8,128)(2,1)S(1)}, u32[]{:S(2)}, u32[]{:S(2)}) collective-permute-start(bf16[2,16,32,128]{3,2,1,0:T(8,128)(2,1)S(1)} %collective-permute-done.6.refs_6_), channel_id=1, source_target_pairs={{0,4},{4,0},{8,12},{12,8},{16,20},{20,16},{24,28},{28,24},{1,5},{5... | collective-permute-start | bytes 786440 | tf_op jit(solution)/shard_map/ppermute | solution.py:27
  55.3 2.0 %collective-permute-start.12 = (bf16[128,2176]{1,0:T(8,128)(2,1)S(1)}, bf16[128,2176]{1,0:T(8,128)(2,1)S(1)}, u32[]{:S(2)}, u32[]{:S(2)}) collective-permute-start(bf16[128,2176]{1,0:T(8,128)(2,1)S(1)} %get-tuple-element.32), channel_id=1, source_target_pairs={{0,1},{1,0},{2,3},{3,2},{4,5},{5,4},{6,7},{7,6},{8,9},{9,8},{10,11... | collective-permute-start | bytes 1671176 | tf_op jit(solution)/shard_map/ppermute | solution.py:27
  57.4 14.7 %collective-permute-start.15 = (bf16[128,2176]{1,0:T(8,128)(2,1)S(1)}, bf16[128,2176]{1,0:T(8,128)(2,1)S(1)}, u32[]{:S(2)}, u32[]{:S(2)}) collective-permute-start(bf16[128,2176]{1,0:T(8,128)(2,1)S(1)} %join.1), channel_id=1, source_target_pairs={{0,2},{1,3},{2,0},{3,1},{4,6},{5,7},{6,4},{7,5},{8,10},{9,11},{10,... | collective-permute-start | bytes 1671176 | tf_op jit(solution)/shard_map/ppermute | solution.py:27
  61.9 1.6 %collective-permute-start.13 = (bf16[64,2176]{1,0:T(8,128)(2,1)S(1)}, bf16[64,2176]{1,0:T(8,128)(2,1)S(1)}, u32[]{:S(2)}, u32[]{:S(2)}) collective-permute-start(bf16[64,2176]{1,0:T(8,128)(2,1)S(1)} %get-tuple-element.35), channel_id=1, source_target_pairs={{0,1},{1,0},{2,3},{3,2},{4,5},{5,4},{6,7},{7,6},{8,9},{9,8},{10,11... | collective-permute-start | bytes 835592 | tf_op jit(solution)/shard_map/ppermute | solution.py:27
  62.0 1.9 %collective-permute-start.14 = (bf16[64,2176]{1,0:T(8,128)(2,1)S(1)}, bf16[64,2176]{1,0:T(8,128)(2,1)S(1)}, u32[]{:S(2)}, u32[]{:S(2)}) collective-permute-start(bf16[64,2176]{1,0:T(8,128)(2,1)S(1)} %get-tuple-element.36), channel_id=1, source_target_pairs={{0,1},{1,0},{2,3},{3,2},{4,5},{5,4},{6,7},{7,6},{8,9},{9,8},{10,11... | collective-permute-start | bytes 835592 | tf_op jit(solution)/shard_map/ppermute | solution.py:27

commit v4 on v3

--- a/solution.py
+++ b/solution.py
@@ -10,6 +10,7 @@
 
 epsilon = 1e-06
 lanes = 128
+chunks = 2
 f32, bf16 = jnp.float32, jnp.bfloat16
 nt = (((1,), (1,)), ((), ()))
 
@@ -31,24 +32,31 @@
     return lax.optimization_barrier((array,) + others)[0]
 
 
-def gather_blocks(block):
+def gather_blocks(blocks):
     count = lax.axis_size("wide")
-    held = {0: block, 1: exchange(block, "wide", 1)}
+    if count == 8 and chunks == 2:
+        first, second = blocks
+        far = [exchange(first, "wide", 4)]
+        above = [exchange(first, "wide", 2)]
+        beside = [exchange(first, "wide", 1)]
+        second = after(second, far[0])
+        far.append(exchange(second, "wide", 4))
+        across = [exchange(far[0], "wide", 2)]
+        far_beside = [exchange(after(far[0], beside[0], above[0]), "wide", 1)]
+        beside.append(exchange(second, "wide", 1))
+        above.append(exchange(second, "wide", 2))
+        across.append(exchange(far[1], "wide", 2))
+        far_beside.append(exchange(after(far[1], beside[1], above[1], far_beside[0]), "wide", 1))
+        across_beside = [exchange(chunk, "wide", 1) for chunk in across]
+        above_beside = [exchange(after(beside[i], across[i]), "wide", 2) for i in range(2)]
+        return blocks, beside, above, above_beside, far, far_beside, across, across_beside
+    held = {0: jnp.stack(blocks)}
     bit = count // 2
-    if count == 8:
-        held[2], held[4] = exchange(block, "wide", 2), exchange(block, "wide", 4)
-        held[6] = exchange(held[4], "wide", 2)
-        held[5] = exchange(after(held[4], held[1], held[2]), "wide", 1)
-        held[7] = exchange(held[6], "wide", 1)
-        held[3] = exchange(after(held[1], held[6]), "wide", 2)
-        return [held[k] for k in range(count)]
-    while bit > 1:
-        for k in [k for k in held if k % 2 == 0]:
+    while bit:
+        for k in list(held):
             held[k | bit] = exchange(held[k], "wide", bit)
         bit //= 2
-    for k in range(2, count, 2):
-        held[k | 1] = exchange(held[k], "wide", 1)
-    return [held[k] for k in range(count)]
+    return [[held[k]] for k in range(count)]
 
 
 def position():
@@ -178,40 +186,42 @@
     )(pltpu.with_memory_space_constraint(targets, pltpu.HBM))
 
 
-def core_sum_kernel(keep_ref, came_ref, send_ref, left_ref):
+def core_sum_kernel(keep_ref, came_ref, *outs):
+    sends, lefts = outs[:chunks], outs[chunks:]
     rows = keep_ref.shape[0]
-    final = send_ref.shape[0]
-    stack = rows - final
+    final = sends[0].shape[0]
+    stack = (rows - chunks * final) // chunks
     tokens = final - stack
     _, x = position()
-    total = keep_ref[:tokens, :] + came_ref[:tokens, :].astype(f32)
-    send_ref[:tokens, :] = total.astype(bf16)
-    left_ref[:tokens, :] = total
-    far = pl.ds(pl.multiple_of(tokens + (1 - x) * stack, stack), stack)
-    near = pl.ds(pl.multiple_of(tokens + x * stack, stack), stack)
-    send_ref[tokens:, :] = (keep_ref[far, :] + came_ref[far, :].astype(f32)).astype(bf16)
-    left_ref[tokens:, :] = keep_ref[near, :] + came_ref[near, :].astype(f32)
+    for i in range(chunks):
+        part = slice(i * tokens, (i + 1) * tokens)
+        total = keep_ref[part, :] + came_ref[part, :].astype(f32)
+        sends[i][:tokens, :] = total.astype(bf16)
+        lefts[i][:tokens, :] = total
+        for side, ref in ((1 - x, sends[i]), (x, lefts[i])):
+            first = chunks * tokens + (side * chunks + i) * stack
+            part = pl.ds(pl.multiple_of(first, stack), stack)
+            total = keep_ref[part, :] + came_ref[part, :].astype(f32)
+            ref[tokens:, :] = total.astype(ref.dtype)
 
 
 def core_sum(keep, came, tokens):
     rows = keep.shape[0]
-    final = tokens + (rows - tokens) // 2
+    final = (tokens + (rows - tokens) // 2) // chunks
     vmem = pl.BlockSpec(memory_space=pltpu.VMEM)
-    return pl.pallas_call(
+    outs = pl.pallas_call(
         core_sum_kernel,
         in_specs=[vmem, vmem],
-        out_specs=[vmem, vmem],
-        out_shape=[
-            jax.ShapeDtypeStruct((final, lanes), bf16),
-            jax.ShapeDtypeStruct((final, lanes), f32),
-        ],
+        out_specs=[vmem] * (2 * chunks),
+        out_shape=[jax.ShapeDtypeStruct((final, lanes), dtype) for dtype in (bf16,) * chunks + (f32,) * chunks],
         compiler_params=params(8),
         cost_estimate=cost(rows * lanes, 12 * rows * lanes),
         name="core_sum",
     )(keep, came)
-
-
-def feature_kernel(programs, lengths, left_ref, came_ref, mine_ref, other_ref, held):
+    return outs[:chunks], outs[chunks:]
+
+
+def feature_kernel(chunk, programs, lengths, left_ref, came_ref, mine_ref, other_ref, held):
     core, _ = position()
     quarter = mine_ref.shape[0]
     out_width = 2 * quarter
@@ -233,7 +243,7 @@
         )
         limit = jnp.zeros((some, span), jnp.int32)
         for s in range(some):
-            limit = jnp.where(program == s, lengths[core * programs + group * some + s], limit)
+            limit = jnp.where(program == s, lengths[(core * chunks + chunk) * programs + group * some + s], limit)
         live = ((token >= 0) & (token < limit)).astype(f32)
         spread = (out_rows[:, None, :] * live[None, :, :]).reshape(out_width * some, span)
         made = jnp.dot(spread.astype(bf16), in_sum, preferred_element_type=f32)
@@ -242,11 +252,11 @@
     other_ref[...] = held[pl.ds((1 - core) * quarter, quarter), :, :].astype(bf16)
 
 
-def make_features(programs, quarter, lengths, left, came):
+def make_features(chunk, programs, quarter, lengths, left, came):
     vmem = pl.BlockSpec(memory_space=pltpu.VMEM)
     shape = jax.ShapeDtypeStruct((quarter, programs, lanes), bf16)
     return pl.pallas_call(
-        functools.partial(feature_kernel, programs),
+        functools.partial(feature_kernel, chunk, programs),
         in_specs=[pl.BlockSpec(memory_space=pltpu.SMEM), vmem, vmem],
         out_specs=[vmem, vmem],
         out_shape=[shape, shape],
@@ -274,10 +284,13 @@
     first = jnp.where(row < rows, (x * 2 + 1 - core) * rows, (x * 2 + core) * rows - rows)
     chosen = (row + first == position_rows).astype(bf16)
     totals = jnp.zeros((2 * rows, lanes), f32)
-    for a in range(0, pieces[0].shape[1], 2):
+    halves = pieces
+    while any(ref.ndim > 3 for ref in halves):
+        halves = [half for ref in halves for half in ([ref.at[i] for i in range(ref.shape[0])] if ref.ndim > 3 else [ref])]
+    for a in range(0, halves[0].shape[0], 2):
         block = jnp.concatenate(
             [
-                jnp.concatenate([piece[i, a + d] for piece in pieces for i in range(2)], axis=0)
+                jnp.concatenate([half[a + d] for half in halves], axis=0)
                 for d in range(2)
             ],
             axis=1,
@@ -387,20 +400,23 @@
 
     send = project(False, *operands)
     keep = project(True, *operands)
-    send, left = core_sum(keep, exchange(send, "narrow", 1), tokens)
-    squares = row_squares(after(targets, send))
+    sends, lefts = core_sum(keep, exchange(send, "narrow", 1), tokens)
+    squares = row_squares(after(targets, sends[0]))
     squares = squares + exchange(squares, "narrow", 1)
     squares = squares + exchange(squares, "narrow", 2)
-    left, squares = lax.optimization_barrier((left, squares))
-    came = exchange(send, "narrow", 2)
-    mine, other = make_features(share, quarter, lengths, left, came)
-    block = jnp.stack([mine, exchange(other, "narrow", 1)])
-    pieces = gather_blocks(block)
-    targets = stage(after(targets, pieces[-2]))
-
-    order = program_output_index.reshape(wide_count, 2, share)
+    blocks = []
+    for i in range(chunks):
+        came = exchange(sends[i], "narrow", 2)
+        left = after(lefts[i], *blocks) if blocks else lefts[i]
+        mine, other = make_features(i, share // chunks, quarter, lengths, left, came)
+        blocks.append(jnp.stack([mine, exchange(other, "narrow", 1)]))
+    pieces = gather_blocks(blocks)
+    targets = stage(after(targets, pieces[-2][-1]))
+    pieces = [chunk for piece in pieces for chunk in piece]
+
+    order = program_output_index.reshape(wide_count, 2, chunks, share // chunks)
     order = jnp.take(order, w ^ jnp.arange(wide_count), axis=0)
-    order = jnp.where(core == 1, order[:, ::-1], order).reshape(1, -1)
+    order = jnp.where(core == 1, order[:, ::-1], order).transpose(0, 2, 1, 3).reshape(1, -1)
     rows = order.shape[1] // narrow_count
 
     far_send, far_keep = partial_scores(True, order, pieces, targets, rows)

time: 73.6 us -> 70.9 us (0.963)
  waiting for transfers between devices: 33.1 us -> 19.5 us
  starting transfers between devices: 16.8 us -> 27 us
    ppermute x16 -> x25, waiting for transfers between devices: 33.1 us -> 19.5 us  [exchange(): return lax.ppermute(array, axis, [(i, i ^ bit) for i in range(count)])]
    ppermute x16 -> x25, starting transfers between devices: 16.8 us -> 27 us  [exchange(): return lax.ppermute(array, axis, [(i, i ^ bit) for i in range(count)])]
    pallas_call x2 -> x3, Pallas kernels: 0.99 us -> 1.71 us  [the longest x2 1.63 us: make_features(): pl.pallas_call(functools.partial(feature_kernel, chunk, programs), in_spe...]
  transfers between devices with their start and end apart: 16 -> 25, of which waited for: 11 -> 11; matrix products, arithmetic and copies ran while one was open for 1% -> 1% of each run, Pallas kernels for 18% -> 20%
where the time goes in v4:
time: 70.9 us; the launch traced here: 70.7 us
  starting transfers between devices  27 us (38%)
  Pallas kernels  23.1 us (33%)
  waiting for transfers between devices  19.5 us (28%)
  local copies, waits for them, and re-layouts  0.78 us (1%)
    ppermute x25, starting transfers between devices, exchange(): return lax.ppermute(array, axis, [(i, i ^ bit) for i in range(count)])  27 us
    ppermute x25, waiting for transfers between devices, exchange(): return lax.ppermute(array, axis, [(i, i ^ bit) for i in range(count)])  19.5 us
    pallas_call x2, Pallas kernels, project(): pl.pallas_call(functools.partial(project_kernel, mine), in_specs=[pl.Bloc...  6.96 us
    pallas_call x2, Pallas kernels, partial_scores(): pl.pallas_call(functools.partial(score_kernel, len(pieces), far), in_spec...  5.82 us
    pallas_call x1, Pallas kernels, row_squares(): pl.pallas_call(square_kernel, in_specs=[pl.BlockSpec(memory_space=pltpu.H...  3.76 us
    pallas_call x1, Pallas kernels, stage(): pl.pallas_call(stage_kernel, in_specs=[pl.BlockSpec(memory_space=pltpu.HB...  3.39 us
    pallas_call x2, Pallas kernels, make_features(): pl.pallas_call(functools.partial(feature_kernel, chunk, programs), in_spe...  1.63 us
  transfers between devices with their start and end apart: 25, of which 11 were waited for; matrix products, arithmetic and copies ran while one was open for 1% of the time, Pallas kernels for 20%

profile of v4, /device:TPU:0, one launch (start us, length us, event | category | flops | bytes accessed | tf_op | source)
XLA Modules:
  0.0 70.7 jit_solution(1052463577182979356)
XLA Ops:
  0.0 3.5 %project.3 = bf16[1536,128]{1,0:T(8,128)(2,1)S(1)} custom-call(bf16[2048,1024]{1,0:T(8,128)(2,1)} %x_hbm.3, bf16[2048,1024]{1,0:T(8,128)(2,1)} %g_hbm.3, bf16[1024,128]{1,0:T(8,128)(2,1)} %w_hbm.3, bf16[1024,128]{1,0:T(8,128)(2,1)} %up_hbm.3, bf16[64,128]{1,0:T(8,128)(2,1)} %bitcast.11), custom_call_target="tpu_custom_call" | custom-call | flops 536870912 | bytes 4194304 | tf_op jit(solution)/shard_map/project/pallas_call | solution.py:117
  3.5 0.5 collective-permute-start
  4.0 3.5 %project.2.keep_ref = f32[1536,128]{1,0:T(8,128)S(1)} custom-call(bf16[2048,1024]{1,0:T(8,128)(2,1)} %x_hbm.3, bf16[2048,1024]{1,0:T(8,128)(2,1)} %g_hbm.3, bf16[1024,128]{1,0:T(8,128)(2,1)} %w_hbm.3, bf16[1024,128]{1,0:T(8,128)(2,1)} %up_hbm.3, bf16[64,128]{1,0:T(8,128)(2,1)} %bitcast.12), custom_call_target="tpu_custom_call" | custom-call | flops 536870912 | bytes 4194304 | tf_op jit(solution)/shard_map/project/pallas_call | solution.py:117
  7.5 0.1 core_sum.1
  7.6 2.6 %collective-permute-start.1 = (bf16[640,128]{1,0:T(8,128)(2,1)S(1)}, bf16[640,128]{1,0:T(8,128)(2,1)S(1)}, u32[]{:S(2)}, u32[]{:S(2)}) collective-permute-start(bf16[640,128]{1,0:T(8,128)(2,1)S(1)} %get-tuple-element.30), channel_id=1, source_target_pairs={{0,2},{1,3},{2,0},{3,1},{4,6},{5,7},{6,4},{7,5},{8,10},{9,11},{10,... | collective-permute-start | bytes 491528 | tf_op jit(solution)/shard_map/ppermute | solution.py:28
  10.2 4.9 %collective-permute-done.1.came_ref = bf16[640,128]{1,0:T(8,128)(2,1)S(1)} collective-permute-done((bf16[640,128]{1,0:T(8,128)(2,1)S(1)}, bf16[640,128]{1,0:T(8,128)(2,1)S(1)}, u32[]{:S(2)}, u32[]{:S(2)}) %collective-permute-start.1) | collective-permute-done | bytes 163872 | tf_op jit(solution)/shard_map/ppermute | solution.py:28
  15.0 0.8 %features.2 = (bf16[16,16,128]{2,1,0:T(8,128)(2,1)S(1)}, bf16[16,16,128]{2,1,0:T(8,128)(2,1)S(1)}) custom-call(s32[64]{0:T(128)S(1)} %copy-done, f32[640,128]{1,0:T(8,128)S(1)} %get-tuple-element.29.left_ref, bf16[640,128]{1,0:T(8,128)(2,1)S(1)} %collective-permute-done.1.came_ref), custom_call_target="tpu_custom_call" | custom-call | flops 100000000 | bytes 655360 | tf_op jit(solution)/shard_map/features/pallas_call | solution.py:258
  15.9 1.8 %collective-permute-start.3 = (bf16[640,128]{1,0:T(8,128)(2,1)S(1)}, bf16[640,128]{1,0:T(8,128)(2,1)S(1)}, u32[]{:S(2)}, u32[]{:S(2)}) collective-permute-start(bf16[640,128]{1,0:T(8,128)(2,1)S(1)} %get-tuple-element.34), channel_id=1, source_target_pairs={{0,2},{1,3},{2,0},{3,1},{4,6},{5,7},{6,4},{7,5},{8,10},{9,11},{10,... | collective-permute-start | bytes 491528 | tf_op jit(solution)/shard_map/ppermute | solution.py:28
  17.8 2.7 %collective-permute-start.5 = (bf16[2,16,16,128]{3,2,1,0:T(8,128)(2,1)S(1)}, bf16[2,16,16,128]{3,2,1,0:T(8,128)(2,1)S(1)}, u32[]{:S(2)}, u32[]{:S(2)}) collective-permute-start(bf16[2,16,16,128]{3,2,1,0:T(8,128)(2,1)S(1)} %pad_maximum_fusion.refs_0_), channel_id=1, source_target_pairs={{0,16},{4,20},{8,24},{12,28},{16,0},{20,4},{24,8},{28,12},{1,17},{... | collective-permute-start | bytes 393224 | tf_op jit(solution)/shard_map/ppermute | solution.py:28
  20.4 2.1 %collective-permute-done.3.came_ref = bf16[640,128]{1,0:T(8,128)(2,1)S(1)} collective-permute-done((bf16[640,128]{1,0:T(8,128)(2,1)S(1)}, bf16[640,128]{1,0:T(8,128)(2,1)S(1)}, u32[]{:S(2)}, u32[]{:S(2)}) %collective-permute-start.3) | collective-permute-done | bytes 163872 | tf_op jit(solution)/shard_map/ppermute | solution.py:28
  22.6 0.8 %features.3 = (bf16[16,16,128]{2,1,0:T(8,128)(2,1)S(1)}, bf16[16,16,128]{2,1,0:T(8,128)(2,1)S(1)}) custom-call(s32[64]{0:T(128)S(1)} %copy-done, f32[640,128]{1,0:T(8,128)S(1)} %get-tuple-element.33.left_ref, bf16[640,128]{1,0:T(8,128)(2,1)S(1)} %collective-permute-done.3.came_ref), custom_call_target="tpu_custom_call" | custom-call | flops 100000000 | bytes 655360 | tf_op jit(solution)/shard_map/features/pallas_call | solution.py:258
  23.4 0.1 collective-permute-start.4
  23.5 1.9 %collective-permute-start.10 = (bf16[2,16,16,128]{3,2,1,0:T(8,128)(2,1)S(1)}, bf16[2,16,16,128]{3,2,1,0:T(8,128)(2,1)S(1)}, u32[]{:S(2)}, u32[]{:S(2)}) collective-permute-start(bf16[2,16,16,128]{3,2,1,0:T(8,128)(2,1)S(1)} %pad_maximum_fusion.refs_0_), channel_id=1, source_target_pairs={{0,8},{4,12},{8,0},{12,4},{16,24},{20,28},{24,16},{28,20},{1,9},{5... | collective-permute-start | bytes 393224 | tf_op jit(solution)/shard_map/ppermute | solution.py:28
  25.4 1.5 %collective-permute-start.8 = (bf16[2,16,16,128]{3,2,1,0:T(8,128)(2,1)S(1)}, bf16[2,16,16,128]{3,2,1,0:T(8,128)(2,1)S(1)}, u32[]{:S(2)}, u32[]{:S(2)}) collective-permute-start(bf16[2,16,16,128]{3,2,1,0:T(8,128)(2,1)S(1)} %pad_maximum_fusion.refs_0_), channel_id=1, source_target_pairs={{0,4},{4,0},{8,12},{12,8},{16,20},{20,16},{24,28},{28,24},{1,5},{5... | collective-permute-start | bytes 393224 | tf_op jit(solution)/shard_map/ppermute | solution.py:28
  26.9 0.3 collective-permute-done.5.refs_8_
  27.2 2.4 %collective-permute-start.6 = (bf16[2,16,16,128]{3,2,1,0:T(8,128)(2,1)S(1)}, bf16[2,16,16,128]{3,2,1,0:T(8,128)(2,1)S(1)}, u32[]{:S(2)}, u32[]{:S(2)}) collective-permute-start(bf16[2,16,16,128]{3,2,1,0:T(8,128)(2,1)S(1)} %pad_maximum_fusion.1.refs_1_), channel_id=1, source_target_pairs={{0,16},{4,20},{8,24},{12,28},{16,0},{20,4},{24,8},{28,12},{1,17},{... | collective-permute-start | bytes 393224 | tf_op jit(solution)/shard_map/ppermute | solution.py:28
  29.6 0.1 reshape.27
  29.7 0.6 gather_fusion
  30.3 1.7 %collective-permute-start.11 = (bf16[2,16,16,128]{3,2,1,0:T(8,128)(2,1)S(1)}, bf16[2,16,16,128]{3,2,1,0:T(8,128)(2,1)S(1)}, u32[]{:S(2)}, u32[]{:S(2)}) collective-permute-start(bf16[2,16,16,128]{3,2,1,0:T(8,128)(2,1)S(1)} %pad_maximum_fusion.1.refs_1_), channel_id=1, source_target_pairs={{0,8},{4,12},{8,0},{12,4},{16,24},{20,28},{24,16},{28,20},{1,9},{5... | collective-permute-start | bytes 393224 | tf_op jit(solution)/shard_map/ppermute | solution.py:28
  31.9 1.5 %collective-permute-start.9 = (bf16[2,16,16,128]{3,2,1,0:T(8,128)(2,1)S(1)}, bf16[2,16,16,128]{3,2,1,0:T(8,128)(2,1)S(1)}, u32[]{:S(2)}, u32[]{:S(2)}) collective-permute-start(bf16[2,16,16,128]{3,2,1,0:T(8,128)(2,1)S(1)} %pad_maximum_fusion.1.refs_1_), channel_id=1, source_target_pairs={{0,4},{4,0},{8,12},{12,8},{16,20},{20,16},{24,28},{28,24},{1,5},{5... | collective-permute-start | bytes 393224 | tf_op jit(solution)/shard_map/ppermute | solution.py:28
  33.5 0.5 collective-permute-start.15
  34.0 0.4 collective-permute-start.12
  34.4 1.7 %collective-permute-done.6.refs_9_ = bf16[2,16,16,128]{3,2,1,0:T(8,128)(2,1)S(1)} collective-permute-done((bf16[2,16,16,128]{3,2,1,0:T(8,128)(2,1)S(1)}, bf16[2,16,16,128]{3,2,1,0:T(8,128)(2,1)S(1)}, u32[]{:S(2)}, u32[]{:S(2)}) %collective-permute-start.6) | collective-permute-done | bytes 131104 | tf_op jit(solution)/shard_map/ppermute | solution.py:28
  36.1 0.6 collective-permute-start.7
  36.7 0.1 broadcast_select_fusion
  36.8 0.6 collective-permute-done.11.refs_5_
  37.4 0.8 %collective-permute-done.9.refs_3_ = bf16[2,16,16,128]{3,2,1,0:T(8,128)(2,1)S(1)} collective-permute-done((bf16[2,16,16,128]{3,2,1,0:T(8,128)(2,1)S(1)}, bf16[2,16,16,128]{3,2,1,0:T(8,128)(2,1)S(1)}, u32[]{:S(2)}, u32[]{:S(2)}) %collective-permute-start.9) | collective-permute-done | bytes 131104 | tf_op jit(solution)/shard_map/ppermute | solution.py:28
  38.2 1.4 %collective-permute-done.15.refs_10_ = bf16[2,16,16,128]{3,2,1,0:T(8,128)(2,1)S(1)} collective-permute-done((bf16[2,16,16,128]{3,2,1,0:T(8,128)(2,1)S(1)}, bf16[2,16,16,128]{3,2,1,0:T(8,128)(2,1)S(1)}, u32[]{:S(2)}, u32[]{:S(2)}) %collective-permute-start.15) | collective-permute-done | bytes 131104 | tf_op jit(solution)/shard_map/ppermute | solution.py:28
  39.6 1.5 %collective-permute-start.16 = (bf16[2,16,16,128]{3,2,1,0:T(8,128)(2,1)S(1)}, bf16[2,16,16,128]{3,2,1,0:T(8,128)(2,1)S(1)}, u32[]{:S(2)}, u32[]{:S(2)}) collective-permute-start(bf16[2,16,16,128]{3,2,1,0:T(8,128)(2,1)S(1)} %collective-permute-done.6.refs_9_), channel_id=1, source_target_pairs={{0,4},{4,0},{8,12},{12,8},{16,20},{20,16},{24,28},{28,24},{1,5},{5... | collective-permute-start | bytes 393224 | tf_op jit(solution)/shard_map/ppermute | solution.py:28
  41.1 0.4 collective-permute-start.13
  41.5 1.2 %collective-permute-start.17 = (bf16[2,16,16,128]{3,2,1,0:T(8,128)(2,1)S(1)}, bf16[2,16,16,128]{3,2,1,0:T(8,128)(2,1)S(1)}, u32[]{:S(2)}, u32[]{:S(2)}) collective-permute-start(bf16[2,16,16,128]{3,2,1,0:T(8,128)(2,1)S(1)} %collective-permute-done.12.refs_12_), channel_id=1, source_target_pairs={{0,4},{4,0},{8,12},{12,8},{16,20},{20,16},{24,28},{28,24},{1,5},{5... | collective-permute-start | bytes 393224 | tf_op jit(solution)/shard_map/ppermute | solution.py:28
  42.7 1.3 %collective-permute-start.14 = (bf16[2,16,16,128]{3,2,1,0:T(8,128)(2,1)S(1)}, bf16[2,16,16,128]{3,2,1,0:T(8,128)(2,1)S(1)}, u32[]{:S(2)}, u32[]{:S(2)}) collective-permute-start(bf16[2,16,16,128]{3,2,1,0:T(8,128)(2,1)S(1)} %collective-permute-done.9.refs_3_), channel_id=1, source_target_pairs={{0,8},{4,12},{8,0},{12,4},{16,24},{20,28},{24,16},{28,20},{1,9},{5... | collective-permute-start | bytes 393224 | tf_op jit(solution)/shard_map/ppermute | solution.py:28
  44.0 1.5 %collective-permute-start.18 = (bf16[2,16,16,128]{3,2,1,0:T(8,128)(2,1)S(1)}, bf16[2,16,16,128]{3,2,1,0:T(8,128)(2,1)S(1)}, u32[]{:S(2)}, u32[]{:S(2)}) collective-permute-start(bf16[2,16,16,128]{3,2,1,0:T(8,128)(2,1)S(1)} %collective-permute-done.7.refs_13_), channel_id=1, source_target_pairs={{0,4},{4,0},{8,12},{12,8},{16,20},{20,16},{24,28},{28,24},{1,5},{5... | collective-permute-start | bytes 393224 | tf_op jit(solution)/shard_map/ppermute | solution.py:28
  45.5 0.1 reshape.28.order_ref
  45.6 3.4 %stage.1.targets_ref = bf16[2048,2048]{1,0:T(8,128)(2,1)S(1)} custom-call(bf16[2048,2048]{1,0:T(8,128)(2,1)} %targets_hbm.1), custom_call_target="tpu_custom_call" | custom-call | bytes 8388608 | tf_op jit(solution)/shard_map/stage/pallas_call | solution.py:177
  49.0 0.4 collective-permute-done.18.refs_15_
  49.4 2.9 %scores_far.1 = (bf16[128,2176]{1,0:T(8,128)(2,1)S(1)}, bf16[128,2176]{1,0:T(8,128)(2,1)S(1)}) custom-call(s32[1,512]{1,0:T(1,128)S(1)} %reshape.28.order_ref, bf16[2048,2048]{1,0:T(8,128)(2,1)S(1)} %stage.1.targets_ref, bf16[2,16,16,128]{3,2,1,0:T(8,128)(2,1)S(1)} %pad_maximum_fusion.refs_0_, bf16[2,16,16,128]{3,2,1,0:T(8,128)(2,1)S(1)} %pad_maximum_fusion.1.refs_1_, ...), custom_call_target="tpu_custom_call" | custom-call | flops 2147483648 | bytes 8388608 | tf_op jit(solution)/shard_map/scores_far/pallas_call | solution.py:318
  52.4 1.9 %collective-permute-done.19.came_ref = bf16[128,2176]{1,0:T(8,128)(2,1)S(1)} collective-permute-done((bf16[128,2176]{1,0:T(8,128)(2,1)S(1)}, bf16[128,2176]{1,0:T(8,128)(2,1)S(1)}, u32[]{:S(2)}, u32[]{:S(2)}) %collective-permute-start.19) | collective-permute-done | bytes 557088 | tf_op jit(solution)/shard_map/ppermute | solution.py:28
  54.3 0.1 join.1
  54.5 1.3 %collective-permute-start.22 = (bf16[128,2176]{1,0:T(8,128)(2,1)S(1)}, bf16[128,2176]{1,0:T(8,128)(2,1)S(1)}, u32[]{:S(2)}, u32[]{:S(2)}) collective-permute-start(bf16[128,2176]{1,0:T(8,128)(2,1)S(1)} %join.1), channel_id=1, source_target_pairs={{0,2},{1,3},{2,0},{3,1},{4,6},{5,7},{6,4},{7,5},{8,10},{9,11},{10,... | collective-permute-start | bytes 1671176 | tf_op jit(solution)/shard_map/ppermute | solution.py:28
  55.8 2.9 %scores_near.1 = (bf16[64,2176]{1,0:T(8,128)(2,1)S(1)}, bf16[64,2176]{1,0:T(8,128)(2,1)S(1)}, bf16[128,2176]{1,0:T(8,128)(2,1)S(1)}) custom-call(s32[1,512]{1,0:T(1,128)S(1)} %reshape.28.order_ref, bf16[2048,2048]{1,0:T(8,128)(2,1)S(1)} %stage.1.targets_ref, bf16[2,16,16,128]{3,2,1,0:T(8,128)(2,1)S(1)} %pad_maximum_fusion.refs_0_, ...), custom_call_target="tpu_custom_call" | custom-call | flops 2147483648 | bytes 8388608 | tf_op jit(solution)/shard_map/scores_near/pallas_call | solution.py:318
  58.8 0.5 collective-permute-start.21
  59.3 3.8 %squares.1 = f32[1,2048]{1,0:T(1,128)S(1)} custom-call(bf16[2048,2048]{1,0:T(8,128)(2,1)} %targets_hbm.1), custom_call_target="tpu_custom_call" | custom-call | flops 8388608 | bytes 8388608 | tf_op jit(solution)/shard_map/squares/pallas_call | solution.py:155
  63.1 0.1 collective-permute-start.23
  63.2 1.1 %collective-permute-done.23 = f32[1,2048]{1,0:T(1,128)S(1)} collective-permute-done((f32[1,2048]{1,0:T(1,128)S(1)}, f32[1,2048]{1,0:T(1,128)S(1)}, u32[]{:S(2)}, u32[]{:S(2)}) %collective-permute-start.23) | collective-permute-done | bytes 8224 | tf_op jit(solution)/shard_map/ppermute | solution.py:28
  64.3 0.8 %collective-permute-start.24 = (f32[1,2048]{1,0:T(1,128)S(1)}, f32[1,2048]{1,0:T(1,128)S(1)}, u32[]{:S(2)}, u32[]{:S(2)}) collective-permute-start(f32[1,2048]{1,0:T(1,128)S(1)} %add.28), channel_id=1, source_target_pairs={{0,2},{1,3},{2,0},{3,1},{4,6},{5,7},{6,4},{7,5},{8,10},{9,11},{10,... | collective-permute-start | bytes 24584 | tf_op jit(solution)/shard_map/ppermute | solution.py:28
  65.2 4.2 %collective-permute-done.24 = f32[1,2048]{1,0:T(1,128)S(1)} collective-permute-done((f32[1,2048]{1,0:T(1,128)S(1)}, f32[1,2048]{1,0:T(1,128)S(1)}, u32[]{:S(2)}, u32[]{:S(2)}) %collective-permute-start.24) | collective-permute-done | bytes 8224 | tf_op jit(solution)/shard_map/ppermute | solution.py:28
  69.4 1.3 %finish.1 = f32[128,2048]{1,0:T(8,128)} custom-call(bf16[128,2176]{1,0:T(8,128)(2,1)S(1)} %get-tuple-element.46.keep_ref, bf16[64,2176]{1,0:T(8,128)(2,1)S(1)} %collective-permute-done.20.low_ref, bf16[64,2176]{1,0:T(8,128)(2,1)S(1)} %collective-permute-done.21.high_ref, bf16[128,2176]{1,0:T(8,128)(2,1)S(1)} %collective-permute-done.22.far_ref, ...), custom_call_target="tpu_custom_call" | custom-call | flops 1048576 | bytes 2621440 | tf_op jit(solution)/shard_map/finish/pallas_call | solution.py:369
  (30 shorter events, 0.4 us)
Async XLA Ops:
  0.0 15.0 %copy-start = (s32[64]{0:T(128)S(1)}, s32[64]{0:T(128)}, u32[]{:S(2)}) copy-start(s32[64]{0:T(128)} %lengths.3) | copy-start | bytes 772
  3.5 26.1 %copy-start.1 = (s32[512]{0:T(512)S(1)}, s32[512]{0:T(512)}, u32[]{:S(2)}) copy-start(s32[512]{0:T(512)} %param.14) | copy-start | bytes 6148
  3.5 4.0 %collective-permute-start = (bf16[1536,128]{1,0:T(8,128)(2,1)S(1)}, bf16[1536,128]{1,0:T(8,128)(2,1)S(1)}, u32[]{:S(2)}, u32[]{:S(2)}) collective-permute-start(bf16[1536,128]{1,0:T(8,128)(2,1)S(1)} %project.3), channel_id=1, source_target_pairs={{0,1},{1,0},{2,3},{3,2},{4,5},{5,4},{6,7},{7,6},{8,9},{9,8},{10,11... | collective-permute-start | bytes 1179656 | tf_op jit(solution)/shard_map/ppermute | solution.py:28
  7.6 7.4 %collective-permute-start.1 = (bf16[640,128]{1,0:T(8,128)(2,1)S(1)}, bf16[640,128]{1,0:T(8,128)(2,1)S(1)}, u32[]{:S(2)}, u32[]{:S(2)}) collective-permute-start(bf16[640,128]{1,0:T(8,128)(2,1)S(1)} %get-tuple-element.30), channel_id=1, source_target_pairs={{0,2},{1,3},{2,0},{3,1},{4,6},{5,7},{6,4},{7,5},{8,10},{9,11},{10,... | collective-permute-start | bytes 491528 | tf_op jit(solution)/shard_map/ppermute | solution.py:28
  15.9 1.9 %collective-permute-start.2 = (bf16[16,16,128]{2,1,0:T(8,128)(2,1)S(1)}, bf16[16,16,128]{2,1,0:T(8,128)(2,1)S(1)}, u32[]{:S(2)}, u32[]{:S(2)}) collective-permute-start(bf16[16,16,128]{2,1,0:T(8,128)(2,1)S(1)} %get-tuple-element.32), channel_id=1, source_target_pairs={{0,1},{1,0},{2,3},{3,2},{4,5},{5,4},{6,7},{7,6},{8,9},{9,8},{10,11... | collective-permute-start | bytes 196616 | tf_op jit(solution)/shard_map/ppermute | solution.py:28
  15.9 6.6 %collective-permute-start.3 = (bf16[640,128]{1,0:T(8,128)(2,1)S(1)}, bf16[640,128]{1,0:T(8,128)(2,1)S(1)}, u32[]{:S(2)}, u32[]{:S(2)}) collective-permute-start(bf16[640,128]{1,0:T(8,128)(2,1)S(1)} %get-tuple-element.34), channel_id=1, source_target_pairs={{0,2},{1,3},{2,0},{3,1},{4,6},{5,7},{6,4},{7,5},{8,10},{9,11},{10,... | collective-permute-start | bytes 491528 | tf_op jit(solution)/shard_map/ppermute | solution.py:28
  17.8 9.4 %collective-permute-start.5 = (bf16[2,16,16,128]{3,2,1,0:T(8,128)(2,1)S(1)}, bf16[2,16,16,128]{3,2,1,0:T(8,128)(2,1)S(1)}, u32[]{:S(2)}, u32[]{:S(2)}) collective-permute-start(bf16[2,16,16,128]{3,2,1,0:T(8,128)(2,1)S(1)} %pad_maximum_fusion.refs_0_), channel_id=1, source_target_pairs={{0,16},{4,20},{8,24},{12,28},{16,0},{20,4},{24,8},{28,12},{1,17},{... | collective-permute-start | bytes 393224 | tf_op jit(solution)/shard_map/ppermute | solution.py:28
  23.4 3.5 %collective-permute-start.4 = (bf16[16,16,128]{2,1,0:T(8,128)(2,1)S(1)}, bf16[16,16,128]{2,1,0:T(8,128)(2,1)S(1)}, u32[]{:S(2)}, u32[]{:S(2)}) collective-permute-start(bf16[16,16,128]{2,1,0:T(8,128)(2,1)S(1)} %get-tuple-element.36), channel_id=1, source_target_pairs={{0,1},{1,0},{2,3},{3,2},{4,5},{5,4},{6,7},{7,6},{8,9},{9,8},{10,11... | collective-permute-start | bytes 196616 | tf_op jit(solution)/shard_map/ppermute | solution.py:28
  23.5 10.0 %collective-permute-start.10 = (bf16[2,16,16,128]{3,2,1,0:T(8,128)(2,1)S(1)}, bf16[2,16,16,128]{3,2,1,0:T(8,128)(2,1)S(1)}, u32[]{:S(2)}, u32[]{:S(2)}) collective-permute-start(bf16[2,16,16,128]{3,2,1,0:T(8,128)(2,1)S(1)} %pad_maximum_fusion.refs_0_), channel_id=1, source_target_pairs={{0,8},{4,12},{8,0},{12,4},{16,24},{20,28},{24,16},{28,20},{1,9},{5... | collective-permute-start | bytes 393224 | tf_op jit(solution)/shard_map/ppermute | solution.py:28
  25.4 8.1 %collective-permute-start.8 = (bf16[2,16,16,128]{3,2,1,0:T(8,128)(2,1)S(1)}, bf16[2,16,16,128]{3,2,1,0:T(8,128)(2,1)S(1)}, u32[]{:S(2)}, u32[]{:S(2)}) collective-permute-start(bf16[2,16,16,128]{3,2,1,0:T(8,128)(2,1)S(1)} %pad_maximum_fusion.refs_0_), channel_id=1, source_target_pairs={{0,4},{4,0},{8,12},{12,8},{16,20},{20,16},{24,28},{28,24},{1,5},{5... | collective-permute-start | bytes 393224 | tf_op jit(solution)/shard_map/ppermute | solution.py:28
  27.2 8.9 %collective-permute-start.6 = (bf16[2,16,16,128]{3,2,1,0:T(8,128)(2,1)S(1)}, bf16[2,16,16,128]{3,2,1,0:T(8,128)(2,1)S(1)}, u32[]{:S(2)}, u32[]{:S(2)}) collective-permute-start(bf16[2,16,16,128]{3,2,1,0:T(8,128)(2,1)S(1)} %pad_maximum_fusion.1.refs_1_), channel_id=1, source_target_pairs={{0,16},{4,20},{8,24},{12,28},{16,0},{20,4},{24,8},{28,12},{1,17},{... | collective-permute-start | bytes 393224 | tf_op jit(solution)/shard_map/ppermute | solution.py:28
  30.3 7.1 %collective-permute-start.11 = (bf16[2,16,16,128]{3,2,1,0:T(8,128)(2,1)S(1)}, bf16[2,16,16,128]{3,2,1,0:T(8,128)(2,1)S(1)}, u32[]{:S(2)}, u32[]{:S(2)}) collective-permute-start(bf16[2,16,16,128]{3,2,1,0:T(8,128)(2,1)S(1)} %pad_maximum_fusion.1.refs_1_), channel_id=1, source_target_pairs={{0,8},{4,12},{8,0},{12,4},{16,24},{20,28},{24,16},{28,20},{1,9},{5... | collective-permute-start | bytes 393224 | tf_op jit(solution)/shard_map/ppermute | solution.py:28
  31.9 6.3 %collective-permute-start.9 = (bf16[2,16,16,128]{3,2,1,0:T(8,128)(2,1)S(1)}, bf16[2,16,16,128]{3,2,1,0:T(8,128)(2,1)S(1)}, u32[]{:S(2)}, u32[]{:S(2)}) collective-permute-start(bf16[2,16,16,128]{3,2,1,0:T(8,128)(2,1)S(1)} %pad_maximum_fusion.1.refs_1_), channel_id=1, source_target_pairs={{0,4},{4,0},{8,12},{12,8},{16,20},{20,16},{24,28},{28,24},{1,5},{5... | collective-permute-start | bytes 393224 | tf_op jit(solution)/shard_map/ppermute | solution.py:28
  33.5 6.1 %collective-permute-start.15 = (bf16[2,16,16,128]{3,2,1,0:T(8,128)(2,1)S(1)}, bf16[2,16,16,128]{3,2,1,0:T(8,128)(2,1)S(1)}, u32[]{:S(2)}, u32[]{:S(2)}) collective-permute-start(bf16[2,16,16,128]{3,2,1,0:T(8,128)(2,1)S(1)} %collective-permute-done.5.refs_8_), channel_id=1, source_target_pairs={{0,4},{4,0},{8,12},{12,8},{16,20},{20,16},{24,28},{28,24},{1,5},{5... | collective-permute-start | bytes 393224 | tf_op jit(solution)/shard_map/ppermute | solution.py:28
  34.0 7.2 %collective-permute-start.12 = (bf16[2,16,16,128]{3,2,1,0:T(8,128)(2,1)S(1)}, bf16[2,16,16,128]{3,2,1,0:T(8,128)(2,1)S(1)}, u32[]{:S(2)}, u32[]{:S(2)}) collective-permute-start(bf16[2,16,16,128]{3,2,1,0:T(8,128)(2,1)S(1)} %collective-permute-done.5.refs_8_), channel_id=1, source_target_pairs={{0,8},{4,12},{8,0},{12,4},{16,24},{20,28},{24,16},{28,20},{1,9},{5... | collective-permute-start | bytes 393224 | tf_op jit(solution)/shard_map/ppermute | solution.py:28
  36.1 6.6 %collective-permute-start.7 = (bf16[2,16,16,128]{3,2,1,0:T(8,128)(2,1)S(1)}, bf16[2,16,16,128]{3,2,1,0:T(8,128)(2,1)S(1)}, u32[]{:S(2)}, u32[]{:S(2)}) collective-permute-start(bf16[2,16,16,128]{3,2,1,0:T(8,128)(2,1)S(1)} %collective-permute-done.6.refs_9_), channel_id=1, source_target_pairs={{0,8},{4,12},{8,0},{12,4},{16,24},{20,28},{24,16},{28,20},{1,9},{5... | collective-permute-start | bytes 393224 | tf_op jit(solution)/shard_map/ppermute | solution.py:28
  39.6 9.4 %collective-permute-start.16 = (bf16[2,16,16,128]{3,2,1,0:T(8,128)(2,1)S(1)}, bf16[2,16,16,128]{3,2,1,0:T(8,128)(2,1)S(1)}, u32[]{:S(2)}, u32[]{:S(2)}) collective-permute-start(bf16[2,16,16,128]{3,2,1,0:T(8,128)(2,1)S(1)} %collective-permute-done.6.refs_9_), channel_id=1, source_target_pairs={{0,4},{4,0},{8,12},{12,8},{16,20},{20,16},{24,28},{28,24},{1,5},{5... | collective-permute-start | bytes 393224 | tf_op jit(solution)/shard_map/ppermute | solution.py:28
  41.1 7.9 %collective-permute-start.13 = (bf16[2,16,16,128]{3,2,1,0:T(8,128)(2,1)S(1)}, bf16[2,16,16,128]{3,2,1,0:T(8,128)(2,1)S(1)}, u32[]{:S(2)}, u32[]{:S(2)}) collective-permute-start(bf16[2,16,16,128]{3,2,1,0:T(8,128)(2,1)S(1)} %collective-permute-done.8.refs_2_), channel_id=1, source_target_pairs={{0,8},{4,12},{8,0},{12,4},{16,24},{20,28},{24,16},{28,20},{1,9},{5... | collective-permute-start | bytes 393224 | tf_op jit(solution)/shard_map/ppermute | solution.py:28
  41.5 7.5 %collective-permute-start.17 = (bf16[2,16,16,128]{3,2,1,0:T(8,128)(2,1)S(1)}, bf16[2,16,16,128]{3,2,1,0:T(8,128)(2,1)S(1)}, u32[]{:S(2)}, u32[]{:S(2)}) collective-permute-start(bf16[2,16,16,128]{3,2,1,0:T(8,128)(2,1)S(1)} %collective-permute-done.12.refs_12_), channel_id=1, source_target_pairs={{0,4},{4,0},{8,12},{12,8},{16,20},{20,16},{24,28},{28,24},{1,5},{5... | collective-permute-start | bytes 393224 | tf_op jit(solution)/shard_map/ppermute | solution.py:28
  42.7 6.3 %collective-permute-start.14 = (bf16[2,16,16,128]{3,2,1,0:T(8,128)(2,1)S(1)}, bf16[2,16,16,128]{3,2,1,0:T(8,128)(2,1)S(1)}, u32[]{:S(2)}, u32[]{:S(2)}) collective-permute-start(bf16[2,16,16,128]{3,2,1,0:T(8,128)(2,1)S(1)} %collective-permute-done.9.refs_3_), channel_id=1, source_target_pairs={{0,8},{4,12},{8,0},{12,4},{16,24},{20,28},{24,16},{28,20},{1,9},{5... | collective-permute-start | bytes 393224 | tf_op jit(solution)/shard_map/ppermute | solution.py:28
  44.0 5.5 %collective-permute-start.18 = (bf16[2,16,16,128]{3,2,1,0:T(8,128)(2,1)S(1)}, bf16[2,16,16,128]{3,2,1,0:T(8,128)(2,1)S(1)}, u32[]{:S(2)}, u32[]{:S(2)}) collective-permute-start(bf16[2,16,16,128]{3,2,1,0:T(8,128)(2,1)S(1)} %collective-permute-done.7.refs_13_), channel_id=1, source_target_pairs={{0,4},{4,0},{8,12},{12,8},{16,20},{20,16},{24,28},{28,24},{1,5},{5... | collective-permute-start | bytes 393224 | tf_op jit(solution)/shard_map/ppermute | solution.py:28
  52.3 2.0 %collective-permute-start.19 = (bf16[128,2176]{1,0:T(8,128)(2,1)S(1)}, bf16[128,2176]{1,0:T(8,128)(2,1)S(1)}, u32[]{:S(2)}, u32[]{:S(2)}) collective-permute-start(bf16[128,2176]{1,0:T(8,128)(2,1)S(1)} %get-tuple-element.44), channel_id=1, source_target_pairs={{0,1},{1,0},{2,3},{3,2},{4,5},{5,4},{6,7},{7,6},{8,9},{9,8},{10,11... | collective-permute-start | bytes 1671176 | tf_op jit(solution)/shard_map/ppermute | solution.py:28
  54.5 14.9 %collective-permute-start.22 = (bf16[128,2176]{1,0:T(8,128)(2,1)S(1)}, bf16[128,2176]{1,0:T(8,128)(2,1)S(1)}, u32[]{:S(2)}, u32[]{:S(2)}) collective-permute-start(bf16[128,2176]{1,0:T(8,128)(2,1)S(1)} %join.1), channel_id=1, source_target_pairs={{0,2},{1,3},{2,0},{3,1},{4,6},{5,7},{6,4},{7,5},{8,10},{9,11},{10,... | collective-permute-start | bytes 1671176 | tf_op jit(solution)/shard_map/ppermute | solution.py:28
  58.7 10.7 %collective-permute-start.20 = (bf16[64,2176]{1,0:T(8,128)(2,1)S(1)}, bf16[64,2176]{1,0:T(8,128)(2,1)S(1)}, u32[]{:S(2)}, u32[]{:S(2)}) collective-permute-start(bf16[64,2176]{1,0:T(8,128)(2,1)S(1)} %get-tuple-element.47), channel_id=1, source_target_pairs={{0,1},{1,0},{2,3},{3,2},{4,5},{5,4},{6,7},{7,6},{8,9},{9,8},{10,11... | collective-permute-start | bytes 835592 | tf_op jit(solution)/shard_map/ppermute | solution.py:28
  58.8 10.6 %collective-permute-start.21 = (bf16[64,2176]{1,0:T(8,128)(2,1)S(1)}, bf16[64,2176]{1,0:T(8,128)(2,1)S(1)}, u32[]{:S(2)}, u32[]{:S(2)}) collective-permute-start(bf16[64,2176]{1,0:T(8,128)(2,1)S(1)} %get-tuple-element.48), channel_id=1, source_target_pairs={{0,1},{1,0},{2,3},{3,2},{4,5},{5,4},{6,7},{7,6},{8,9},{9,8},{10,11... | collective-permute-start | bytes 835592 | tf_op jit(solution)/shard_map/ppermute | solution.py:28
  63.1 1.2 %collective-permute-start.23 = (f32[1,2048]{1,0:T(1,128)S(1)}, f32[1,2048]{1,0:T(1,128)S(1)}, u32[]{:S(2)}, u32[]{:S(2)}) collective-permute-start(f32[1,2048]{1,0:T(1,128)S(1)} %squares.1), channel_id=1, source_target_pairs={{0,1},{1,0},{2,3},{3,2},{4,5},{5,4},{6,7},{7,6},{8,9},{9,8},{10,11... | collective-permute-start | bytes 24584 | tf_op jit(solution)/shard_map/ppermute | solution.py:28
  64.3 5.1 %collective-permute-start.24 = (f32[1,2048]{1,0:T(1,128)S(1)}, f32[1,2048]{1,0:T(1,128)S(1)}, u32[]{:S(2)}, u32[]{:S(2)}) collective-permute-start(f32[1,2048]{1,0:T(1,128)S(1)} %add.28), channel_id=1, source_target_pairs={{0,2},{1,3},{2,0},{3,1},{4,6},{5,7},{6,4},{7,5},{8,10},{9,11},{10,... | collective-permute-start | bytes 24584 | tf_op jit(solution)/shard_map/ppermute | solution.py:28

commit v5 on v4

--- a/solution.py
+++ b/solution.py
@@ -11,6 +11,7 @@
 epsilon = 1e-06
 lanes = 128
 chunks = 2
+middle = lanes // 2
 f32, bf16 = jnp.float32, jnp.bfloat16
 nt = (((1,), (1,)), ((), ()))
 
@@ -46,9 +47,9 @@
         beside.append(exchange(second, "wide", 1))
         above.append(exchange(second, "wide", 2))
         across.append(exchange(far[1], "wide", 2))
-        far_beside.append(exchange(after(far[1], beside[1], above[1], far_beside[0]), "wide", 1))
+        far_beside.append(exchange(after(far[1], beside[1], above[1]), "wide", 1))
         across_beside = [exchange(chunk, "wide", 1) for chunk in across]
-        above_beside = [exchange(after(beside[i], across[i]), "wide", 2) for i in range(2)]
+        above_beside = [exchange(after(beside[0], across[0]), "wide", 2), exchange(after(beside[1], across[1]), "wide", 2)]
         return blocks, beside, above, above_beside, far, far_beside, across, across_beside
     held = {0: jnp.stack(blocks)}
     bit = count // 2
@@ -64,73 +65,111 @@
     return n % 2, n // 2
 
 
-def project_kernel(mine, x_hbm, g_hbm, w_hbm, up_hbm, rank_hbm, out_ref, x, g, w, up, rank, sems):
+def project_rows(x, g, w, up, rank_twice, out_ref, i, tokens):
+    sub = x.shape[0]
+    out_width = rank_twice.shape[0] // 2
+    stack = tokens // lanes * out_width
+    in_part = jnp.dot(x, w, preferred_element_type=f32)
+    reduced = jnp.dot(g, up, preferred_element_type=f32)
+    high = reduced.astype(bf16)
+    low = (reduced - high.astype(f32)).astype(bf16)
+    both = jnp.concatenate([high, low], axis=1)
+    out_part = lax.dot_general(rank_twice, both, nt, preferred_element_type=f32)
+    out_ref[i * sub : (i + 1) * sub, :] = in_part.astype(out_ref.dtype)
+    for side in range(2):
+        for piece in range(sub // lanes):
+            row = tokens + side * stack + (i * (sub // lanes) + piece) * out_width
+            out_ref[row : row + out_width, :] = out_part[
+                side * out_width : (side + 1) * out_width, piece * lanes : (piece + 1) * lanes
+            ].astype(out_ref.dtype)
+
+
+def project_send_kernel(
+    x_hbm, g_hbm, w_hbm, up_hbm, rank_hbm, out_ref, x_mine, g_mine, w, up, x, g, rank, sems
+):
     core, _ = position()
-    half = core if mine else 1 - core
     steps, sub = x.shape[:2]
     tokens = steps * sub
-    out_width = rank.shape[0] // 2
-    stack = tokens // lanes * out_width
-
-    def copies(i):
-        rows = pl.ds(pl.multiple_of((half * steps + i) * sub, sub), sub)
-        return [
-            pltpu.make_async_copy(x_hbm.at[rows, :], x.at[i], sems.at[2 * i]),
-            pltpu.make_async_copy(g_hbm.at[rows, :], g.at[i], sems.at[2 * i + 1]),
-        ]
-
-    weights = [
-        pltpu.make_async_copy(w_hbm, w, sems.at[2 * steps]),
-        pltpu.make_async_copy(up_hbm, up, sems.at[2 * steps + 1]),
-        pltpu.make_async_copy(rank_hbm, rank, sems.at[2 * steps + 2]),
+
+    def rows(half, i):
+        return pl.ds(pl.multiple_of((half * steps + i) * sub, sub), sub)
+
+    started = [
+        pltpu.make_async_copy(w_hbm, w, sems.at[0]),
+        pltpu.make_async_copy(up_hbm, up, sems.at[1]),
+        pltpu.make_async_copy(rank_hbm, rank, sems.at[2]),
     ]
-    started = [copies(i) for i in range(steps)]
-    for copy in weights + [copy for pair in started for copy in pair]:
+    for i in range(steps):
+        part = rows(1 - core, i)
+        started.append(pltpu.make_async_copy(x_hbm.at[part, :], x.at[i], sems.at[len(started)]))
+        started.append(pltpu.make_async_copy(g_hbm.at[part, :], g.at[i], sems.at[len(started)]))
+    part = pl.ds(pl.multiple_of(core * tokens, tokens), tokens)
+    started.append(pltpu.make_async_copy(x_hbm.at[part, :], x_mine, sems.at[len(started)]))
+    started.append(pltpu.make_async_copy(g_hbm.at[part, :], g_mine, sems.at[len(started)]))
+    for copy in started:
         copy.start()
-    for copy in weights:
+    for copy in started[:3]:
         copy.wait()
     rank_twice = jnp.concatenate([rank[...], rank[...]], axis=1)
     for i in range(steps):
-        for copy in started[i]:
-            copy.wait()
-        in_part = jnp.dot(x[i], w[...], preferred_element_type=f32)
-        reduced = jnp.dot(g[i], up[...], preferred_element_type=f32)
-        high = reduced.astype(bf16)
-        low = (reduced - high.astype(f32)).astype(bf16)
-        both = jnp.concatenate([high, low], axis=1)
-        out_part = lax.dot_general(rank_twice, both, nt, preferred_element_type=f32)
-        out_ref[i * sub : (i + 1) * sub, :] = in_part.astype(out_ref.dtype)
-        for side in range(2):
-            for piece in range(sub // lanes):
-                row = tokens + side * stack + (i * (sub // lanes) + piece) * out_width
-                out_ref[row : row + out_width, :] = out_part[
-                    side * out_width : (side + 1) * out_width, piece * lanes : (piece + 1) * lanes
-                ].astype(out_ref.dtype)
-
-
-def project(mine, x, g, w, up, rank):
-    tokens = x.shape[0] // 2
+        started[3 + 2 * i].wait()
+        started[4 + 2 * i].wait()
+        project_rows(x[i], g[i], w[...], up[...], rank_twice, out_ref, i, tokens)
+    started[-2].wait()
+    started[-1].wait()
+
+
+def project_keep_kernel(x, g, w, up, rank, out_ref):
+    rank_twice = jnp.concatenate([rank[...], rank[...]], axis=1)
+    tokens = x.shape[0]
+    sub = min(512, tokens)
+    for i in range(tokens // sub):
+        part = slice(i * sub, (i + 1) * sub)
+        project_rows(x[part, :], g[part, :], w[...], up[...], rank_twice, out_ref, i, tokens)
+
+
+def project_send(x, g, w, up, rank):
+    tokens, depth = x.shape[0] // 2, x.shape[1]
     sub = min(512, tokens)
     steps = tokens // sub
-    depth = x.shape[1]
     rows = tokens + tokens // lanes * rank.shape[0]
-    return pl.pallas_call(
-        functools.partial(project_kernel, mine),
+    vmem = pl.BlockSpec(memory_space=pltpu.VMEM)
+    return pl.pallas_call(
+        project_send_kernel,
         in_specs=[pl.BlockSpec(memory_space=pltpu.HBM)] * 5,
-        out_specs=pl.BlockSpec(memory_space=pltpu.VMEM),
-        out_shape=jax.ShapeDtypeStruct((rows, lanes), f32 if mine else bf16),
+        out_specs=[vmem] * 5,
+        out_shape=[
+            jax.ShapeDtypeStruct((rows, lanes), bf16),
+            pltpu.VMEM((tokens, depth), bf16),
+            pltpu.VMEM((tokens, depth), bf16),
+            pltpu.VMEM(w.shape, bf16),
+            pltpu.VMEM(up.shape, bf16),
+        ],
         scratch_shapes=[
             pltpu.VMEM((steps, sub, depth), bf16),
             pltpu.VMEM((steps, sub, depth), bf16),
-            pltpu.VMEM(w.shape, bf16),
-            pltpu.VMEM(up.shape, bf16),
             pltpu.VMEM(rank.shape, bf16),
-            pltpu.SemaphoreType.DMA((2 * steps + 3,)),
+            pltpu.SemaphoreType.DMA((2 * steps + 5,)),
         ],
+        compiler_params=params(24),
+        cost_estimate=cost(4 * tokens * depth * lanes, 8 * tokens * depth),
+        name="project_send",
+    )(*(pltpu.with_memory_space_constraint(array, pltpu.HBM) for array in (x, g, w, up, rank)))
+
+
+def project_keep(x, g, w, up, rank):
+    tokens, depth = x.shape
+    rows = tokens + tokens // lanes * rank.shape[0]
+    vmem = pl.BlockSpec(memory_space=pltpu.VMEM)
+    return pl.pallas_call(
+        project_keep_kernel,
+        in_specs=[vmem] * 5,
+        out_specs=vmem,
+        out_shape=jax.ShapeDtypeStruct((rows, lanes), f32),
         compiler_params=params(16),
         cost_estimate=cost(4 * tokens * depth * lanes, 4 * tokens * depth),
-        name="project",
-    )(*(pltpu.with_memory_space_constraint(array, pltpu.HBM) for array in (x, g, w, up, rank)))
+        name="project_keep",
+    )(*(pltpu.with_memory_space_constraint(array, pltpu.VMEM) for array in (x, g, w, up)), rank)
 
 
 def square_kernel(targets_hbm, squares_ref, targets, sems):
@@ -140,23 +179,28 @@
         part = pl.ds(i * rows, rows)
         started.append(pltpu.make_async_copy(targets_hbm.at[part, :], targets.at[i], sems.at[i]))
         started[-1].start()
+    lane = lax.broadcasted_iota(jnp.int32, (lanes, lanes), 1)
+    squares = jnp.zeros((lanes, lanes), f32)
     for i in range(parts):
         started[i].wait()
-        totals = jnp.zeros((rows, lanes), f32)
-        for k in range(depth // lanes):
-            wide = targets[i, :, k * lanes : (k + 1) * lanes].astype(f32)
-            totals += wide * wide
-        squares_ref[:, i * rows : (i + 1) * rows] = jnp.sum(totals.T, axis=0, keepdims=True)
-
-
-def row_squares(targets):
+        for first in range(0, rows, lanes):
+            totals = jnp.zeros((lanes, lanes), f32)
+            for k in range(depth // lanes):
+                wide = targets[i, first : first + lanes, k * lanes : (k + 1) * lanes].astype(f32)
+                totals += wide * wide
+            total = jnp.sum(totals, axis=1, keepdims=True)
+            squares = jnp.where(lane == (i * rows + first) // lanes, total, squares)
+    squares_ref[...] = squares
+
+
+def column_squares(targets):
     columns, depth = targets.shape
     rows = min(256, columns)
     return pl.pallas_call(
         square_kernel,
         in_specs=[pl.BlockSpec(memory_space=pltpu.HBM)],
         out_specs=pl.BlockSpec(memory_space=pltpu.VMEM),
-        out_shape=jax.ShapeDtypeStruct((1, columns), f32),
+        out_shape=jax.ShapeDtypeStruct((lanes, lanes), f32),
         scratch_shapes=[
             pltpu.VMEM((columns // rows, rows, depth), targets.dtype),
             pltpu.SemaphoreType.DMA((columns // rows,)),
@@ -218,7 +262,7 @@
         cost_estimate=cost(rows * lanes, 12 * rows * lanes),
         name="core_sum",
     )(keep, came)
-    return outs[:chunks], outs[chunks:]
+    return list(outs[:chunks]), list(outs[chunks:])
 
 
 def feature_kernel(chunk, programs, lengths, left_ref, came_ref, mine_ref, other_ref, held):
@@ -267,7 +311,7 @@
     )(lengths, left, came)
 
 
-def score_kernel(count, far, order_ref, targets_ref, *refs):
+def score_kernel(count, far, order_ref, squares_ref, targets_ref, *refs):
     pieces, sends, (keep_ref, ordered) = refs[:count], refs[count:-2], refs[-2:]
     columns, rows = targets_ref.shape[0], keep_ref.shape[0]
 
@@ -298,7 +342,11 @@
         found = jnp.dot(chosen, block, preferred_element_type=f32)
         ordered[:, a * lanes : (a + 2) * lanes] = found.astype(bf16)
         totals += found[:, :lanes] * found[:, :lanes] + found[:, lanes:] * found[:, lanes:]
-    store(columns, lanes, totals.astype(bf16))
+    lane = lax.broadcasted_iota(jnp.int32, (2 * rows, lanes), 1)
+    row_squares = jnp.sum(totals, axis=1, keepdims=True)
+    spare = jnp.zeros((rows - lanes, lanes), f32)
+    squares = jnp.concatenate([squares_ref[...], spare] * 2 if rows > lanes else [squares_ref[...]] * 2, axis=0)
+    store(columns, lanes, jnp.where(lane == middle, row_squares, squares).astype(bf16))
     tile = min(512, columns)
     for j in range(0, columns, tile):
         scores = lax.dot_general(
@@ -307,7 +355,7 @@
         store(j, tile, scores)
 
 
-def partial_scores(far, order, pieces, targets, rows):
+def partial_scores(far, order, squares, pieces, targets, rows):
     columns, depth = targets.shape
     held = 2 * (4 * rows * depth + 4 * rows * columns + 8 * rows * order.size)
     limit = 6 + held // 1024**2
@@ -317,14 +365,14 @@
     whole = jax.ShapeDtypeStruct((rows, columns + lanes), bf16)
     return pl.pallas_call(
         functools.partial(score_kernel, len(pieces), far),
-        in_specs=[vmem] * (2 + len(pieces)),
+        in_specs=[vmem] * (3 + len(pieces)),
         out_specs=[vmem] * (sends + 1),
         out_shape=[shape] * sends + [whole],
         scratch_shapes=[pltpu.VMEM((2 * rows, depth), bf16)],
         compiler_params=params(limit),
         cost_estimate=cost(4 * rows * columns * depth, 2 * columns * depth),
         name="scores_far" if far else "scores_near",
-    )(order, pltpu.with_memory_space_constraint(targets, pltpu.VMEM), *pieces)
+    )(order, squares, pltpu.with_memory_space_constraint(targets, pltpu.VMEM), *pieces)
 
 
 def join_kernel(keep_ref, came_ref, out_ref):
@@ -344,37 +392,37 @@
     )(keep, came)
 
 
-def finish_kernel(root_count, keep_ref, low_ref, high_ref, far_ref, squares_ref, out_ref):
+def finish_kernel(root_count, keep_ref, low_ref, high_ref, far_ref, out_ref):
     columns = out_ref.shape[1]
-    tile = min(512, columns)
     height = low_ref.shape[0]
-    for i, near_ref in enumerate((low_ref, high_ref)):
+
+    def total(i, first, size):
+        rows, strip = slice(i * height, (i + 1) * height), slice(first, first + size)
+        mine = keep_ref[rows, strip].astype(f32) + (low_ref, high_ref)[i][:, strip].astype(f32)
+        return mine + far_ref[rows, strip].astype(f32)
+
+    squares = jnp.concatenate([total(i, columns, lanes) for i in range(2)], axis=0)
+    row_scale = lax.rsqrt(squares[:, middle : middle + 1] + epsilon) * root_count
+    column_scale = lax.rsqrt(squares[:lanes, :].T + epsilon)
+    for i in range(2):
         rows = slice(i * height, (i + 1) * height)
-
-        def total(first, size):
-            strip = slice(first, first + size)
-            mine = keep_ref[rows, strip].astype(f32) + near_ref[:, strip].astype(f32)
-            return mine + far_ref[rows, strip].astype(f32)
-
-        squares = jnp.sum(total(columns, lanes), axis=1, keepdims=True)
-        row_scale = lax.rsqrt(squares + epsilon) * root_count
-        for j in range(0, columns, tile):
-            column_scale = lax.rsqrt(squares_ref[:, j : j + tile] + epsilon)
-            out_ref[rows, j : j + tile] = total(j, tile) * row_scale * column_scale
-
-
-def finish(root_count, keep, low, high, far, squares):
-    rows, columns = keep.shape[0], squares.shape[1]
+        for q in range(columns // lanes):
+            scaled = total(i, q * lanes, lanes) * row_scale[rows, :] * column_scale[q : q + 1, :]
+            out_ref[rows, q * lanes : (q + 1) * lanes] = scaled
+
+
+def finish(root_count, keep, low, high, far):
+    rows, columns = keep.shape[0], keep.shape[1] - lanes
     vmem = pl.BlockSpec(memory_space=pltpu.VMEM)
     return pl.pallas_call(
         functools.partial(finish_kernel, root_count),
-        in_specs=[vmem] * 5,
+        in_specs=[vmem] * 4,
         out_specs=vmem,
         out_shape=jax.ShapeDtypeStruct((rows, columns), f32),
         compiler_params=params(24),
         cost_estimate=cost(4 * rows * columns, 10 * rows * columns),
         name="finish",
-    )(keep, low, high, far, squares)
+    )(keep, low, high, far)
 
 
 def shards(
@@ -396,14 +444,13 @@
     share = programs // 2
     tokens = share * length
     rank = rank_side_projection.T
-    operands = (layer_input_rows, output_gradient_rows, input_side_projection, adapter_up_weight, rank)
-
-    send = project(False, *operands)
-    keep = project(True, *operands)
+    send, *staged = project_send(
+        layer_input_rows, output_gradient_rows, input_side_projection, adapter_up_weight, rank
+    )
+    keep = project_keep(*staged, rank)
     sends, lefts = core_sum(keep, exchange(send, "narrow", 1), tokens)
-    squares = row_squares(after(targets, sends[0]))
-    squares = squares + exchange(squares, "narrow", 1)
-    squares = squares + exchange(squares, "narrow", 2)
+    squares = column_squares(after(targets, sends[0]))
+    lefts[0], squares = lax.optimization_barrier((lefts[0], squares))
     blocks = []
     for i in range(chunks):
         came = exchange(sends[i], "narrow", 2)
@@ -419,14 +466,14 @@
     order = jnp.where(core == 1, order[:, ::-1], order).transpose(0, 2, 1, 3).reshape(1, -1)
     rows = order.shape[1] // narrow_count
 
-    far_send, far_keep = partial_scores(True, order, pieces, targets, rows)
+    far_send, far_keep = partial_scores(True, order, squares, pieces, targets, rows)
     far = join(far_keep, exchange(far_send, "narrow", 1))
     order, far = lax.optimization_barrier((order, far))
     far = exchange(far, "narrow", 2)
-    *near_sends, near_keep = partial_scores(False, order, pieces, targets, rows)
+    *near_sends, near_keep = partial_scores(False, order, squares, pieces, targets, rows)
     near = [exchange(part, "narrow", 1) for part in near_sends]
     root_count = math.sqrt(float(targets.shape[1] * narrow_count))
-    return finish(root_count, near_keep, *near, far, squares)
+    return finish(root_count, near_keep, *near, far)
 
 
 def solution(mesh):

time: 70.9 us -> 68.6 us (0.968)
  Pallas kernels: 23.1 us -> 21.3 us
    pallas_call x3, Pallas kernels: 10.7 us -> 9.05 us  [the longest x1 3.75 us: column_squares(): pl.pallas_call(square_kernel, in_specs=[pl.BlockSpec(memory_space=pltpu.H...]
    ppermute x25 -> x23, waiting for transfers between devices: 19.5 us -> 19.1 us  [exchange(): return lax.ppermute(array, axis, [(i, i ^ bit) for i in range(count)])]
    ppermute x25 -> x23, starting transfers between devices: 27 us -> 26.8 us  [exchange(): return lax.ppermute(array, axis, [(i, i ^ bit) for i in range(count)])]
  transfers between devices with their start and end apart: 25 -> 23, of which waited for: 11 -> 12; matrix products, arithmetic and copies ran while one was open for 1% -> 1% of each run, Pallas kernels for 20% -> 18%
where the time goes in v5:
time: 68.6 us; the launch traced here: 68.4 us
  starting transfers between devices  26.8 us (39%)
  Pallas kernels  21.3 us (31%)
  waiting for transfers between devices  19.1 us (28%)
  local copies, waits for them, and re-layouts  0.79 us (1%)
    ppermute x23, starting transfers between devices, exchange(): return lax.ppermute(array, axis, [(i, i ^ bit) for i in range(count)])  26.8 us
    ppermute x23, waiting for transfers between devices, exchange(): return lax.ppermute(array, axis, [(i, i ^ bit) for i in range(count)])  19.1 us
    pallas_call x2, Pallas kernels, partial_scores(): pl.pallas_call(functools.partial(score_kernel, len(pieces), far), in_spec...  5.83 us
    pallas_call x1, Pallas kernels, column_squares(): pl.pallas_call(square_kernel, in_specs=[pl.BlockSpec(memory_space=pltpu.H...  3.75 us
    pallas_call x1, Pallas kernels, project_send(): pl.pallas_call(project_send_kernel, in_specs=[pl.BlockSpec(memory_space=p...  3.74 us
    pallas_call x1, Pallas kernels, stage(): pl.pallas_call(stage_kernel, in_specs=[pl.BlockSpec(memory_space=pltpu.HB...  3.39 us
    pallas_call x2, Pallas kernels, make_features(): pl.pallas_call(functools.partial(feature_kernel, chunk, programs), in_spe...  1.62 us
    pallas_call x1, Pallas kernels, project_keep(): pl.pallas_call(project_keep_kernel, in_specs=[vmem] * 5, out_specs=vmem,...  1.56 us
  transfers between devices with their start and end apart: 23, of which 12 were waited for; matrix products, arithmetic and copies ran while one was open for 1% of the time, Pallas kernels for 18%

profile of v5, /device:TPU:0, one launch (start us, length us, event | category | flops | bytes accessed | tf_op | source)
XLA Modules:
  0.0 68.4 jit_solution(10925509162261957193)
XLA Ops:
  0.0 3.7 %project_send.1 = (bf16[1536,128]{1,0:T(8,128)(2,1)S(1)}, bf16[1024,1024]{1,0:T(8,128)(2,1)S(1)}, bf16[1024,1024]{1,0:T(8,128)(2,1)S(1)}, bf16[1024,128]{1,0:T(8,128)(2,1)S(1)}, bf16[1024,128]{1,0:T(8,128)(2,1)S(1)}) custom-call(bf16[2048,1024]{1,0:T(8,128)(2,1)} %x_hbm.1, bf16[2048,1024]{1,0:T(8,128)(2,1)} %g_hbm.1, bf16[1024,128]{1,0:T(8,128)(2,1)} %w_hbm.1, ...), custom_call_target="tpu_custom_call" | custom-call | flops 536870912 | bytes 8388608 | tf_op jit(solution)/shard_map/project_send/pallas_call | solution.py:137
  3.7 0.5 collective-permute-start
  4.3 1.6 %project_keep.1.keep_ref = f32[1536,128]{1,0:T(8,128)S(1)} custom-call(bf16[1024,1024]{1,0:T(8,128)(2,1)S(1)} %get-tuple-element.35.x, bf16[1024,1024]{1,0:T(8,128)(2,1)S(1)} %get-tuple-element.36.g, bf16[1024,128]{1,0:T(8,128)(2,1)S(1)} %get-tuple-element.37.w, bf16[1024,128]{1,0:T(8,128)(2,1)S(1)} %get-tuple-element.38.up, bf16[64,128]{1,0:T(8,128)(2,1)S(1)} %bitcast.10), custom_call_target="tpu_custom_call" | custom-call | flops 536870912 | bytes 4194304 | tf_op jit(solution)/shard_map/project_keep/pallas_call | solution.py:164
  5.8 0.1 core_sum.1
  6.0 2.7 %collective-permute-start.1 = (bf16[640,128]{1,0:T(8,128)(2,1)S(1)}, bf16[640,128]{1,0:T(8,128)(2,1)S(1)}, u32[]{:S(2)}, u32[]{:S(2)}) collective-permute-start(bf16[640,128]{1,0:T(8,128)(2,1)S(1)} %get-tuple-element.41), channel_id=1, source_target_pairs={{0,2},{1,3},{2,0},{3,1},{4,6},{5,7},{6,4},{7,5},{8,10},{9,11},{10,... | collective-permute-start | bytes 491528 | tf_op jit(solution)/shard_map/ppermute | solution.py:29
  8.7 3.8 %squares.1.squares_ref = f32[128,128]{1,0:T(8,128)S(1)} custom-call(bf16[2048,2048]{1,0:T(8,128)(2,1)} %targets_hbm.1), custom_call_target="tpu_custom_call" | custom-call | flops 8388608 | bytes 8388608 | tf_op jit(solution)/shard_map/squares/pallas_call | solution.py:199
  12.4 1.0 %collective-permute-done.1.came_ref = bf16[640,128]{1,0:T(8,128)(2,1)S(1)} collective-permute-done((bf16[640,128]{1,0:T(8,128)(2,1)S(1)}, bf16[640,128]{1,0:T(8,128)(2,1)S(1)}, u32[]{:S(2)}, u32[]{:S(2)}) %collective-permute-start.1) | collective-permute-done | bytes 163872 | tf_op jit(solution)/shard_map/ppermute | solution.py:29
  13.4 0.8 %features.2 = (bf16[16,16,128]{2,1,0:T(8,128)(2,1)S(1)}, bf16[16,16,128]{2,1,0:T(8,128)(2,1)S(1)}) custom-call(s32[64]{0:T(128)S(1)} %copy-done.1, f32[640,128]{1,0:T(8,128)S(1)} %get-tuple-element.45.left_ref, bf16[640,128]{1,0:T(8,128)(2,1)S(1)} %collective-permute-done.1.came_ref), custom_call_target="tpu_custom_call" | custom-call | flops 100000000 | bytes 655360 | tf_op jit(solution)/shard_map/features/pallas_call | solution.py:302
  14.2 0.1 collective-permute-start.2
  14.3 1.8 %collective-permute-start.3 = (bf16[640,128]{1,0:T(8,128)(2,1)S(1)}, bf16[640,128]{1,0:T(8,128)(2,1)S(1)}, u32[]{:S(2)}, u32[]{:S(2)}) collective-permute-start(bf16[640,128]{1,0:T(8,128)(2,1)S(1)} %get-tuple-element.49), channel_id=1, source_target_pairs={{0,2},{1,3},{2,0},{3,1},{4,6},{5,7},{6,4},{7,5},{8,10},{9,11},{10,... | collective-permute-start | bytes 491528 | tf_op jit(solution)/shard_map/ppermute | solution.py:29
  16.1 2.7 %collective-permute-start.5 = (bf16[2,16,16,128]{3,2,1,0:T(8,128)(2,1)S(1)}, bf16[2,16,16,128]{3,2,1,0:T(8,128)(2,1)S(1)}, u32[]{:S(2)}, u32[]{:S(2)}) collective-permute-start(bf16[2,16,16,128]{3,2,1,0:T(8,128)(2,1)S(1)} %pad_maximum_fusion.refs_0_), channel_id=1, source_target_pairs={{0,16},{4,20},{8,24},{12,28},{16,0},{20,4},{24,8},{28,12},{1,17},{... | collective-permute-start | bytes 393224 | tf_op jit(solution)/shard_map/ppermute | solution.py:29
  18.8 2.1 %collective-permute-done.3.came_ref = bf16[640,128]{1,0:T(8,128)(2,1)S(1)} collective-permute-done((bf16[640,128]{1,0:T(8,128)(2,1)S(1)}, bf16[640,128]{1,0:T(8,128)(2,1)S(1)}, u32[]{:S(2)}, u32[]{:S(2)}) %collective-permute-start.3) | collective-permute-done | bytes 163872 | tf_op jit(solution)/shard_map/ppermute | solution.py:29
  20.9 0.8 %features.3 = (bf16[16,16,128]{2,1,0:T(8,128)(2,1)S(1)}, bf16[16,16,128]{2,1,0:T(8,128)(2,1)S(1)}) custom-call(s32[64]{0:T(128)S(1)} %copy-done.1, f32[640,128]{1,0:T(8,128)S(1)} %get-tuple-element.48.left_ref, bf16[640,128]{1,0:T(8,128)(2,1)S(1)} %collective-permute-done.3.came_ref), custom_call_target="tpu_custom_call" | custom-call | flops 100000000 | bytes 655360 | tf_op jit(solution)/shard_map/features/pallas_call | solution.py:302
  21.7 0.1 collective-permute-start.4
  21.8 1.9 %collective-permute-start.10 = (bf16[2,16,16,128]{3,2,1,0:T(8,128)(2,1)S(1)}, bf16[2,16,16,128]{3,2,1,0:T(8,128)(2,1)S(1)}, u32[]{:S(2)}, u32[]{:S(2)}) collective-permute-start(bf16[2,16,16,128]{3,2,1,0:T(8,128)(2,1)S(1)} %pad_maximum_fusion.refs_0_), channel_id=1, source_target_pairs={{0,8},{4,12},{8,0},{12,4},{16,24},{20,28},{24,16},{28,20},{1,9},{5... | collective-permute-start | bytes 393224 | tf_op jit(solution)/shard_map/ppermute | solution.py:29
  23.7 1.5 %collective-permute-start.8 = (bf16[2,16,16,128]{3,2,1,0:T(8,128)(2,1)S(1)}, bf16[2,16,16,128]{3,2,1,0:T(8,128)(2,1)S(1)}, u32[]{:S(2)}, u32[]{:S(2)}) collective-permute-start(bf16[2,16,16,128]{3,2,1,0:T(8,128)(2,1)S(1)} %pad_maximum_fusion.refs_0_), channel_id=1, source_target_pairs={{0,4},{4,0},{8,12},{12,8},{16,20},{20,16},{24,28},{28,24},{1,5},{5... | collective-permute-start | bytes 393224 | tf_op jit(solution)/shard_map/ppermute | solution.py:29
  25.2 0.3 collective-permute-done.5.refs_8_
  25.5 2.4 %collective-permute-start.6 = (bf16[2,16,16,128]{3,2,1,0:T(8,128)(2,1)S(1)}, bf16[2,16,16,128]{3,2,1,0:T(8,128)(2,1)S(1)}, u32[]{:S(2)}, u32[]{:S(2)}) collective-permute-start(bf16[2,16,16,128]{3,2,1,0:T(8,128)(2,1)S(1)} %pad_maximum_fusion.1.refs_1_), channel_id=1, source_target_pairs={{0,16},{4,20},{8,24},{12,28},{16,0},{20,4},{24,8},{28,12},{1,17},{... | collective-permute-start | bytes 393224 | tf_op jit(solution)/shard_map/ppermute | solution.py:29
  27.9 0.1 reshape.27
  28.0 0.6 gather_fusion
  28.6 1.7 %collective-permute-start.11 = (bf16[2,16,16,128]{3,2,1,0:T(8,128)(2,1)S(1)}, bf16[2,16,16,128]{3,2,1,0:T(8,128)(2,1)S(1)}, u32[]{:S(2)}, u32[]{:S(2)}) collective-permute-start(bf16[2,16,16,128]{3,2,1,0:T(8,128)(2,1)S(1)} %pad_maximum_fusion.1.refs_1_), channel_id=1, source_target_pairs={{0,8},{4,12},{8,0},{12,4},{16,24},{20,28},{24,16},{28,20},{1,9},{5... | collective-permute-start | bytes 393224 | tf_op jit(solution)/shard_map/ppermute | solution.py:29
  30.3 1.5 %collective-permute-start.9 = (bf16[2,16,16,128]{3,2,1,0:T(8,128)(2,1)S(1)}, bf16[2,16,16,128]{3,2,1,0:T(8,128)(2,1)S(1)}, u32[]{:S(2)}, u32[]{:S(2)}) collective-permute-start(bf16[2,16,16,128]{3,2,1,0:T(8,128)(2,1)S(1)} %pad_maximum_fusion.1.refs_1_), channel_id=1, source_target_pairs={{0,4},{4,0},{8,12},{12,8},{16,20},{20,16},{24,28},{28,24},{1,5},{5... | collective-permute-start | bytes 393224 | tf_op jit(solution)/shard_map/ppermute | solution.py:29
  31.8 0.5 collective-permute-start.15
  32.3 0.4 collective-permute-start.12
  32.7 1.7 %collective-permute-done.6.refs_9_ = bf16[2,16,16,128]{3,2,1,0:T(8,128)(2,1)S(1)} collective-permute-done((bf16[2,16,16,128]{3,2,1,0:T(8,128)(2,1)S(1)}, bf16[2,16,16,128]{3,2,1,0:T(8,128)(2,1)S(1)}, u32[]{:S(2)}, u32[]{:S(2)}) %collective-permute-start.6) | collective-permute-done | bytes 131104 | tf_op jit(solution)/shard_map/ppermute | solution.py:29
  34.4 0.6 collective-permute-start.7
  35.0 0.1 broadcast_select_fusion
  35.1 0.6 collective-permute-done.11.refs_5_
  35.7 0.8 %collective-permute-done.9.refs_3_ = bf16[2,16,16,128]{3,2,1,0:T(8,128)(2,1)S(1)} collective-permute-done((bf16[2,16,16,128]{3,2,1,0:T(8,128)(2,1)S(1)}, bf16[2,16,16,128]{3,2,1,0:T(8,128)(2,1)S(1)}, u32[]{:S(2)}, u32[]{:S(2)}) %collective-permute-start.9) | collective-permute-done | bytes 131104 | tf_op jit(solution)/shard_map/ppermute | solution.py:29
  36.5 1.5 %collective-permute-start.16 = (bf16[2,16,16,128]{3,2,1,0:T(8,128)(2,1)S(1)}, bf16[2,16,16,128]{3,2,1,0:T(8,128)(2,1)S(1)}, u32[]{:S(2)}, u32[]{:S(2)}) collective-permute-start(bf16[2,16,16,128]{3,2,1,0:T(8,128)(2,1)S(1)} %collective-permute-done.6.refs_9_), channel_id=1, source_target_pairs={{0,4},{4,0},{8,12},{12,8},{16,20},{20,16},{24,28},{28,24},{1,5},{5... | collective-permute-start | bytes 393224 | tf_op jit(solution)/shard_map/ppermute | solution.py:29
  38.1 0.7 collective-permute-done.12.refs_12_
  38.7 0.7 %collective-permute-start.13 = (bf16[2,16,16,128]{3,2,1,0:T(8,128)(2,1)S(1)}, bf16[2,16,16,128]{3,2,1,0:T(8,128)(2,1)S(1)}, u32[]{:S(2)}, u32[]{:S(2)}) collective-permute-start(bf16[2,16,16,128]{3,2,1,0:T(8,128)(2,1)S(1)} %collective-permute-done.8.refs_2_), channel_id=1, source_target_pairs={{0,8},{4,12},{8,0},{12,4},{16,24},{20,28},{24,16},{28,20},{1,9},{5... | collective-permute-start | bytes 393224 | tf_op jit(solution)/shard_map/ppermute | solution.py:29
  39.5 1.5 %collective-permute-start.17 = (bf16[2,16,16,128]{3,2,1,0:T(8,128)(2,1)S(1)}, bf16[2,16,16,128]{3,2,1,0:T(8,128)(2,1)S(1)}, u32[]{:S(2)}, u32[]{:S(2)}) collective-permute-start(bf16[2,16,16,128]{3,2,1,0:T(8,128)(2,1)S(1)} %collective-permute-done.12.refs_12_), channel_id=1, source_target_pairs={{0,4},{4,0},{8,12},{12,8},{16,20},{20,16},{24,28},{28,24},{1,5},{5... | collective-permute-start | bytes 393224 | tf_op jit(solution)/shard_map/ppermute | solution.py:29
  41.0 0.6 collective-permute-done.7.refs_13_
  41.6 0.7 %collective-permute-start.14 = (bf16[2,16,16,128]{3,2,1,0:T(8,128)(2,1)S(1)}, bf16[2,16,16,128]{3,2,1,0:T(8,128)(2,1)S(1)}, u32[]{:S(2)}, u32[]{:S(2)}) collective-permute-start(bf16[2,16,16,128]{3,2,1,0:T(8,128)(2,1)S(1)} %collective-permute-done.9.refs_3_), channel_id=1, source_target_pairs={{0,8},{4,12},{8,0},{12,4},{16,24},{20,28},{24,16},{28,20},{1,9},{5... | collective-permute-start | bytes 393224 | tf_op jit(solution)/shard_map/ppermute | solution.py:29
  42.3 1.5 %collective-permute-start.18 = (bf16[2,16,16,128]{3,2,1,0:T(8,128)(2,1)S(1)}, bf16[2,16,16,128]{3,2,1,0:T(8,128)(2,1)S(1)}, u32[]{:S(2)}, u32[]{:S(2)}) collective-permute-start(bf16[2,16,16,128]{3,2,1,0:T(8,128)(2,1)S(1)} %collective-permute-done.7.refs_13_), channel_id=1, source_target_pairs={{0,4},{4,0},{8,12},{12,8},{16,20},{20,16},{24,28},{28,24},{1,5},{5... | collective-permute-start | bytes 393224 | tf_op jit(solution)/shard_map/ppermute | solution.py:29
  43.8 0.1 reshape.28.order_ref
  43.9 3.4 %stage.1.targets_ref = bf16[2048,2048]{1,0:T(8,128)(2,1)S(1)} custom-call(bf16[2048,2048]{1,0:T(8,128)(2,1)} %targets_hbm.1), custom_call_target="tpu_custom_call" | custom-call | bytes 8388608 | tf_op jit(solution)/shard_map/stage/pallas_call | solution.py:221
  47.4 2.9 %scores_far.1 = (bf16[128,2176]{1,0:T(8,128)(2,1)S(1)}, bf16[128,2176]{1,0:T(8,128)(2,1)S(1)}) custom-call(s32[1,512]{1,0:T(1,128)S(1)} %reshape.28.order_ref, f32[128,128]{1,0:T(8,128)S(1)} %squares.1.squares_ref, bf16[2048,2048]{1,0:T(8,128)(2,1)S(1)} %stage.1.targets_ref, bf16[2,16,16,128]{3,2,1,0:T(8,128)(2,1)S(1)} %pad_maximum_fusion.refs_0_, ...), custom_call_target="tpu_custom_call" | custom-call | flops 2147483648 | bytes 8388608 | tf_op jit(solution)/shard_map/scores_far/pallas_call | solution.py:366
  50.4 1.9 %collective-permute-done.19.came_ref = bf16[128,2176]{1,0:T(8,128)(2,1)S(1)} collective-permute-done((bf16[128,2176]{1,0:T(8,128)(2,1)S(1)}, bf16[128,2176]{1,0:T(8,128)(2,1)S(1)}, u32[]{:S(2)}, u32[]{:S(2)}) %collective-permute-start.19) | collective-permute-done | bytes 557088 | tf_op jit(solution)/shard_map/ppermute | solution.py:29
  52.3 0.1 join.1
  52.5 1.8 %collective-permute-start.22 = (bf16[128,2176]{1,0:T(8,128)(2,1)S(1)}, bf16[128,2176]{1,0:T(8,128)(2,1)S(1)}, u32[]{:S(2)}, u32[]{:S(2)}) collective-permute-start(bf16[128,2176]{1,0:T(8,128)(2,1)S(1)} %join.1), channel_id=1, source_target_pairs={{0,2},{1,3},{2,0},{3,1},{4,6},{5,7},{6,4},{7,5},{8,10},{9,11},{10,... | collective-permute-start | bytes 1671176 | tf_op jit(solution)/shard_map/ppermute | solution.py:29
  54.2 2.9 %scores_near.1 = (bf16[64,2176]{1,0:T(8,128)(2,1)S(1)}, bf16[64,2176]{1,0:T(8,128)(2,1)S(1)}, bf16[128,2176]{1,0:T(8,128)(2,1)S(1)}) custom-call(s32[1,512]{1,0:T(1,128)S(1)} %reshape.28.order_ref, f32[128,128]{1,0:T(8,128)S(1)} %squares.1.squares_ref, bf16[2048,2048]{1,0:T(8,128)(2,1)S(1)} %stage.1.targets_ref, ...), custom_call_target="tpu_custom_call" | custom-call | flops 2147483648 | bytes 8388608 | tf_op jit(solution)/shard_map/scores_near/pallas_call | solution.py:366
  57.2 0.5 collective-permute-start.21
  57.7 1.0 %collective-permute-done.20.low_ref = bf16[64,2176]{1,0:T(8,128)(2,1)S(1)} collective-permute-done((bf16[64,2176]{1,0:T(8,128)(2,1)S(1)}, bf16[64,2176]{1,0:T(8,128)(2,1)S(1)}, u32[]{:S(2)}, u32[]{:S(2)}) %collective-permute-start.20) | collective-permute-done | bytes 278560 | tf_op jit(solution)/shard_map/ppermute | solution.py:29
  58.8 0.4 collective-permute-done.21.high_ref
  59.2 8.0 %collective-permute-done.22.far_ref = bf16[128,2176]{1,0:T(8,128)(2,1)S(1)} collective-permute-done((bf16[128,2176]{1,0:T(8,128)(2,1)S(1)}, bf16[128,2176]{1,0:T(8,128)(2,1)S(1)}, u32[]{:S(2)}, u32[]{:S(2)}) %collective-permute-start.22) | collective-permute-done | bytes 557088 | tf_op jit(solution)/shard_map/ppermute | solution.py:29
  67.2 1.2 %finish.1 = f32[128,2048]{1,0:T(8,128)} custom-call(bf16[128,2176]{1,0:T(8,128)(2,1)S(1)} %get-tuple-element.61.keep_ref, bf16[64,2176]{1,0:T(8,128)(2,1)S(1)} %collective-permute-done.20.low_ref, bf16[64,2176]{1,0:T(8,128)(2,1)S(1)} %collective-permute-done.21.high_ref, bf16[128,2176]{1,0:T(8,128)(2,1)S(1)} %collective-permute-done.22.far_ref), custom_call_target="tpu_custom_call" | custom-call | flops 1048576 | bytes 2621440 | tf_op jit(solution)/shard_map/finish/pallas_call | solution.py:417
  (26 shorter events, 0.3 us)
Async XLA Ops:
  0.0 4.3 %copy-start = (bf16[128,64]{0,1:T(8,128)(2,1)S(1)}, bf16[128,64]{0,1:T(8,128)(2,1)}, u32[]{:S(2)}) copy-start(bf16[128,64]{0,1:T(8,128)(2,1)} %param.12) | copy-start | bytes 49156
  3.7 2.1 %collective-permute-start = (bf16[1536,128]{1,0:T(8,128)(2,1)S(1)}, bf16[1536,128]{1,0:T(8,128)(2,1)S(1)}, u32[]{:S(2)}, u32[]{:S(2)}) collective-permute-start(bf16[1536,128]{1,0:T(8,128)(2,1)S(1)} %get-tuple-element.39), channel_id=1, source_target_pairs={{0,1},{1,0},{2,3},{3,2},{4,5},{5,4},{6,7},{7,6},{8,9},{9,8},{10,11... | collective-permute-start | bytes 1179656 | tf_op jit(solution)/shard_map/ppermute | solution.py:29
  5.9 7.5 %copy-start.1 = (s32[64]{0:T(128)S(1)}, s32[64]{0:T(128)}, u32[]{:S(2)}) copy-start(s32[64]{0:T(128)} %lengths.3) | copy-start | bytes 772
  5.9 22.0 %copy-start.2 = (s32[512]{0:T(512)S(1)}, s32[512]{0:T(512)}, u32[]{:S(2)}) copy-start(s32[512]{0:T(512)} %param.14) | copy-start | bytes 6148
  6.0 7.4 %collective-permute-start.1 = (bf16[640,128]{1,0:T(8,128)(2,1)S(1)}, bf16[640,128]{1,0:T(8,128)(2,1)S(1)}, u32[]{:S(2)}, u32[]{:S(2)}) collective-permute-start(bf16[640,128]{1,0:T(8,128)(2,1)S(1)} %get-tuple-element.41), channel_id=1, source_target_pairs={{0,2},{1,3},{2,0},{3,1},{4,6},{5,7},{6,4},{7,5},{8,10},{9,11},{10,... | collective-permute-start | bytes 491528 | tf_op jit(solution)/shard_map/ppermute | solution.py:29
  14.2 1.9 %collective-permute-start.2 = (bf16[16,16,128]{2,1,0:T(8,128)(2,1)S(1)}, bf16[16,16,128]{2,1,0:T(8,128)(2,1)S(1)}, u32[]{:S(2)}, u32[]{:S(2)}) collective-permute-start(bf16[16,16,128]{2,1,0:T(8,128)(2,1)S(1)} %get-tuple-element.47), channel_id=1, source_target_pairs={{0,1},{1,0},{2,3},{3,2},{4,5},{5,4},{6,7},{7,6},{8,9},{9,8},{10,11... | collective-permute-start | bytes 196616 | tf_op jit(solution)/shard_map/ppermute | solution.py:29
  14.3 6.6 %collective-permute-start.3 = (bf16[640,128]{1,0:T(8,128)(2,1)S(1)}, bf16[640,128]{1,0:T(8,128)(2,1)S(1)}, u32[]{:S(2)}, u32[]{:S(2)}) collective-permute-start(bf16[640,128]{1,0:T(8,128)(2,1)S(1)} %get-tuple-element.49), channel_id=1, source_target_pairs={{0,2},{1,3},{2,0},{3,1},{4,6},{5,7},{6,4},{7,5},{8,10},{9,11},{10,... | collective-permute-start | bytes 491528 | tf_op jit(solution)/shard_map/ppermute | solution.py:29
  16.1 9.4 %collective-permute-start.5 = (bf16[2,16,16,128]{3,2,1,0:T(8,128)(2,1)S(1)}, bf16[2,16,16,128]{3,2,1,0:T(8,128)(2,1)S(1)}, u32[]{:S(2)}, u32[]{:S(2)}) collective-permute-start(bf16[2,16,16,128]{3,2,1,0:T(8,128)(2,1)S(1)} %pad_maximum_fusion.refs_0_), channel_id=1, source_target_pairs={{0,16},{4,20},{8,24},{12,28},{16,0},{20,4},{24,8},{28,12},{1,17},{... | collective-permute-start | bytes 393224 | tf_op jit(solution)/shard_map/ppermute | solution.py:29
  21.7 3.5 %collective-permute-start.4 = (bf16[16,16,128]{2,1,0:T(8,128)(2,1)S(1)}, bf16[16,16,128]{2,1,0:T(8,128)(2,1)S(1)}, u32[]{:S(2)}, u32[]{:S(2)}) collective-permute-start(bf16[16,16,128]{2,1,0:T(8,128)(2,1)S(1)} %get-tuple-element.51), channel_id=1, source_target_pairs={{0,1},{1,0},{2,3},{3,2},{4,5},{5,4},{6,7},{7,6},{8,9},{9,8},{10,11... | collective-permute-start | bytes 196616 | tf_op jit(solution)/shard_map/ppermute | solution.py:29
  21.8 10.0 %collective-permute-start.10 = (bf16[2,16,16,128]{3,2,1,0:T(8,128)(2,1)S(1)}, bf16[2,16,16,128]{3,2,1,0:T(8,128)(2,1)S(1)}, u32[]{:S(2)}, u32[]{:S(2)}) collective-permute-start(bf16[2,16,16,128]{3,2,1,0:T(8,128)(2,1)S(1)} %pad_maximum_fusion.refs_0_), channel_id=1, source_target_pairs={{0,8},{4,12},{8,0},{12,4},{16,24},{20,28},{24,16},{28,20},{1,9},{5... | collective-permute-start | bytes 393224 | tf_op jit(solution)/shard_map/ppermute | solution.py:29
  23.7 8.1 %collective-permute-start.8 = (bf16[2,16,16,128]{3,2,1,0:T(8,128)(2,1)S(1)}, bf16[2,16,16,128]{3,2,1,0:T(8,128)(2,1)S(1)}, u32[]{:S(2)}, u32[]{:S(2)}) collective-permute-start(bf16[2,16,16,128]{3,2,1,0:T(8,128)(2,1)S(1)} %pad_maximum_fusion.refs_0_), channel_id=1, source_target_pairs={{0,4},{4,0},{8,12},{12,8},{16,20},{20,16},{24,28},{28,24},{1,5},{5... | collective-permute-start | bytes 393224 | tf_op jit(solution)/shard_map/ppermute | solution.py:29
  25.5 8.9 %collective-permute-start.6 = (bf16[2,16,16,128]{3,2,1,0:T(8,128)(2,1)S(1)}, bf16[2,16,16,128]{3,2,1,0:T(8,128)(2,1)S(1)}, u32[]{:S(2)}, u32[]{:S(2)}) collective-permute-start(bf16[2,16,16,128]{3,2,1,0:T(8,128)(2,1)S(1)} %pad_maximum_fusion.1.refs_1_), channel_id=1, source_target_pairs={{0,16},{4,20},{8,24},{12,28},{16,0},{20,4},{24,8},{28,12},{1,17},{... | collective-permute-start | bytes 393224 | tf_op jit(solution)/shard_map/ppermute | solution.py:29
  28.6 7.1 %collective-permute-start.11 = (bf16[2,16,16,128]{3,2,1,0:T(8,128)(2,1)S(1)}, bf16[2,16,16,128]{3,2,1,0:T(8,128)(2,1)S(1)}, u32[]{:S(2)}, u32[]{:S(2)}) collective-permute-start(bf16[2,16,16,128]{3,2,1,0:T(8,128)(2,1)S(1)} %pad_maximum_fusion.1.refs_1_), channel_id=1, source_target_pairs={{0,8},{4,12},{8,0},{12,4},{16,24},{20,28},{24,16},{28,20},{1,9},{5... | collective-permute-start | bytes 393224 | tf_op jit(solution)/shard_map/ppermute | solution.py:29
  30.3 6.3 %collective-permute-start.9 = (bf16[2,16,16,128]{3,2,1,0:T(8,128)(2,1)S(1)}, bf16[2,16,16,128]{3,2,1,0:T(8,128)(2,1)S(1)}, u32[]{:S(2)}, u32[]{:S(2)}) collective-permute-start(bf16[2,16,16,128]{3,2,1,0:T(8,128)(2,1)S(1)} %pad_maximum_fusion.1.refs_1_), channel_id=1, source_target_pairs={{0,4},{4,0},{8,12},{12,8},{16,20},{20,16},{24,28},{28,24},{1,5},{5... | collective-permute-start | bytes 393224 | tf_op jit(solution)/shard_map/ppermute | solution.py:29
  31.8 10.5 %collective-permute-start.15 = (bf16[2,16,16,128]{3,2,1,0:T(8,128)(2,1)S(1)}, bf16[2,16,16,128]{3,2,1,0:T(8,128)(2,1)S(1)}, u32[]{:S(2)}, u32[]{:S(2)}) collective-permute-start(bf16[2,16,16,128]{3,2,1,0:T(8,128)(2,1)S(1)} %collective-permute-done.5.refs_8_), channel_id=1, source_target_pairs={{0,4},{4,0},{8,12},{12,8},{16,20},{20,16},{24,28},{28,24},{1,5},{5... | collective-permute-start | bytes 393224 | tf_op jit(solution)/shard_map/ppermute | solution.py:29
  32.3 6.4 %collective-permute-start.12 = (bf16[2,16,16,128]{3,2,1,0:T(8,128)(2,1)S(1)}, bf16[2,16,16,128]{3,2,1,0:T(8,128)(2,1)S(1)}, u32[]{:S(2)}, u32[]{:S(2)}) collective-permute-start(bf16[2,16,16,128]{3,2,1,0:T(8,128)(2,1)S(1)} %collective-permute-done.5.refs_8_), channel_id=1, source_target_pairs={{0,8},{4,12},{8,0},{12,4},{16,24},{20,28},{24,16},{28,20},{1,9},{5... | collective-permute-start | bytes 393224 | tf_op jit(solution)/shard_map/ppermute | solution.py:29
  34.4 7.1 %collective-permute-start.7 = (bf16[2,16,16,128]{3,2,1,0:T(8,128)(2,1)S(1)}, bf16[2,16,16,128]{3,2,1,0:T(8,128)(2,1)S(1)}, u32[]{:S(2)}, u32[]{:S(2)}) collective-permute-start(bf16[2,16,16,128]{3,2,1,0:T(8,128)(2,1)S(1)} %collective-permute-done.6.refs_9_), channel_id=1, source_target_pairs={{0,8},{4,12},{8,0},{12,4},{16,24},{20,28},{24,16},{28,20},{1,9},{5... | collective-permute-start | bytes 393224 | tf_op jit(solution)/shard_map/ppermute | solution.py:29
  36.5 10.8 %collective-permute-start.16 = (bf16[2,16,16,128]{3,2,1,0:T(8,128)(2,1)S(1)}, bf16[2,16,16,128]{3,2,1,0:T(8,128)(2,1)S(1)}, u32[]{:S(2)}, u32[]{:S(2)}) collective-permute-start(bf16[2,16,16,128]{3,2,1,0:T(8,128)(2,1)S(1)} %collective-permute-done.6.refs_9_), channel_id=1, source_target_pairs={{0,4},{4,0},{8,12},{12,8},{16,20},{20,16},{24,28},{28,24},{1,5},{5... | collective-permute-start | bytes 393224 | tf_op jit(solution)/shard_map/ppermute | solution.py:29
  38.7 8.6 %collective-permute-start.13 = (bf16[2,16,16,128]{3,2,1,0:T(8,128)(2,1)S(1)}, bf16[2,16,16,128]{3,2,1,0:T(8,128)(2,1)S(1)}, u32[]{:S(2)}, u32[]{:S(2)}) collective-permute-start(bf16[2,16,16,128]{3,2,1,0:T(8,128)(2,1)S(1)} %collective-permute-done.8.refs_2_), channel_id=1, source_target_pairs={{0,8},{4,12},{8,0},{12,4},{16,24},{20,28},{24,16},{28,20},{1,9},{5... | collective-permute-start | bytes 393224 | tf_op jit(solution)/shard_map/ppermute | solution.py:29
  39.5 7.9 %collective-permute-start.17 = (bf16[2,16,16,128]{3,2,1,0:T(8,128)(2,1)S(1)}, bf16[2,16,16,128]{3,2,1,0:T(8,128)(2,1)S(1)}, u32[]{:S(2)}, u32[]{:S(2)}) collective-permute-start(bf16[2,16,16,128]{3,2,1,0:T(8,128)(2,1)S(1)} %collective-permute-done.12.refs_12_), channel_id=1, source_target_pairs={{0,4},{4,0},{8,12},{12,8},{16,20},{20,16},{24,28},{28,24},{1,5},{5... | collective-permute-start | bytes 393224 | tf_op jit(solution)/shard_map/ppermute | solution.py:29
  41.6 5.8 %collective-permute-start.14 = (bf16[2,16,16,128]{3,2,1,0:T(8,128)(2,1)S(1)}, bf16[2,16,16,128]{3,2,1,0:T(8,128)(2,1)S(1)}, u32[]{:S(2)}, u32[]{:S(2)}) collective-permute-start(bf16[2,16,16,128]{3,2,1,0:T(8,128)(2,1)S(1)} %collective-permute-done.9.refs_3_), channel_id=1, source_target_pairs={{0,8},{4,12},{8,0},{12,4},{16,24},{20,28},{24,16},{28,20},{1,9},{5... | collective-permute-start | bytes 393224 | tf_op jit(solution)/shard_map/ppermute | solution.py:29
  42.3 5.1 %collective-permute-start.18 = (bf16[2,16,16,128]{3,2,1,0:T(8,128)(2,1)S(1)}, bf16[2,16,16,128]{3,2,1,0:T(8,128)(2,1)S(1)}, u32[]{:S(2)}, u32[]{:S(2)}) collective-permute-start(bf16[2,16,16,128]{3,2,1,0:T(8,128)(2,1)S(1)} %collective-permute-done.7.refs_13_), channel_id=1, source_target_pairs={{0,4},{4,0},{8,12},{12,8},{16,20},{20,16},{24,28},{28,24},{1,5},{5... | collective-permute-start | bytes 393224 | tf_op jit(solution)/shard_map/ppermute | solution.py:29
  50.3 2.0 %collective-permute-start.19 = (bf16[128,2176]{1,0:T(8,128)(2,1)S(1)}, bf16[128,2176]{1,0:T(8,128)(2,1)S(1)}, u32[]{:S(2)}, u32[]{:S(2)}) collective-permute-start(bf16[128,2176]{1,0:T(8,128)(2,1)S(1)} %get-tuple-element.59), channel_id=1, source_target_pairs={{0,1},{1,0},{2,3},{3,2},{4,5},{5,4},{6,7},{7,6},{8,9},{9,8},{10,11... | collective-permute-start | bytes 1671176 | tf_op jit(solution)/shard_map/ppermute | solution.py:29
  52.5 14.7 %collective-permute-start.22 = (bf16[128,2176]{1,0:T(8,128)(2,1)S(1)}, bf16[128,2176]{1,0:T(8,128)(2,1)S(1)}, u32[]{:S(2)}, u32[]{:S(2)}) collective-permute-start(bf16[128,2176]{1,0:T(8,128)(2,1)S(1)} %join.1), channel_id=1, source_target_pairs={{0,2},{1,3},{2,0},{3,1},{4,6},{5,7},{6,4},{7,5},{8,10},{9,11},{10,... | collective-permute-start | bytes 1671176 | tf_op jit(solution)/shard_map/ppermute | solution.py:29
  57.2 1.6 %collective-permute-start.20 = (bf16[64,2176]{1,0:T(8,128)(2,1)S(1)}, bf16[64,2176]{1,0:T(8,128)(2,1)S(1)}, u32[]{:S(2)}, u32[]{:S(2)}) collective-permute-start(bf16[64,2176]{1,0:T(8,128)(2,1)S(1)} %get-tuple-element.62), channel_id=1, source_target_pairs={{0,1},{1,0},{2,3},{3,2},{4,5},{5,4},{6,7},{7,6},{8,9},{9,8},{10,11... | collective-permute-start | bytes 835592 | tf_op jit(solution)/shard_map/ppermute | solution.py:29
  57.2 1.9 %collective-permute-start.21 = (bf16[64,2176]{1,0:T(8,128)(2,1)S(1)}, bf16[64,2176]{1,0:T(8,128)(2,1)S(1)}, u32[]{:S(2)}, u32[]{:S(2)}) collective-permute-start(bf16[64,2176]{1,0:T(8,128)(2,1)S(1)} %get-tuple-element.63), channel_id=1, source_target_pairs={{0,1},{1,0},{2,3},{3,2},{4,5},{5,4},{6,7},{7,6},{8,9},{9,8},{10,11... | collective-permute-start | bytes 835592 | tf_op jit(solution)/shard_map/ppermute | solution.py:29

commit v6 on v5

--- a/solution.py
+++ b/solution.py
@@ -51,13 +51,18 @@
         across_beside = [exchange(chunk, "wide", 1) for chunk in across]
         above_beside = [exchange(after(beside[0], across[0]), "wide", 2), exchange(after(beside[1], across[1]), "wide", 2)]
         return blocks, beside, above, above_beside, far, far_beside, across, across_beside
-    held = {0: jnp.stack(blocks)}
+    held = {0: blocks}
     bit = count // 2
     while bit:
         for k in list(held):
-            held[k | bit] = exchange(held[k], "wide", bit)
+            held[k | bit] = [exchange(chunk, "wide", bit) for chunk in held[k]]
         bit //= 2
-    return [[held[k]] for k in range(count)]
+    return [held[k] for k in range(count)]
+
+
+def parts_of(programs):
+    number = programs // chunks
+    return [(i * number, number) for i in range(chunks)]
 
 
 def position():
@@ -230,34 +235,36 @@
     )(pltpu.with_memory_space_constraint(targets, pltpu.HBM))
 
 
-def core_sum_kernel(keep_ref, came_ref, *outs):
+def core_sum_kernel(parts, length, keep_ref, came_ref, *outs):
     sends, lefts = outs[:chunks], outs[chunks:]
     rows = keep_ref.shape[0]
-    final = sends[0].shape[0]
-    stack = (rows - chunks * final) // chunks
-    tokens = final - stack
+    tokens = sum(number for _, number in parts) * length
+    stack = (rows - tokens) // 2
     _, x = position()
-    for i in range(chunks):
-        part = slice(i * tokens, (i + 1) * tokens)
+    for (first, number), send_ref, left_ref in zip(parts, sends, lefts):
+        size = number * length
+        part = slice(first * length, first * length + size)
         total = keep_ref[part, :] + came_ref[part, :].astype(f32)
-        sends[i][:tokens, :] = total.astype(bf16)
-        lefts[i][:tokens, :] = total
-        for side, ref in ((1 - x, sends[i]), (x, lefts[i])):
-            first = chunks * tokens + (side * chunks + i) * stack
-            part = pl.ds(pl.multiple_of(first, stack), stack)
+        send_ref[:size, :] = total.astype(bf16)
+        left_ref[:size, :] = total
+        height = stack * size // tokens
+        for side, ref in ((1 - x, send_ref), (x, left_ref)):
+            start = tokens + side * stack + stack * first * length // tokens
+            part = pl.ds(pl.multiple_of(start, 32), height)
             total = keep_ref[part, :] + came_ref[part, :].astype(f32)
-            ref[tokens:, :] = total.astype(ref.dtype)
-
-
-def core_sum(keep, came, tokens):
+            ref[size:, :] = total.astype(ref.dtype)
+
+
+def core_sum(keep, came, parts, length):
     rows = keep.shape[0]
-    final = (tokens + (rows - tokens) // 2) // chunks
+    tokens = sum(number for _, number in parts) * length
+    heights = [(tokens + (rows - tokens) // 2) * number * length // tokens for _, number in parts]
     vmem = pl.BlockSpec(memory_space=pltpu.VMEM)
     outs = pl.pallas_call(
-        core_sum_kernel,
+        functools.partial(core_sum_kernel, parts, length),
         in_specs=[vmem, vmem],
         out_specs=[vmem] * (2 * chunks),
-        out_shape=[jax.ShapeDtypeStruct((final, lanes), dtype) for dtype in (bf16,) * chunks + (f32,) * chunks],
+        out_shape=[jax.ShapeDtypeStruct((height, lanes), dtype) for dtype in (bf16, f32) for height in heights],
         compiler_params=params(8),
         cost_estimate=cost(rows * lanes, 12 * rows * lanes),
         name="core_sum",
@@ -265,7 +272,7 @@
     return list(outs[:chunks]), list(outs[chunks:])
 
 
-def feature_kernel(chunk, programs, lengths, left_ref, came_ref, mine_ref, other_ref, held):
+def feature_kernel(first, core_programs, programs, lengths, left_ref, came_ref, mine_ref, other_ref, held):
     core, _ = position()
     quarter = mine_ref.shape[0]
     out_width = 2 * quarter
@@ -279,15 +286,15 @@
     for group in range(programs // some):
         rows = slice(group * span, (group + 1) * span)
         in_sum = (left_ref[rows, :] + came_ref[rows, :].astype(f32)).astype(bf16)
-        first = tokens + group * (span // lanes) * out_width
-        rows = slice(first, first + span // lanes * out_width)
+        start = tokens + group * (span // lanes) * out_width
+        rows = slice(start, start + span // lanes * out_width)
         out_sum = left_ref[rows, :] + came_ref[rows, :].astype(f32)
         out_rows = jnp.concatenate(
             [out_sum[i * out_width : (i + 1) * out_width, :] for i in range(span // lanes)], axis=1
         )
         limit = jnp.zeros((some, span), jnp.int32)
         for s in range(some):
-            limit = jnp.where(program == s, lengths[(core * chunks + chunk) * programs + group * some + s], limit)
+            limit = jnp.where(program == s, lengths[core * core_programs + first + group * some + s], limit)
         live = ((token >= 0) & (token < limit)).astype(f32)
         spread = (out_rows[:, None, :] * live[None, :, :]).reshape(out_width * some, span)
         made = jnp.dot(spread.astype(bf16), in_sum, preferred_element_type=f32)
@@ -296,11 +303,11 @@
     other_ref[...] = held[pl.ds((1 - core) * quarter, quarter), :, :].astype(bf16)
 
 
-def make_features(chunk, programs, quarter, lengths, left, came):
+def make_features(first, core_programs, programs, quarter, lengths, left, came):
     vmem = pl.BlockSpec(memory_space=pltpu.VMEM)
     shape = jax.ShapeDtypeStruct((quarter, programs, lanes), bf16)
     return pl.pallas_call(
-        functools.partial(feature_kernel, chunk, programs),
+        functools.partial(feature_kernel, first, core_programs, programs),
         in_specs=[pl.BlockSpec(memory_space=pltpu.SMEM), vmem, vmem],
         out_specs=[vmem, vmem],
         out_shape=[shape, shape],
@@ -442,28 +449,30 @@
     length = layer_input_rows.shape[0] // programs
     quarter = rank_side_projection.shape[1] // narrow_count
     share = programs // 2
-    tokens = share * length
+    parts = parts_of(share)
     rank = rank_side_projection.T
     send, *staged = project_send(
         layer_input_rows, output_gradient_rows, input_side_projection, adapter_up_weight, rank
     )
     keep = project_keep(*staged, rank)
-    sends, lefts = core_sum(keep, exchange(send, "narrow", 1), tokens)
+    sends, lefts = core_sum(keep, exchange(send, "narrow", 1), parts, length)
     squares = column_squares(after(targets, sends[0]))
     lefts[0], squares = lax.optimization_barrier((lefts[0], squares))
     blocks = []
     for i in range(chunks):
         came = exchange(sends[i], "narrow", 2)
         left = after(lefts[i], *blocks) if blocks else lefts[i]
-        mine, other = make_features(i, share // chunks, quarter, lengths, left, came)
+        mine, other = make_features(parts[i][0], share, parts[i][1], quarter, lengths, left, came)
         blocks.append(jnp.stack([mine, exchange(other, "narrow", 1)]))
     pieces = gather_blocks(blocks)
     targets = stage(after(targets, pieces[-2][-1]))
     pieces = [chunk for piece in pieces for chunk in piece]
 
-    order = program_output_index.reshape(wide_count, 2, chunks, share // chunks)
+    order = program_output_index.reshape(wide_count, 2, share)
     order = jnp.take(order, w ^ jnp.arange(wide_count), axis=0)
-    order = jnp.where(core == 1, order[:, ::-1], order).transpose(0, 2, 1, 3).reshape(1, -1)
+    order = jnp.where(core == 1, order[:, ::-1], order)
+    order = [order[:, :, first : first + number].reshape(wide_count, -1) for first, number in parts]
+    order = jnp.concatenate(order, axis=1).reshape(1, -1)
     rows = order.shape[1] // narrow_count
 
     far_send, far_keep = partial_scores(True, order, squares, pieces, targets, rows)

time: 68.6 us -> 67.7 us (0.987)
  starting transfers between devices: 26.8 us -> 23.7 us
  waiting for transfers between devices: 19.1 us -> 21 us
    ppermute x23, starting transfers between devices: 26.8 us -> 23.7 us  [exchange(): return lax.ppermute(array, axis, [(i, i ^ bit) for i in range(count)])]
    ppermute x23, waiting for transfers between devices: 19.1 us -> 21 us  [exchange(): return lax.ppermute(array, axis, [(i, i ^ bit) for i in range(count)])]
  transfers between devices with their start and end apart: 23 -> 23, of which waited for: 12 -> 13; matrix products, arithmetic and copies ran while one was open for 1% -> 2% of each run, Pallas kernels for 18% -> 20%
where the time goes in v6:
time: 67.7 us; the launch traced here: 67.6 us
  starting transfers between devices  23.7 us (35%)
  Pallas kernels  21.4 us (32%)
  waiting for transfers between devices  21 us (31%)
  local copies, waits for them, and re-layouts  1.01 us (1%)
    ppermute x23, starting transfers between devices, exchange(): return lax.ppermute(array, axis, [(i, i ^ bit) for i in range(count)])  23.7 us
    ppermute x23, waiting for transfers between devices, exchange(): return lax.ppermute(array, axis, [(i, i ^ bit) for i in range(count)])  21 us
    pallas_call x2, Pallas kernels, partial_scores(): pl.pallas_call(functools.partial(score_kernel, len(pieces), far), in_spec...  5.83 us
    pallas_call x1, Pallas kernels, column_squares(): pl.pallas_call(square_kernel, in_specs=[pl.BlockSpec(memory_space=pltpu.H...  3.77 us
    pallas_call x1, Pallas kernels, project_send(): pl.pallas_call(project_send_kernel, in_specs=[pl.BlockSpec(memory_space=p...  3.74 us
    pallas_call x1, Pallas kernels, stage(): pl.pallas_call(stage_kernel, in_specs=[pl.BlockSpec(memory_space=pltpu.HB...  3.39 us
    pallas_call x2, Pallas kernels, make_features(): pl.pallas_call(functools.partial(feature_kernel, first, core_programs, pr...  1.63 us
    pallas_call x1, Pallas kernels, project_keep(): pl.pallas_call(project_keep_kernel, in_specs=[vmem] * 5, out_specs=vmem,...  1.56 us
  transfers between devices with their start and end apart: 23, of which 13 were waited for; matrix products, arithmetic and copies ran while one was open for 2% of the time, Pallas kernels for 20%

profile of v6, /device:TPU:0, one launch (start us, length us, event | category | flops | bytes accessed | tf_op | source)
XLA Modules:
  0.0 67.6 jit_solution(16640027875064115569)
XLA Ops:
  0.0 3.7 %project_send.1 = (bf16[1536,128]{1,0:T(8,128)(2,1)S(1)}, bf16[1024,1024]{1,0:T(8,128)(2,1)S(1)}, bf16[1024,1024]{1,0:T(8,128)(2,1)S(1)}, bf16[1024,128]{1,0:T(8,128)(2,1)S(1)}, bf16[1024,128]{1,0:T(8,128)(2,1)S(1)}) custom-call(bf16[2048,1024]{1,0:T(8,128)(2,1)} %x_hbm.1, bf16[2048,1024]{1,0:T(8,128)(2,1)} %g_hbm.1, bf16[1024,128]{1,0:T(8,128)(2,1)} %w_hbm.1, ...), custom_call_target="tpu_custom_call" | custom-call | flops 536870912 | bytes 8388608 | tf_op jit(solution)/shard_map/project_send/pallas_call | solution.py:142
  3.7 0.5 collective-permute-start
  4.3 1.6 %project_keep.1.keep_ref = f32[1536,128]{1,0:T(8,128)S(1)} custom-call(bf16[1024,1024]{1,0:T(8,128)(2,1)S(1)} %get-tuple-element.35.x, bf16[1024,1024]{1,0:T(8,128)(2,1)S(1)} %get-tuple-element.36.g, bf16[1024,128]{1,0:T(8,128)(2,1)S(1)} %get-tuple-element.37.w, bf16[1024,128]{1,0:T(8,128)(2,1)S(1)} %get-tuple-element.38.up, bf16[64,128]{1,0:T(8,128)(2,1)S(1)} %bitcast.8), custom_call_target="tpu_custom_call" | custom-call | flops 536870912 | bytes 4194304 | tf_op jit(solution)/shard_map/project_keep/pallas_call | solution.py:169
  5.9 2.7 %collective-permute-start.1 = (bf16[640,128]{1,0:T(8,128)(2,1)S(1)}, bf16[640,128]{1,0:T(8,128)(2,1)S(1)}, u32[]{:S(2)}, u32[]{:S(2)}) collective-permute-start(bf16[640,128]{1,0:T(8,128)(2,1)S(1)} %get-tuple-element.41), channel_id=1, source_target_pairs={{0,2},{1,3},{2,0},{3,1},{4,6},{5,7},{6,4},{7,5},{8,10},{9,11},{10,... | collective-permute-start | bytes 491528 | tf_op jit(solution)/shard_map/ppermute | solution.py:29
  8.6 3.8 %squares.1.squares_ref = f32[128,128]{1,0:T(8,128)S(1)} custom-call(bf16[2048,2048]{1,0:T(8,128)(2,1)} %targets_hbm.1), custom_call_target="tpu_custom_call" | custom-call | flops 8388608 | bytes 8388608 | tf_op jit(solution)/shard_map/squares/pallas_call | solution.py:204
  12.4 0.1 collective-permute-start.3
  12.5 0.8 %collective-permute-done.1.came_ref = bf16[640,128]{1,0:T(8,128)(2,1)S(1)} collective-permute-done((bf16[640,128]{1,0:T(8,128)(2,1)S(1)}, bf16[640,128]{1,0:T(8,128)(2,1)S(1)}, u32[]{:S(2)}, u32[]{:S(2)}) %collective-permute-start.1) | collective-permute-done | bytes 163872 | tf_op jit(solution)/shard_map/ppermute | solution.py:29
  13.4 0.8 %features.2 = (bf16[16,16,128]{2,1,0:T(8,128)(2,1)S(1)}, bf16[16,16,128]{2,1,0:T(8,128)(2,1)S(1)}) custom-call(s32[64]{0:T(128)S(1)} %copy-done.1, f32[640,128]{1,0:T(8,128)S(1)} %get-tuple-element.45.left_ref, bf16[640,128]{1,0:T(8,128)(2,1)S(1)} %collective-permute-done.1.came_ref), custom_call_target="tpu_custom_call" | custom-call | flops 100000000 | bytes 655360 | tf_op jit(solution)/shard_map/features/pallas_call | solution.py:309
  14.3 1.2 %collective-permute-done.2 = bf16[16,16,128]{2,1,0:T(8,128)(2,1)S(1)} collective-permute-done((bf16[16,16,128]{2,1,0:T(8,128)(2,1)S(1)}, bf16[16,16,128]{2,1,0:T(8,128)(2,1)S(1)}, u32[]{:S(2)}, u32[]{:S(2)}) %collective-permute-start.2) | collective-permute-done | bytes 65568 | tf_op jit(solution)/shard_map/ppermute | solution.py:29
  15.5 2.9 %collective-permute-start.5 = (bf16[2,16,16,128]{3,2,1,0:T(8,128)(2,1)S(1)}, bf16[2,16,16,128]{3,2,1,0:T(8,128)(2,1)S(1)}, u32[]{:S(2)}, u32[]{:S(2)}) collective-permute-start(bf16[2,16,16,128]{3,2,1,0:T(8,128)(2,1)S(1)} %pad_maximum_fusion.refs_0_), channel_id=1, source_target_pairs={{0,16},{4,20},{8,24},{12,28},{16,0},{20,4},{24,8},{28,12},{1,17},{... | collective-permute-start | bytes 393224 | tf_op jit(solution)/shard_map/ppermute | solution.py:29
  18.4 0.3 collective-permute-done.3.came_ref
  18.7 0.8 %features.3 = (bf16[16,16,128]{2,1,0:T(8,128)(2,1)S(1)}, bf16[16,16,128]{2,1,0:T(8,128)(2,1)S(1)}) custom-call(s32[64]{0:T(128)S(1)} %copy-done.1, f32[640,128]{1,0:T(8,128)S(1)} %get-tuple-element.48.left_ref, bf16[640,128]{1,0:T(8,128)(2,1)S(1)} %collective-permute-done.3.came_ref), custom_call_target="tpu_custom_call" | custom-call | flops 100000000 | bytes 655360 | tf_op jit(solution)/shard_map/features/pallas_call | solution.py:309
  19.6 0.1 reshape.33
  19.7 0.6 gather_fusion
  20.3 1.6 %collective-permute-start.10 = (bf16[2,16,16,128]{3,2,1,0:T(8,128)(2,1)S(1)}, bf16[2,16,16,128]{3,2,1,0:T(8,128)(2,1)S(1)}, u32[]{:S(2)}, u32[]{:S(2)}) collective-permute-start(bf16[2,16,16,128]{3,2,1,0:T(8,128)(2,1)S(1)} %pad_maximum_fusion.refs_0_), channel_id=1, source_target_pairs={{0,8},{4,12},{8,0},{12,4},{16,24},{20,28},{24,16},{28,20},{1,9},{5... | collective-permute-start | bytes 393224 | tf_op jit(solution)/shard_map/ppermute | solution.py:29
  21.9 1.5 %collective-permute-start.8 = (bf16[2,16,16,128]{3,2,1,0:T(8,128)(2,1)S(1)}, bf16[2,16,16,128]{3,2,1,0:T(8,128)(2,1)S(1)}, u32[]{:S(2)}, u32[]{:S(2)}) collective-permute-start(bf16[2,16,16,128]{3,2,1,0:T(8,128)(2,1)S(1)} %pad_maximum_fusion.refs_0_), channel_id=1, source_target_pairs={{0,4},{4,0},{8,12},{12,8},{16,20},{20,16},{24,28},{28,24},{1,5},{5... | collective-permute-start | bytes 393224 | tf_op jit(solution)/shard_map/ppermute | solution.py:29
  23.5 1.7 %collective-permute-done.5.refs_8_ = bf16[2,16,16,128]{3,2,1,0:T(8,128)(2,1)S(1)} collective-permute-done((bf16[2,16,16,128]{3,2,1,0:T(8,128)(2,1)S(1)}, bf16[2,16,16,128]{3,2,1,0:T(8,128)(2,1)S(1)}, u32[]{:S(2)}, u32[]{:S(2)}) %collective-permute-start.5) | collective-permute-done | bytes 131104 | tf_op jit(solution)/shard_map/ppermute | solution.py:29
  25.1 1.0 %collective-permute-start.6 = (bf16[2,16,16,128]{3,2,1,0:T(8,128)(2,1)S(1)}, bf16[2,16,16,128]{3,2,1,0:T(8,128)(2,1)S(1)}, u32[]{:S(2)}, u32[]{:S(2)}) collective-permute-start(bf16[2,16,16,128]{3,2,1,0:T(8,128)(2,1)S(1)} %pad_maximum_fusion.1.refs_1_), channel_id=1, source_target_pairs={{0,16},{4,20},{8,24},{12,28},{16,0},{20,4},{24,8},{28,12},{1,17},{... | collective-permute-start | bytes 393224 | tf_op jit(solution)/shard_map/ppermute | solution.py:29
  26.2 3.2 %collective-permute-start.11 = (bf16[2,16,16,128]{3,2,1,0:T(8,128)(2,1)S(1)}, bf16[2,16,16,128]{3,2,1,0:T(8,128)(2,1)S(1)}, u32[]{:S(2)}, u32[]{:S(2)}) collective-permute-start(bf16[2,16,16,128]{3,2,1,0:T(8,128)(2,1)S(1)} %pad_maximum_fusion.1.refs_1_), channel_id=1, source_target_pairs={{0,8},{4,12},{8,0},{12,4},{16,24},{20,28},{24,16},{28,20},{1,9},{5... | collective-permute-start | bytes 393224 | tf_op jit(solution)/shard_map/ppermute | solution.py:29
  29.4 1.5 %collective-permute-start.9 = (bf16[2,16,16,128]{3,2,1,0:T(8,128)(2,1)S(1)}, bf16[2,16,16,128]{3,2,1,0:T(8,128)(2,1)S(1)}, u32[]{:S(2)}, u32[]{:S(2)}) collective-permute-start(bf16[2,16,16,128]{3,2,1,0:T(8,128)(2,1)S(1)} %pad_maximum_fusion.1.refs_1_), channel_id=1, source_target_pairs={{0,4},{4,0},{8,12},{12,8},{16,20},{20,16},{24,28},{28,24},{1,5},{5... | collective-permute-start | bytes 393224 | tf_op jit(solution)/shard_map/ppermute | solution.py:29
  30.9 0.5 collective-permute-start.15
  31.5 0.1 collective-permute-start.12
  31.5 2.3 %collective-permute-done.6.refs_9_ = bf16[2,16,16,128]{3,2,1,0:T(8,128)(2,1)S(1)} collective-permute-done((bf16[2,16,16,128]{3,2,1,0:T(8,128)(2,1)S(1)}, bf16[2,16,16,128]{3,2,1,0:T(8,128)(2,1)S(1)}, u32[]{:S(2)}, u32[]{:S(2)}) %collective-permute-start.6) | collective-permute-done | bytes 131104 | tf_op jit(solution)/shard_map/ppermute | solution.py:29
  33.8 0.1 broadcast_select_fusion.1
  33.9 0.6 collective-permute-done.11.refs_5_
  34.5 1.1 %collective-permute-done.9.refs_3_ = bf16[2,16,16,128]{3,2,1,0:T(8,128)(2,1)S(1)} collective-permute-done((bf16[2,16,16,128]{3,2,1,0:T(8,128)(2,1)S(1)}, bf16[2,16,16,128]{3,2,1,0:T(8,128)(2,1)S(1)}, u32[]{:S(2)}, u32[]{:S(2)}) %collective-permute-start.9) | collective-permute-done | bytes 131104 | tf_op jit(solution)/shard_map/ppermute | solution.py:29
  35.6 1.6 %collective-permute-start.16 = (bf16[2,16,16,128]{3,2,1,0:T(8,128)(2,1)S(1)}, bf16[2,16,16,128]{3,2,1,0:T(8,128)(2,1)S(1)}, u32[]{:S(2)}, u32[]{:S(2)}) collective-permute-start(bf16[2,16,16,128]{3,2,1,0:T(8,128)(2,1)S(1)} %collective-permute-done.6.refs_9_), channel_id=1, source_target_pairs={{0,4},{4,0},{8,12},{12,8},{16,20},{20,16},{24,28},{28,24},{1,5},{5... | collective-permute-start | bytes 393224 | tf_op jit(solution)/shard_map/ppermute | solution.py:29
  37.2 0.7 %collective-permute-done.12.refs_12_ = bf16[2,16,16,128]{3,2,1,0:T(8,128)(2,1)S(1)} collective-permute-done((bf16[2,16,16,128]{3,2,1,0:T(8,128)(2,1)S(1)}, bf16[2,16,16,128]{3,2,1,0:T(8,128)(2,1)S(1)}, u32[]{:S(2)}, u32[]{:S(2)}) %collective-permute-start.12) | collective-permute-done | bytes 131104 | tf_op jit(solution)/shard_map/ppermute | solution.py:29
  37.9 0.6 collective-permute-start.13
  38.5 1.5 %collective-permute-start.17 = (bf16[2,16,16,128]{3,2,1,0:T(8,128)(2,1)S(1)}, bf16[2,16,16,128]{3,2,1,0:T(8,128)(2,1)S(1)}, u32[]{:S(2)}, u32[]{:S(2)}) collective-permute-start(bf16[2,16,16,128]{3,2,1,0:T(8,128)(2,1)S(1)} %collective-permute-done.12.refs_12_), channel_id=1, source_target_pairs={{0,4},{4,0},{8,12},{12,8},{16,20},{20,16},{24,28},{28,24},{1,5},{5... | collective-permute-start | bytes 393224 | tf_op jit(solution)/shard_map/ppermute | solution.py:29
  40.1 0.6 collective-permute-done.7.refs_13_
  40.7 0.7 %collective-permute-start.14 = (bf16[2,16,16,128]{3,2,1,0:T(8,128)(2,1)S(1)}, bf16[2,16,16,128]{3,2,1,0:T(8,128)(2,1)S(1)}, u32[]{:S(2)}, u32[]{:S(2)}) collective-permute-start(bf16[2,16,16,128]{3,2,1,0:T(8,128)(2,1)S(1)} %collective-permute-done.9.refs_3_), channel_id=1, source_target_pairs={{0,8},{4,12},{8,0},{12,4},{16,24},{20,28},{24,16},{28,20},{1,9},{5... | collective-permute-start | bytes 393224 | tf_op jit(solution)/shard_map/ppermute | solution.py:29
  41.5 1.2 %collective-permute-start.18 = (bf16[2,16,16,128]{3,2,1,0:T(8,128)(2,1)S(1)}, bf16[2,16,16,128]{3,2,1,0:T(8,128)(2,1)S(1)}, u32[]{:S(2)}, u32[]{:S(2)}) collective-permute-start(bf16[2,16,16,128]{3,2,1,0:T(8,128)(2,1)S(1)} %collective-permute-done.7.refs_13_), channel_id=1, source_target_pairs={{0,4},{4,0},{8,12},{12,8},{16,20},{20,16},{24,28},{28,24},{1,5},{5... | collective-permute-start | bytes 393224 | tf_op jit(solution)/shard_map/ppermute | solution.py:29
  42.8 0.1 reshape.34
  42.9 0.1 reshape.35
  42.9 0.1 pad_add_fusion
  43.0 0.1 reshape.36.order_ref
  43.1 3.4 %stage.1.targets_ref = bf16[2048,2048]{1,0:T(8,128)(2,1)S(1)} custom-call(bf16[2048,2048]{1,0:T(8,128)(2,1)} %targets_hbm.1), custom_call_target="tpu_custom_call" | custom-call | bytes 8388608 | tf_op jit(solution)/shard_map/stage/pallas_call | solution.py:226
  46.5 2.9 %scores_far.1 = (bf16[128,2176]{1,0:T(8,128)(2,1)S(1)}, bf16[128,2176]{1,0:T(8,128)(2,1)S(1)}) custom-call(s32[1,512]{1,0:T(1,128)S(1)} %reshape.36.order_ref, f32[128,128]{1,0:T(8,128)S(1)} %squares.1.squares_ref, bf16[2048,2048]{1,0:T(8,128)(2,1)S(1)} %stage.1.targets_ref, bf16[2,16,16,128]{3,2,1,0:T(8,128)(2,1)S(1)} %pad_maximum_fusion.refs_0_, ...), custom_call_target="tpu_custom_call" | custom-call | flops 2147483648 | bytes 8388608 | tf_op jit(solution)/shard_map/scores_far/pallas_call | solution.py:373
  49.5 1.9 %collective-permute-done.19.came_ref = bf16[128,2176]{1,0:T(8,128)(2,1)S(1)} collective-permute-done((bf16[128,2176]{1,0:T(8,128)(2,1)S(1)}, bf16[128,2176]{1,0:T(8,128)(2,1)S(1)}, u32[]{:S(2)}, u32[]{:S(2)}) %collective-permute-start.19) | collective-permute-done | bytes 557088 | tf_op jit(solution)/shard_map/ppermute | solution.py:29
  51.5 0.1 join.1
  51.6 1.6 %collective-permute-start.22 = (bf16[128,2176]{1,0:T(8,128)(2,1)S(1)}, bf16[128,2176]{1,0:T(8,128)(2,1)S(1)}, u32[]{:S(2)}, u32[]{:S(2)}) collective-permute-start(bf16[128,2176]{1,0:T(8,128)(2,1)S(1)} %join.1), channel_id=1, source_target_pairs={{0,2},{1,3},{2,0},{3,1},{4,6},{5,7},{6,4},{7,5},{8,10},{9,11},{10,... | collective-permute-start | bytes 1671176 | tf_op jit(solution)/shard_map/ppermute | solution.py:29
  53.2 2.9 %scores_near.1 = (bf16[64,2176]{1,0:T(8,128)(2,1)S(1)}, bf16[64,2176]{1,0:T(8,128)(2,1)S(1)}, bf16[128,2176]{1,0:T(8,128)(2,1)S(1)}) custom-call(s32[1,512]{1,0:T(1,128)S(1)} %reshape.36.order_ref, f32[128,128]{1,0:T(8,128)S(1)} %squares.1.squares_ref, bf16[2048,2048]{1,0:T(8,128)(2,1)S(1)} %stage.1.targets_ref, ...), custom_call_target="tpu_custom_call" | custom-call | flops 2147483648 | bytes 8388608 | tf_op jit(solution)/shard_map/scores_near/pallas_call | solution.py:373
  56.2 0.5 collective-permute-start.21
  56.7 1.0 %collective-permute-done.20.low_ref = bf16[64,2176]{1,0:T(8,128)(2,1)S(1)} collective-permute-done((bf16[64,2176]{1,0:T(8,128)(2,1)S(1)}, bf16[64,2176]{1,0:T(8,128)(2,1)S(1)}, u32[]{:S(2)}, u32[]{:S(2)}) %collective-permute-start.20) | collective-permute-done | bytes 278560 | tf_op jit(solution)/shard_map/ppermute | solution.py:29
  57.7 0.4 collective-permute-done.21.high_ref
  58.1 8.2 %collective-permute-done.22.far_ref = bf16[128,2176]{1,0:T(8,128)(2,1)S(1)} collective-permute-done((bf16[128,2176]{1,0:T(8,128)(2,1)S(1)}, bf16[128,2176]{1,0:T(8,128)(2,1)S(1)}, u32[]{:S(2)}, u32[]{:S(2)}) %collective-permute-start.22) | collective-permute-done | bytes 557088 | tf_op jit(solution)/shard_map/ppermute | solution.py:29
  66.4 1.2 %finish.1 = f32[128,2048]{1,0:T(8,128)} custom-call(bf16[128,2176]{1,0:T(8,128)(2,1)S(1)} %get-tuple-element.61.keep_ref, bf16[64,2176]{1,0:T(8,128)(2,1)S(1)} %collective-permute-done.20.low_ref, bf16[64,2176]{1,0:T(8,128)(2,1)S(1)} %collective-permute-done.21.high_ref, bf16[128,2176]{1,0:T(8,128)(2,1)S(1)} %collective-permute-done.22.far_ref), custom_call_target="tpu_custom_call" | custom-call | flops 1048576 | bytes 2621440 | tf_op jit(solution)/shard_map/finish/pallas_call | solution.py:424
  (30 shorter events, 0.6 us)
Async XLA Ops:
  0.0 4.3 %copy-start = (bf16[128,64]{0,1:T(8,128)(2,1)S(1)}, bf16[128,64]{0,1:T(8,128)(2,1)}, u32[]{:S(2)}) copy-start(bf16[128,64]{0,1:T(8,128)(2,1)} %param.12) | copy-start | bytes 49156
  3.7 2.1 %collective-permute-start = (bf16[1536,128]{1,0:T(8,128)(2,1)S(1)}, bf16[1536,128]{1,0:T(8,128)(2,1)S(1)}, u32[]{:S(2)}, u32[]{:S(2)}) collective-permute-start(bf16[1536,128]{1,0:T(8,128)(2,1)S(1)} %get-tuple-element.39), channel_id=1, source_target_pairs={{0,1},{1,0},{2,3},{3,2},{4,5},{5,4},{6,7},{7,6},{8,9},{9,8},{10,11... | collective-permute-start | bytes 1179656 | tf_op jit(solution)/shard_map/ppermute | solution.py:29
  5.9 7.4 %collective-permute-start.1 = (bf16[640,128]{1,0:T(8,128)(2,1)S(1)}, bf16[640,128]{1,0:T(8,128)(2,1)S(1)}, u32[]{:S(2)}, u32[]{:S(2)}) collective-permute-start(bf16[640,128]{1,0:T(8,128)(2,1)S(1)} %get-tuple-element.41), channel_id=1, source_target_pairs={{0,2},{1,3},{2,0},{3,1},{4,6},{5,7},{6,4},{7,5},{8,10},{9,11},{10,... | collective-permute-start | bytes 491528 | tf_op jit(solution)/shard_map/ppermute | solution.py:29
  8.6 4.7 %copy-start.1 = (s32[64]{0:T(128)S(1)}, s32[64]{0:T(128)}, u32[]{:S(2)}) copy-start(s32[64]{0:T(128)} %lengths.3) | copy-start | bytes 772
  8.6 11.0 %copy-start.2 = (s32[512]{0:T(512)S(1)}, s32[512]{0:T(512)}, u32[]{:S(2)}) copy-start(s32[512]{0:T(512)} %param.14) | copy-start | bytes 6148
  12.4 6.2 %collective-permute-start.3 = (bf16[640,128]{1,0:T(8,128)(2,1)S(1)}, bf16[640,128]{1,0:T(8,128)(2,1)S(1)}, u32[]{:S(2)}, u32[]{:S(2)}) collective-permute-start(bf16[640,128]{1,0:T(8,128)(2,1)S(1)} %get-tuple-element.49), channel_id=1, source_target_pairs={{0,2},{1,3},{2,0},{3,1},{4,6},{5,7},{6,4},{7,5},{8,10},{9,11},{10,... | collective-permute-start | bytes 491528 | tf_op jit(solution)/shard_map/ppermute | solution.py:29
  14.2 1.3 %collective-permute-start.2 = (bf16[16,16,128]{2,1,0:T(8,128)(2,1)S(1)}, bf16[16,16,128]{2,1,0:T(8,128)(2,1)S(1)}, u32[]{:S(2)}, u32[]{:S(2)}) collective-permute-start(bf16[16,16,128]{2,1,0:T(8,128)(2,1)S(1)} %get-tuple-element.47), channel_id=1, source_target_pairs={{0,1},{1,0},{2,3},{3,2},{4,5},{5,4},{6,7},{7,6},{8,9},{9,8},{10,11... | collective-permute-start | bytes 196616 | tf_op jit(solution)/shard_map/ppermute | solution.py:29
  15.5 9.6 %collective-permute-start.5 = (bf16[2,16,16,128]{3,2,1,0:T(8,128)(2,1)S(1)}, bf16[2,16,16,128]{3,2,1,0:T(8,128)(2,1)S(1)}, u32[]{:S(2)}, u32[]{:S(2)}) collective-permute-start(bf16[2,16,16,128]{3,2,1,0:T(8,128)(2,1)S(1)} %pad_maximum_fusion.refs_0_), channel_id=1, source_target_pairs={{0,16},{4,20},{8,24},{12,28},{16,0},{20,4},{24,8},{28,12},{1,17},{... | collective-permute-start | bytes 393224 | tf_op jit(solution)/shard_map/ppermute | solution.py:29
  19.5 3.9 %collective-permute-start.4 = (bf16[16,16,128]{2,1,0:T(8,128)(2,1)S(1)}, bf16[16,16,128]{2,1,0:T(8,128)(2,1)S(1)}, u32[]{:S(2)}, u32[]{:S(2)}) collective-permute-start(bf16[16,16,128]{2,1,0:T(8,128)(2,1)S(1)} %get-tuple-element.51), channel_id=1, source_target_pairs={{0,1},{1,0},{2,3},{3,2},{4,5},{5,4},{6,7},{7,6},{8,9},{9,8},{10,11... | collective-permute-start | bytes 196616 | tf_op jit(solution)/shard_map/ppermute | solution.py:29
  20.3 10.7 %collective-permute-start.10 = (bf16[2,16,16,128]{3,2,1,0:T(8,128)(2,1)S(1)}, bf16[2,16,16,128]{3,2,1,0:T(8,128)(2,1)S(1)}, u32[]{:S(2)}, u32[]{:S(2)}) collective-permute-start(bf16[2,16,16,128]{3,2,1,0:T(8,128)(2,1)S(1)} %pad_maximum_fusion.refs_0_), channel_id=1, source_target_pairs={{0,8},{4,12},{8,0},{12,4},{16,24},{20,28},{24,16},{28,20},{1,9},{5... | collective-permute-start | bytes 393224 | tf_op jit(solution)/shard_map/ppermute | solution.py:29
  21.9 9.0 %collective-permute-start.8 = (bf16[2,16,16,128]{3,2,1,0:T(8,128)(2,1)S(1)}, bf16[2,16,16,128]{3,2,1,0:T(8,128)(2,1)S(1)}, u32[]{:S(2)}, u32[]{:S(2)}) collective-permute-start(bf16[2,16,16,128]{3,2,1,0:T(8,128)(2,1)S(1)} %pad_maximum_fusion.refs_0_), channel_id=1, source_target_pairs={{0,4},{4,0},{8,12},{12,8},{16,20},{20,16},{24,28},{28,24},{1,5},{5... | collective-permute-start | bytes 393224 | tf_op jit(solution)/shard_map/ppermute | solution.py:29
  25.1 8.7 %collective-permute-start.6 = (bf16[2,16,16,128]{3,2,1,0:T(8,128)(2,1)S(1)}, bf16[2,16,16,128]{3,2,1,0:T(8,128)(2,1)S(1)}, u32[]{:S(2)}, u32[]{:S(2)}) collective-permute-start(bf16[2,16,16,128]{3,2,1,0:T(8,128)(2,1)S(1)} %pad_maximum_fusion.1.refs_1_), channel_id=1, source_target_pairs={{0,16},{4,20},{8,24},{12,28},{16,0},{20,4},{24,8},{28,12},{1,17},{... | collective-permute-start | bytes 393224 | tf_op jit(solution)/shard_map/ppermute | solution.py:29
  26.2 8.3 %collective-permute-start.11 = (bf16[2,16,16,128]{3,2,1,0:T(8,128)(2,1)S(1)}, bf16[2,16,16,128]{3,2,1,0:T(8,128)(2,1)S(1)}, u32[]{:S(2)}, u32[]{:S(2)}) collective-permute-start(bf16[2,16,16,128]{3,2,1,0:T(8,128)(2,1)S(1)} %pad_maximum_fusion.1.refs_1_), channel_id=1, source_target_pairs={{0,8},{4,12},{8,0},{12,4},{16,24},{20,28},{24,16},{28,20},{1,9},{5... | collective-permute-start | bytes 393224 | tf_op jit(solution)/shard_map/ppermute | solution.py:29
  29.4 6.2 %collective-permute-start.9 = (bf16[2,16,16,128]{3,2,1,0:T(8,128)(2,1)S(1)}, bf16[2,16,16,128]{3,2,1,0:T(8,128)(2,1)S(1)}, u32[]{:S(2)}, u32[]{:S(2)}) collective-permute-start(bf16[2,16,16,128]{3,2,1,0:T(8,128)(2,1)S(1)} %pad_maximum_fusion.1.refs_1_), channel_id=1, source_target_pairs={{0,4},{4,0},{8,12},{12,8},{16,20},{20,16},{24,28},{28,24},{1,5},{5... | collective-permute-start | bytes 393224 | tf_op jit(solution)/shard_map/ppermute | solution.py:29
  30.9 10.5 %collective-permute-start.15 = (bf16[2,16,16,128]{3,2,1,0:T(8,128)(2,1)S(1)}, bf16[2,16,16,128]{3,2,1,0:T(8,128)(2,1)S(1)}, u32[]{:S(2)}, u32[]{:S(2)}) collective-permute-start(bf16[2,16,16,128]{3,2,1,0:T(8,128)(2,1)S(1)} %collective-permute-done.5.refs_8_), channel_id=1, source_target_pairs={{0,4},{4,0},{8,12},{12,8},{16,20},{20,16},{24,28},{28,24},{1,5},{5... | collective-permute-start | bytes 393224 | tf_op jit(solution)/shard_map/ppermute | solution.py:29
  31.5 6.4 %collective-permute-start.12 = (bf16[2,16,16,128]{3,2,1,0:T(8,128)(2,1)S(1)}, bf16[2,16,16,128]{3,2,1,0:T(8,128)(2,1)S(1)}, u32[]{:S(2)}, u32[]{:S(2)}) collective-permute-start(bf16[2,16,16,128]{3,2,1,0:T(8,128)(2,1)S(1)} %collective-permute-done.5.refs_8_), channel_id=1, source_target_pairs={{0,8},{4,12},{8,0},{12,4},{16,24},{20,28},{24,16},{28,20},{1,9},{5... | collective-permute-start | bytes 393224 | tf_op jit(solution)/shard_map/ppermute | solution.py:29
  33.8 6.9 %collective-permute-start.7 = (bf16[2,16,16,128]{3,2,1,0:T(8,128)(2,1)S(1)}, bf16[2,16,16,128]{3,2,1,0:T(8,128)(2,1)S(1)}, u32[]{:S(2)}, u32[]{:S(2)}) collective-permute-start(bf16[2,16,16,128]{3,2,1,0:T(8,128)(2,1)S(1)} %collective-permute-done.6.refs_9_), channel_id=1, source_target_pairs={{0,8},{4,12},{8,0},{12,4},{16,24},{20,28},{24,16},{28,20},{1,9},{5... | collective-permute-start | bytes 393224 | tf_op jit(solution)/shard_map/ppermute | solution.py:29
  35.6 10.9 %collective-permute-start.16 = (bf16[2,16,16,128]{3,2,1,0:T(8,128)(2,1)S(1)}, bf16[2,16,16,128]{3,2,1,0:T(8,128)(2,1)S(1)}, u32[]{:S(2)}, u32[]{:S(2)}) collective-permute-start(bf16[2,16,16,128]{3,2,1,0:T(8,128)(2,1)S(1)} %collective-permute-done.6.refs_9_), channel_id=1, source_target_pairs={{0,4},{4,0},{8,12},{12,8},{16,20},{20,16},{24,28},{28,24},{1,5},{5... | collective-permute-start | bytes 393224 | tf_op jit(solution)/shard_map/ppermute | solution.py:29
  37.9 8.6 %collective-permute-start.13 = (bf16[2,16,16,128]{3,2,1,0:T(8,128)(2,1)S(1)}, bf16[2,16,16,128]{3,2,1,0:T(8,128)(2,1)S(1)}, u32[]{:S(2)}, u32[]{:S(2)}) collective-permute-start(bf16[2,16,16,128]{3,2,1,0:T(8,128)(2,1)S(1)} %collective-permute-done.8.refs_2_), channel_id=1, source_target_pairs={{0,8},{4,12},{8,0},{12,4},{16,24},{20,28},{24,16},{28,20},{1,9},{5... | collective-permute-start | bytes 393224 | tf_op jit(solution)/shard_map/ppermute | solution.py:29
  38.5 8.0 %collective-permute-start.17 = (bf16[2,16,16,128]{3,2,1,0:T(8,128)(2,1)S(1)}, bf16[2,16,16,128]{3,2,1,0:T(8,128)(2,1)S(1)}, u32[]{:S(2)}, u32[]{:S(2)}) collective-permute-start(bf16[2,16,16,128]{3,2,1,0:T(8,128)(2,1)S(1)} %collective-permute-done.12.refs_12_), channel_id=1, source_target_pairs={{0,4},{4,0},{8,12},{12,8},{16,20},{20,16},{24,28},{28,24},{1,5},{5... | collective-permute-start | bytes 393224 | tf_op jit(solution)/shard_map/ppermute | solution.py:29
  40.7 5.8 %collective-permute-start.14 = (bf16[2,16,16,128]{3,2,1,0:T(8,128)(2,1)S(1)}, bf16[2,16,16,128]{3,2,1,0:T(8,128)(2,1)S(1)}, u32[]{:S(2)}, u32[]{:S(2)}) collective-permute-start(bf16[2,16,16,128]{3,2,1,0:T(8,128)(2,1)S(1)} %collective-permute-done.9.refs_3_), channel_id=1, source_target_pairs={{0,8},{4,12},{8,0},{12,4},{16,24},{20,28},{24,16},{28,20},{1,9},{5... | collective-permute-start | bytes 393224 | tf_op jit(solution)/shard_map/ppermute | solution.py:29
  41.5 5.1 %collective-permute-start.18 = (bf16[2,16,16,128]{3,2,1,0:T(8,128)(2,1)S(1)}, bf16[2,16,16,128]{3,2,1,0:T(8,128)(2,1)S(1)}, u32[]{:S(2)}, u32[]{:S(2)}) collective-permute-start(bf16[2,16,16,128]{3,2,1,0:T(8,128)(2,1)S(1)} %collective-permute-done.7.refs_13_), channel_id=1, source_target_pairs={{0,4},{4,0},{8,12},{12,8},{16,20},{20,16},{24,28},{28,24},{1,5},{5... | collective-permute-start | bytes 393224 | tf_op jit(solution)/shard_map/ppermute | solution.py:29
  49.5 2.0 %collective-permute-start.19 = (bf16[128,2176]{1,0:T(8,128)(2,1)S(1)}, bf16[128,2176]{1,0:T(8,128)(2,1)S(1)}, u32[]{:S(2)}, u32[]{:S(2)}) collective-permute-start(bf16[128,2176]{1,0:T(8,128)(2,1)S(1)} %get-tuple-element.59), channel_id=1, source_target_pairs={{0,1},{1,0},{2,3},{3,2},{4,5},{5,4},{6,7},{7,6},{8,9},{9,8},{10,11... | collective-permute-start | bytes 1671176 | tf_op jit(solution)/shard_map/ppermute | solution.py:29
  51.6 14.7 %collective-permute-start.22 = (bf16[128,2176]{1,0:T(8,128)(2,1)S(1)}, bf16[128,2176]{1,0:T(8,128)(2,1)S(1)}, u32[]{:S(2)}, u32[]{:S(2)}) collective-permute-start(bf16[128,2176]{1,0:T(8,128)(2,1)S(1)} %join.1), channel_id=1, source_target_pairs={{0,2},{1,3},{2,0},{3,1},{4,6},{5,7},{6,4},{7,5},{8,10},{9,11},{10,... | collective-permute-start | bytes 1671176 | tf_op jit(solution)/shard_map/ppermute | solution.py:29
  56.1 1.6 %collective-permute-start.20 = (bf16[64,2176]{1,0:T(8,128)(2,1)S(1)}, bf16[64,2176]{1,0:T(8,128)(2,1)S(1)}, u32[]{:S(2)}, u32[]{:S(2)}) collective-permute-start(bf16[64,2176]{1,0:T(8,128)(2,1)S(1)} %get-tuple-element.62), channel_id=1, source_target_pairs={{0,1},{1,0},{2,3},{3,2},{4,5},{5,4},{6,7},{7,6},{8,9},{9,8},{10,11... | collective-permute-start | bytes 835592 | tf_op jit(solution)/shard_map/ppermute | solution.py:29
  56.2 1.9 %collective-permute-start.21 = (bf16[64,2176]{1,0:T(8,128)(2,1)S(1)}, bf16[64,2176]{1,0:T(8,128)(2,1)S(1)}, u32[]{:S(2)}, u32[]{:S(2)}) collective-permute-start(bf16[64,2176]{1,0:T(8,128)(2,1)S(1)} %get-tuple-element.63), channel_id=1, source_target_pairs={{0,1},{1,0},{2,3},{3,2},{4,5},{5,4},{6,7},{7,6},{8,9},{9,8},{10,11... | collective-permute-start | bytes 835592 | tf_op jit(solution)/shard_map/ppermute | solution.py:29

commit v7 on v6

--- a/solution.py
+++ b/solution.py
@@ -49,7 +49,9 @@
         across.append(exchange(far[1], "wide", 2))
         far_beside.append(exchange(after(far[1], beside[1], above[1]), "wide", 1))
         across_beside = [exchange(chunk, "wide", 1) for chunk in across]
-        above_beside = [exchange(after(beside[0], across[0]), "wide", 2), exchange(after(beside[1], across[1]), "wide", 2)]
+        above_beside = [
+            exchange(after(chunk, there), "wide", 2) for chunk, there in zip(beside, (far[1], across[0]))
+        ]
         return blocks, beside, above, above_beside, far, far_beside, across, across_beside
     held = {0: blocks}
     bit = count // 2

time: 67.7 us -> 67.3 us (level)
  no operation moved by 1% of the time
where the time goes in v7:
time: 67.3 us; the launch traced here: 67.1 us
  starting transfers between devices  23.6 us (35%)
  Pallas kernels  21.4 us (32%)
  waiting for transfers between devices  20.7 us (31%)
  local copies, waits for them, and re-layouts  1.01 us (2%)
    ppermute x23, starting transfers between devices, exchange(): return lax.ppermute(array, axis, [(i, i ^ bit) for i in range(count)])  23.6 us
    ppermute x23, waiting for transfers between devices, exchange(): return lax.ppermute(array, axis, [(i, i ^ bit) for i in range(count)])  20.7 us
    pallas_call x2, Pallas kernels, partial_scores(): pl.pallas_call(functools.partial(score_kernel, len(pieces), far), in_spec...  5.83 us
    pallas_call x1, Pallas kernels, column_squares(): pl.pallas_call(square_kernel, in_specs=[pl.BlockSpec(memory_space=pltpu.H...  3.77 us
    pallas_call x1, Pallas kernels, project_send(): pl.pallas_call(project_send_kernel, in_specs=[pl.BlockSpec(memory_space=p...  3.74 us
    pallas_call x1, Pallas kernels, stage(): pl.pallas_call(stage_kernel, in_specs=[pl.BlockSpec(memory_space=pltpu.HB...  3.39 us
    pallas_call x2, Pallas kernels, make_features(): pl.pallas_call(functools.partial(feature_kernel, first, core_programs, pr...  1.63 us
    pallas_call x1, Pallas kernels, project_keep(): pl.pallas_call(project_keep_kernel, in_specs=[vmem] * 5, out_specs=vmem,...  1.56 us
  transfers between devices with their start and end apart: 23, of which 13 were waited for; matrix products, arithmetic and copies ran while one was open for 2% of the time, Pallas kernels for 20%

profile of v7, /device:TPU:0, one launch (start us, length us, event | category | flops | bytes accessed | tf_op | source)
XLA Modules:
  0.0 67.1 jit_solution(931470266986817375)
XLA Ops:
  0.0 3.7 %project_send.1 = (bf16[1536,128]{1,0:T(8,128)(2,1)S(1)}, bf16[1024,1024]{1,0:T(8,128)(2,1)S(1)}, bf16[1024,1024]{1,0:T(8,128)(2,1)S(1)}, bf16[1024,128]{1,0:T(8,128)(2,1)S(1)}, bf16[1024,128]{1,0:T(8,128)(2,1)S(1)}) custom-call(bf16[2048,1024]{1,0:T(8,128)(2,1)} %x_hbm.1, bf16[2048,1024]{1,0:T(8,128)(2,1)} %g_hbm.1, bf16[1024,128]{1,0:T(8,128)(2,1)} %w_hbm.1, ...), custom_call_target="tpu_custom_call" | custom-call | flops 536870912 | bytes 8388608 | tf_op jit(solution)/shard_map/project_send/pallas_call | solution.py:144
  3.7 0.5 collective-permute-start
  4.3 1.6 %project_keep.1.keep_ref = f32[1536,128]{1,0:T(8,128)S(1)} custom-call(bf16[1024,1024]{1,0:T(8,128)(2,1)S(1)} %get-tuple-element.35.x, bf16[1024,1024]{1,0:T(8,128)(2,1)S(1)} %get-tuple-element.36.g, bf16[1024,128]{1,0:T(8,128)(2,1)S(1)} %get-tuple-element.37.w, bf16[1024,128]{1,0:T(8,128)(2,1)S(1)} %get-tuple-element.38.up, bf16[64,128]{1,0:T(8,128)(2,1)S(1)} %bitcast.8), custom_call_target="tpu_custom_call" | custom-call | flops 536870912 | bytes 4194304 | tf_op jit(solution)/shard_map/project_keep/pallas_call | solution.py:171
  5.9 2.7 %collective-permute-start.1 = (bf16[640,128]{1,0:T(8,128)(2,1)S(1)}, bf16[640,128]{1,0:T(8,128)(2,1)S(1)}, u32[]{:S(2)}, u32[]{:S(2)}) collective-permute-start(bf16[640,128]{1,0:T(8,128)(2,1)S(1)} %get-tuple-element.41), channel_id=1, source_target_pairs={{0,2},{1,3},{2,0},{3,1},{4,6},{5,7},{6,4},{7,5},{8,10},{9,11},{10,... | collective-permute-start | bytes 491528 | tf_op jit(solution)/shard_map/ppermute | solution.py:29
  8.6 3.8 %squares.1.squares_ref = f32[128,128]{1,0:T(8,128)S(1)} custom-call(bf16[2048,2048]{1,0:T(8,128)(2,1)} %targets_hbm.1), custom_call_target="tpu_custom_call" | custom-call | flops 8388608 | bytes 8388608 | tf_op jit(solution)/shard_map/squares/pallas_call | solution.py:206
  12.4 0.1 collective-permute-start.3
  12.5 0.8 %collective-permute-done.1.came_ref = bf16[640,128]{1,0:T(8,128)(2,1)S(1)} collective-permute-done((bf16[640,128]{1,0:T(8,128)(2,1)S(1)}, bf16[640,128]{1,0:T(8,128)(2,1)S(1)}, u32[]{:S(2)}, u32[]{:S(2)}) %collective-permute-start.1) | collective-permute-done | bytes 163872 | tf_op jit(solution)/shard_map/ppermute | solution.py:29
  13.4 0.8 %features.2 = (bf16[16,16,128]{2,1,0:T(8,128)(2,1)S(1)}, bf16[16,16,128]{2,1,0:T(8,128)(2,1)S(1)}) custom-call(s32[64]{0:T(128)S(1)} %copy-done.1, f32[640,128]{1,0:T(8,128)S(1)} %get-tuple-element.45.left_ref, bf16[640,128]{1,0:T(8,128)(2,1)S(1)} %collective-permute-done.1.came_ref), custom_call_target="tpu_custom_call" | custom-call | flops 100000000 | bytes 655360 | tf_op jit(solution)/shard_map/features/pallas_call | solution.py:311
  14.3 1.2 %collective-permute-done.2 = bf16[16,16,128]{2,1,0:T(8,128)(2,1)S(1)} collective-permute-done((bf16[16,16,128]{2,1,0:T(8,128)(2,1)S(1)}, bf16[16,16,128]{2,1,0:T(8,128)(2,1)S(1)}, u32[]{:S(2)}, u32[]{:S(2)}) %collective-permute-start.2) | collective-permute-done | bytes 65568 | tf_op jit(solution)/shard_map/ppermute | solution.py:29
  15.5 2.9 %collective-permute-start.5 = (bf16[2,16,16,128]{3,2,1,0:T(8,128)(2,1)S(1)}, bf16[2,16,16,128]{3,2,1,0:T(8,128)(2,1)S(1)}, u32[]{:S(2)}, u32[]{:S(2)}) collective-permute-start(bf16[2,16,16,128]{3,2,1,0:T(8,128)(2,1)S(1)} %pad_maximum_fusion.refs_0_), channel_id=1, source_target_pairs={{0,16},{4,20},{8,24},{12,28},{16,0},{20,4},{24,8},{28,12},{1,17},{... | collective-permute-start | bytes 393224 | tf_op jit(solution)/shard_map/ppermute | solution.py:29
  18.4 0.3 collective-permute-done.3.came_ref
  18.7 0.8 %features.3 = (bf16[16,16,128]{2,1,0:T(8,128)(2,1)S(1)}, bf16[16,16,128]{2,1,0:T(8,128)(2,1)S(1)}) custom-call(s32[64]{0:T(128)S(1)} %copy-done.1, f32[640,128]{1,0:T(8,128)S(1)} %get-tuple-element.48.left_ref, bf16[640,128]{1,0:T(8,128)(2,1)S(1)} %collective-permute-done.3.came_ref), custom_call_target="tpu_custom_call" | custom-call | flops 100000000 | bytes 655360 | tf_op jit(solution)/shard_map/features/pallas_call | solution.py:311
  19.6 0.1 reshape.33
  19.7 0.6 gather_fusion
  20.3 1.6 %collective-permute-start.10 = (bf16[2,16,16,128]{3,2,1,0:T(8,128)(2,1)S(1)}, bf16[2,16,16,128]{3,2,1,0:T(8,128)(2,1)S(1)}, u32[]{:S(2)}, u32[]{:S(2)}) collective-permute-start(bf16[2,16,16,128]{3,2,1,0:T(8,128)(2,1)S(1)} %pad_maximum_fusion.refs_0_), channel_id=1, source_target_pairs={{0,8},{4,12},{8,0},{12,4},{16,24},{20,28},{24,16},{28,20},{1,9},{5... | collective-permute-start | bytes 393224 | tf_op jit(solution)/shard_map/ppermute | solution.py:29
  21.9 1.5 %collective-permute-start.8 = (bf16[2,16,16,128]{3,2,1,0:T(8,128)(2,1)S(1)}, bf16[2,16,16,128]{3,2,1,0:T(8,128)(2,1)S(1)}, u32[]{:S(2)}, u32[]{:S(2)}) collective-permute-start(bf16[2,16,16,128]{3,2,1,0:T(8,128)(2,1)S(1)} %pad_maximum_fusion.refs_0_), channel_id=1, source_target_pairs={{0,4},{4,0},{8,12},{12,8},{16,20},{20,16},{24,28},{28,24},{1,5},{5... | collective-permute-start | bytes 393224 | tf_op jit(solution)/shard_map/ppermute | solution.py:29
  23.5 1.7 %collective-permute-done.5.refs_8_ = bf16[2,16,16,128]{3,2,1,0:T(8,128)(2,1)S(1)} collective-permute-done((bf16[2,16,16,128]{3,2,1,0:T(8,128)(2,1)S(1)}, bf16[2,16,16,128]{3,2,1,0:T(8,128)(2,1)S(1)}, u32[]{:S(2)}, u32[]{:S(2)}) %collective-permute-start.5) | collective-permute-done | bytes 131104 | tf_op jit(solution)/shard_map/ppermute | solution.py:29
  25.1 1.0 %collective-permute-start.6 = (bf16[2,16,16,128]{3,2,1,0:T(8,128)(2,1)S(1)}, bf16[2,16,16,128]{3,2,1,0:T(8,128)(2,1)S(1)}, u32[]{:S(2)}, u32[]{:S(2)}) collective-permute-start(bf16[2,16,16,128]{3,2,1,0:T(8,128)(2,1)S(1)} %pad_maximum_fusion.1.refs_1_), channel_id=1, source_target_pairs={{0,16},{4,20},{8,24},{12,28},{16,0},{20,4},{24,8},{28,12},{1,17},{... | collective-permute-start | bytes 393224 | tf_op jit(solution)/shard_map/ppermute | solution.py:29
  26.2 3.2 %collective-permute-start.11 = (bf16[2,16,16,128]{3,2,1,0:T(8,128)(2,1)S(1)}, bf16[2,16,16,128]{3,2,1,0:T(8,128)(2,1)S(1)}, u32[]{:S(2)}, u32[]{:S(2)}) collective-permute-start(bf16[2,16,16,128]{3,2,1,0:T(8,128)(2,1)S(1)} %pad_maximum_fusion.1.refs_1_), channel_id=1, source_target_pairs={{0,8},{4,12},{8,0},{12,4},{16,24},{20,28},{24,16},{28,20},{1,9},{5... | collective-permute-start | bytes 393224 | tf_op jit(solution)/shard_map/ppermute | solution.py:29
  29.4 1.5 %collective-permute-start.9 = (bf16[2,16,16,128]{3,2,1,0:T(8,128)(2,1)S(1)}, bf16[2,16,16,128]{3,2,1,0:T(8,128)(2,1)S(1)}, u32[]{:S(2)}, u32[]{:S(2)}) collective-permute-start(bf16[2,16,16,128]{3,2,1,0:T(8,128)(2,1)S(1)} %pad_maximum_fusion.1.refs_1_), channel_id=1, source_target_pairs={{0,4},{4,0},{8,12},{12,8},{16,20},{20,16},{24,28},{28,24},{1,5},{5... | collective-permute-start | bytes 393224 | tf_op jit(solution)/shard_map/ppermute | solution.py:29
  30.9 0.5 collective-permute-start.15
  31.5 0.1 collective-permute-start.13
  31.5 2.3 %collective-permute-done.6.refs_9_ = bf16[2,16,16,128]{3,2,1,0:T(8,128)(2,1)S(1)} collective-permute-done((bf16[2,16,16,128]{3,2,1,0:T(8,128)(2,1)S(1)}, bf16[2,16,16,128]{3,2,1,0:T(8,128)(2,1)S(1)}, u32[]{:S(2)}, u32[]{:S(2)}) %collective-permute-start.6) | collective-permute-done | bytes 131104 | tf_op jit(solution)/shard_map/ppermute | solution.py:29
  33.8 0.1 broadcast_select_fusion.1
  33.9 0.6 collective-permute-done.11.refs_5_
  34.5 1.1 %collective-permute-done.9.refs_3_ = bf16[2,16,16,128]{3,2,1,0:T(8,128)(2,1)S(1)} collective-permute-done((bf16[2,16,16,128]{3,2,1,0:T(8,128)(2,1)S(1)}, bf16[2,16,16,128]{3,2,1,0:T(8,128)(2,1)S(1)}, u32[]{:S(2)}, u32[]{:S(2)}) %collective-permute-start.9) | collective-permute-done | bytes 131104 | tf_op jit(solution)/shard_map/ppermute | solution.py:29
  35.6 0.4 collective-permute-start.12
  36.0 1.5 %collective-permute-start.16 = (bf16[2,16,16,128]{3,2,1,0:T(8,128)(2,1)S(1)}, bf16[2,16,16,128]{3,2,1,0:T(8,128)(2,1)S(1)}, u32[]{:S(2)}, u32[]{:S(2)}) collective-permute-start(bf16[2,16,16,128]{3,2,1,0:T(8,128)(2,1)S(1)} %collective-permute-done.6.refs_9_), channel_id=1, source_target_pairs={{0,4},{4,0},{8,12},{12,8},{16,20},{20,16},{24,28},{28,24},{1,5},{5... | collective-permute-start | bytes 393224 | tf_op jit(solution)/shard_map/ppermute | solution.py:29
  37.5 0.4 collective-permute-done.13.refs_12_
  37.9 1.3 %collective-permute-start.14 = (bf16[2,16,16,128]{3,2,1,0:T(8,128)(2,1)S(1)}, bf16[2,16,16,128]{3,2,1,0:T(8,128)(2,1)S(1)}, u32[]{:S(2)}, u32[]{:S(2)}) collective-permute-start(bf16[2,16,16,128]{3,2,1,0:T(8,128)(2,1)S(1)} %collective-permute-done.9.refs_3_), channel_id=1, source_target_pairs={{0,8},{4,12},{8,0},{12,4},{16,24},{20,28},{24,16},{28,20},{1,9},{5... | collective-permute-start | bytes 393224 | tf_op jit(solution)/shard_map/ppermute | solution.py:29
  39.2 0.9 %collective-permute-start.17 = (bf16[2,16,16,128]{3,2,1,0:T(8,128)(2,1)S(1)}, bf16[2,16,16,128]{3,2,1,0:T(8,128)(2,1)S(1)}, u32[]{:S(2)}, u32[]{:S(2)}) collective-permute-start(bf16[2,16,16,128]{3,2,1,0:T(8,128)(2,1)S(1)} %collective-permute-done.13.refs_12_), channel_id=1, source_target_pairs={{0,4},{4,0},{8,12},{12,8},{16,20},{20,16},{24,28},{28,24},{1,5},{5... | collective-permute-start | bytes 393224 | tf_op jit(solution)/shard_map/ppermute | solution.py:29
  40.1 0.6 collective-permute-done.7.refs_13_
  40.7 1.5 %collective-permute-start.18 = (bf16[2,16,16,128]{3,2,1,0:T(8,128)(2,1)S(1)}, bf16[2,16,16,128]{3,2,1,0:T(8,128)(2,1)S(1)}, u32[]{:S(2)}, u32[]{:S(2)}) collective-permute-start(bf16[2,16,16,128]{3,2,1,0:T(8,128)(2,1)S(1)} %collective-permute-done.7.refs_13_), channel_id=1, source_target_pairs={{0,4},{4,0},{8,12},{12,8},{16,20},{20,16},{24,28},{28,24},{1,5},{5... | collective-permute-start | bytes 393224 | tf_op jit(solution)/shard_map/ppermute | solution.py:29
  42.3 0.1 reshape.34
  42.4 0.1 reshape.35
  42.5 0.1 pad_add_fusion
  42.5 0.1 reshape.36.order_ref
  42.6 3.4 %stage.1.targets_ref = bf16[2048,2048]{1,0:T(8,128)(2,1)S(1)} custom-call(bf16[2048,2048]{1,0:T(8,128)(2,1)} %targets_hbm.1), custom_call_target="tpu_custom_call" | custom-call | bytes 8388608 | tf_op jit(solution)/shard_map/stage/pallas_call | solution.py:228
  46.1 2.9 %scores_far.1 = (bf16[128,2176]{1,0:T(8,128)(2,1)S(1)}, bf16[128,2176]{1,0:T(8,128)(2,1)S(1)}) custom-call(s32[1,512]{1,0:T(1,128)S(1)} %reshape.36.order_ref, f32[128,128]{1,0:T(8,128)S(1)} %squares.1.squares_ref, bf16[2048,2048]{1,0:T(8,128)(2,1)S(1)} %stage.1.targets_ref, bf16[2,16,16,128]{3,2,1,0:T(8,128)(2,1)S(1)} %pad_maximum_fusion.refs_0_, ...), custom_call_target="tpu_custom_call" | custom-call | flops 2147483648 | bytes 8388608 | tf_op jit(solution)/shard_map/scores_far/pallas_call | solution.py:375
  49.1 1.9 %collective-permute-done.19.came_ref = bf16[128,2176]{1,0:T(8,128)(2,1)S(1)} collective-permute-done((bf16[128,2176]{1,0:T(8,128)(2,1)S(1)}, bf16[128,2176]{1,0:T(8,128)(2,1)S(1)}, u32[]{:S(2)}, u32[]{:S(2)}) %collective-permute-start.19) | collective-permute-done | bytes 557088 | tf_op jit(solution)/shard_map/ppermute | solution.py:29
  51.0 0.1 join.1
  51.2 1.6 %collective-permute-start.22 = (bf16[128,2176]{1,0:T(8,128)(2,1)S(1)}, bf16[128,2176]{1,0:T(8,128)(2,1)S(1)}, u32[]{:S(2)}, u32[]{:S(2)}) collective-permute-start(bf16[128,2176]{1,0:T(8,128)(2,1)S(1)} %join.1), channel_id=1, source_target_pairs={{0,2},{1,3},{2,0},{3,1},{4,6},{5,7},{6,4},{7,5},{8,10},{9,11},{10,... | collective-permute-start | bytes 1671176 | tf_op jit(solution)/shard_map/ppermute | solution.py:29
  52.7 2.9 %scores_near.1 = (bf16[64,2176]{1,0:T(8,128)(2,1)S(1)}, bf16[64,2176]{1,0:T(8,128)(2,1)S(1)}, bf16[128,2176]{1,0:T(8,128)(2,1)S(1)}) custom-call(s32[1,512]{1,0:T(1,128)S(1)} %reshape.36.order_ref, f32[128,128]{1,0:T(8,128)S(1)} %squares.1.squares_ref, bf16[2048,2048]{1,0:T(8,128)(2,1)S(1)} %stage.1.targets_ref, ...), custom_call_target="tpu_custom_call" | custom-call | flops 2147483648 | bytes 8388608 | tf_op jit(solution)/shard_map/scores_near/pallas_call | solution.py:375
  55.7 0.5 collective-permute-start.21
  56.2 1.0 %collective-permute-done.20.low_ref = bf16[64,2176]{1,0:T(8,128)(2,1)S(1)} collective-permute-done((bf16[64,2176]{1,0:T(8,128)(2,1)S(1)}, bf16[64,2176]{1,0:T(8,128)(2,1)S(1)}, u32[]{:S(2)}, u32[]{:S(2)}) %collective-permute-start.20) | collective-permute-done | bytes 278560 | tf_op jit(solution)/shard_map/ppermute | solution.py:29
  57.3 0.4 collective-permute-done.21.high_ref
  57.7 8.2 %collective-permute-done.22.far_ref = bf16[128,2176]{1,0:T(8,128)(2,1)S(1)} collective-permute-done((bf16[128,2176]{1,0:T(8,128)(2,1)S(1)}, bf16[128,2176]{1,0:T(8,128)(2,1)S(1)}, u32[]{:S(2)}, u32[]{:S(2)}) %collective-permute-start.22) | collective-permute-done | bytes 557088 | tf_op jit(solution)/shard_map/ppermute | solution.py:29
  65.9 1.2 %finish.1 = f32[128,2048]{1,0:T(8,128)} custom-call(bf16[128,2176]{1,0:T(8,128)(2,1)S(1)} %get-tuple-element.61.keep_ref, bf16[64,2176]{1,0:T(8,128)(2,1)S(1)} %collective-permute-done.20.low_ref, bf16[64,2176]{1,0:T(8,128)(2,1)S(1)} %collective-permute-done.21.high_ref, bf16[128,2176]{1,0:T(8,128)(2,1)S(1)} %collective-permute-done.22.far_ref), custom_call_target="tpu_custom_call" | custom-call | flops 1048576 | bytes 2621440 | tf_op jit(solution)/shard_map/finish/pallas_call | solution.py:426
  (30 shorter events, 0.6 us)
Async XLA Ops:
  0.0 4.3 %copy-start = (bf16[128,64]{0,1:T(8,128)(2,1)S(1)}, bf16[128,64]{0,1:T(8,128)(2,1)}, u32[]{:S(2)}) copy-start(bf16[128,64]{0,1:T(8,128)(2,1)} %param.12) | copy-start | bytes 49156
  3.7 2.1 %collective-permute-start = (bf16[1536,128]{1,0:T(8,128)(2,1)S(1)}, bf16[1536,128]{1,0:T(8,128)(2,1)S(1)}, u32[]{:S(2)}, u32[]{:S(2)}) collective-permute-start(bf16[1536,128]{1,0:T(8,128)(2,1)S(1)} %get-tuple-element.39), channel_id=1, source_target_pairs={{0,1},{1,0},{2,3},{3,2},{4,5},{5,4},{6,7},{7,6},{8,9},{9,8},{10,11... | collective-permute-start | bytes 1179656 | tf_op jit(solution)/shard_map/ppermute | solution.py:29
  5.9 7.4 %collective-permute-start.1 = (bf16[640,128]{1,0:T(8,128)(2,1)S(1)}, bf16[640,128]{1,0:T(8,128)(2,1)S(1)}, u32[]{:S(2)}, u32[]{:S(2)}) collective-permute-start(bf16[640,128]{1,0:T(8,128)(2,1)S(1)} %get-tuple-element.41), channel_id=1, source_target_pairs={{0,2},{1,3},{2,0},{3,1},{4,6},{5,7},{6,4},{7,5},{8,10},{9,11},{10,... | collective-permute-start | bytes 491528 | tf_op jit(solution)/shard_map/ppermute | solution.py:29
  8.6 4.7 %copy-start.1 = (s32[64]{0:T(128)S(1)}, s32[64]{0:T(128)}, u32[]{:S(2)}) copy-start(s32[64]{0:T(128)} %lengths.3) | copy-start | bytes 772
  8.6 11.0 %copy-start.2 = (s32[512]{0:T(512)S(1)}, s32[512]{0:T(512)}, u32[]{:S(2)}) copy-start(s32[512]{0:T(512)} %param.14) | copy-start | bytes 6148
  12.4 6.2 %collective-permute-start.3 = (bf16[640,128]{1,0:T(8,128)(2,1)S(1)}, bf16[640,128]{1,0:T(8,128)(2,1)S(1)}, u32[]{:S(2)}, u32[]{:S(2)}) collective-permute-start(bf16[640,128]{1,0:T(8,128)(2,1)S(1)} %get-tuple-element.49), channel_id=1, source_target_pairs={{0,2},{1,3},{2,0},{3,1},{4,6},{5,7},{6,4},{7,5},{8,10},{9,11},{10,... | collective-permute-start | bytes 491528 | tf_op jit(solution)/shard_map/ppermute | solution.py:29
  14.2 1.3 %collective-permute-start.2 = (bf16[16,16,128]{2,1,0:T(8,128)(2,1)S(1)}, bf16[16,16,128]{2,1,0:T(8,128)(2,1)S(1)}, u32[]{:S(2)}, u32[]{:S(2)}) collective-permute-start(bf16[16,16,128]{2,1,0:T(8,128)(2,1)S(1)} %get-tuple-element.47), channel_id=1, source_target_pairs={{0,1},{1,0},{2,3},{3,2},{4,5},{5,4},{6,7},{7,6},{8,9},{9,8},{10,11... | collective-permute-start | bytes 196616 | tf_op jit(solution)/shard_map/ppermute | solution.py:29
  15.5 9.6 %collective-permute-start.5 = (bf16[2,16,16,128]{3,2,1,0:T(8,128)(2,1)S(1)}, bf16[2,16,16,128]{3,2,1,0:T(8,128)(2,1)S(1)}, u32[]{:S(2)}, u32[]{:S(2)}) collective-permute-start(bf16[2,16,16,128]{3,2,1,0:T(8,128)(2,1)S(1)} %pad_maximum_fusion.refs_0_), channel_id=1, source_target_pairs={{0,16},{4,20},{8,24},{12,28},{16,0},{20,4},{24,8},{28,12},{1,17},{... | collective-permute-start | bytes 393224 | tf_op jit(solution)/shard_map/ppermute | solution.py:29
  19.5 3.9 %collective-permute-start.4 = (bf16[16,16,128]{2,1,0:T(8,128)(2,1)S(1)}, bf16[16,16,128]{2,1,0:T(8,128)(2,1)S(1)}, u32[]{:S(2)}, u32[]{:S(2)}) collective-permute-start(bf16[16,16,128]{2,1,0:T(8,128)(2,1)S(1)} %get-tuple-element.51), channel_id=1, source_target_pairs={{0,1},{1,0},{2,3},{3,2},{4,5},{5,4},{6,7},{7,6},{8,9},{9,8},{10,11... | collective-permute-start | bytes 196616 | tf_op jit(solution)/shard_map/ppermute | solution.py:29
  20.3 10.7 %collective-permute-start.10 = (bf16[2,16,16,128]{3,2,1,0:T(8,128)(2,1)S(1)}, bf16[2,16,16,128]{3,2,1,0:T(8,128)(2,1)S(1)}, u32[]{:S(2)}, u32[]{:S(2)}) collective-permute-start(bf16[2,16,16,128]{3,2,1,0:T(8,128)(2,1)S(1)} %pad_maximum_fusion.refs_0_), channel_id=1, source_target_pairs={{0,8},{4,12},{8,0},{12,4},{16,24},{20,28},{24,16},{28,20},{1,9},{5... | collective-permute-start | bytes 393224 | tf_op jit(solution)/shard_map/ppermute | solution.py:29
  21.9 9.0 %collective-permute-start.8 = (bf16[2,16,16,128]{3,2,1,0:T(8,128)(2,1)S(1)}, bf16[2,16,16,128]{3,2,1,0:T(8,128)(2,1)S(1)}, u32[]{:S(2)}, u32[]{:S(2)}) collective-permute-start(bf16[2,16,16,128]{3,2,1,0:T(8,128)(2,1)S(1)} %pad_maximum_fusion.refs_0_), channel_id=1, source_target_pairs={{0,4},{4,0},{8,12},{12,8},{16,20},{20,16},{24,28},{28,24},{1,5},{5... | collective-permute-start | bytes 393224 | tf_op jit(solution)/shard_map/ppermute | solution.py:29
  25.1 8.7 %collective-permute-start.6 = (bf16[2,16,16,128]{3,2,1,0:T(8,128)(2,1)S(1)}, bf16[2,16,16,128]{3,2,1,0:T(8,128)(2,1)S(1)}, u32[]{:S(2)}, u32[]{:S(2)}) collective-permute-start(bf16[2,16,16,128]{3,2,1,0:T(8,128)(2,1)S(1)} %pad_maximum_fusion.1.refs_1_), channel_id=1, source_target_pairs={{0,16},{4,20},{8,24},{12,28},{16,0},{20,4},{24,8},{28,12},{1,17},{... | collective-permute-start | bytes 393224 | tf_op jit(solution)/shard_map/ppermute | solution.py:29
  26.2 8.3 %collective-permute-start.11 = (bf16[2,16,16,128]{3,2,1,0:T(8,128)(2,1)S(1)}, bf16[2,16,16,128]{3,2,1,0:T(8,128)(2,1)S(1)}, u32[]{:S(2)}, u32[]{:S(2)}) collective-permute-start(bf16[2,16,16,128]{3,2,1,0:T(8,128)(2,1)S(1)} %pad_maximum_fusion.1.refs_1_), channel_id=1, source_target_pairs={{0,8},{4,12},{8,0},{12,4},{16,24},{20,28},{24,16},{28,20},{1,9},{5... | collective-permute-start | bytes 393224 | tf_op jit(solution)/shard_map/ppermute | solution.py:29
  29.4 6.2 %collective-permute-start.9 = (bf16[2,16,16,128]{3,2,1,0:T(8,128)(2,1)S(1)}, bf16[2,16,16,128]{3,2,1,0:T(8,128)(2,1)S(1)}, u32[]{:S(2)}, u32[]{:S(2)}) collective-permute-start(bf16[2,16,16,128]{3,2,1,0:T(8,128)(2,1)S(1)} %pad_maximum_fusion.1.refs_1_), channel_id=1, source_target_pairs={{0,4},{4,0},{8,12},{12,8},{16,20},{20,16},{24,28},{28,24},{1,5},{5... | collective-permute-start | bytes 393224 | tf_op jit(solution)/shard_map/ppermute | solution.py:29
  30.9 8.2 %collective-permute-start.15 = (bf16[2,16,16,128]{3,2,1,0:T(8,128)(2,1)S(1)}, bf16[2,16,16,128]{3,2,1,0:T(8,128)(2,1)S(1)}, u32[]{:S(2)}, u32[]{:S(2)}) collective-permute-start(bf16[2,16,16,128]{3,2,1,0:T(8,128)(2,1)S(1)} %collective-permute-done.5.refs_8_), channel_id=1, source_target_pairs={{0,4},{4,0},{8,12},{12,8},{16,20},{20,16},{24,28},{28,24},{1,5},{5... | collective-permute-start | bytes 393224 | tf_op jit(solution)/shard_map/ppermute | solution.py:29
  31.5 6.4 %collective-permute-start.13 = (bf16[2,16,16,128]{3,2,1,0:T(8,128)(2,1)S(1)}, bf16[2,16,16,128]{3,2,1,0:T(8,128)(2,1)S(1)}, u32[]{:S(2)}, u32[]{:S(2)}) collective-permute-start(bf16[2,16,16,128]{3,2,1,0:T(8,128)(2,1)S(1)} %collective-permute-done.5.refs_8_), channel_id=1, source_target_pairs={{0,8},{4,12},{8,0},{12,4},{16,24},{20,28},{24,16},{28,20},{1,9},{5... | collective-permute-start | bytes 393224 | tf_op jit(solution)/shard_map/ppermute | solution.py:29
  33.8 6.9 %collective-permute-start.7 = (bf16[2,16,16,128]{3,2,1,0:T(8,128)(2,1)S(1)}, bf16[2,16,16,128]{3,2,1,0:T(8,128)(2,1)S(1)}, u32[]{:S(2)}, u32[]{:S(2)}) collective-permute-start(bf16[2,16,16,128]{3,2,1,0:T(8,128)(2,1)S(1)} %collective-permute-done.6.refs_9_), channel_id=1, source_target_pairs={{0,8},{4,12},{8,0},{12,4},{16,24},{20,28},{24,16},{28,20},{1,9},{5... | collective-permute-start | bytes 393224 | tf_op jit(solution)/shard_map/ppermute | solution.py:29
  35.6 10.4 %collective-permute-start.12 = (bf16[2,16,16,128]{3,2,1,0:T(8,128)(2,1)S(1)}, bf16[2,16,16,128]{3,2,1,0:T(8,128)(2,1)S(1)}, u32[]{:S(2)}, u32[]{:S(2)}) collective-permute-start(bf16[2,16,16,128]{3,2,1,0:T(8,128)(2,1)S(1)} %collective-permute-done.8.refs_2_), channel_id=1, source_target_pairs={{0,8},{4,12},{8,0},{12,4},{16,24},{20,28},{24,16},{28,20},{1,9},{5... | collective-permute-start | bytes 393224 | tf_op jit(solution)/shard_map/ppermute | solution.py:29
  36.0 10.0 %collective-permute-start.16 = (bf16[2,16,16,128]{3,2,1,0:T(8,128)(2,1)S(1)}, bf16[2,16,16,128]{3,2,1,0:T(8,128)(2,1)S(1)}, u32[]{:S(2)}, u32[]{:S(2)}) collective-permute-start(bf16[2,16,16,128]{3,2,1,0:T(8,128)(2,1)S(1)} %collective-permute-done.6.refs_9_), channel_id=1, source_target_pairs={{0,4},{4,0},{8,12},{12,8},{16,20},{20,16},{24,28},{28,24},{1,5},{5... | collective-permute-start | bytes 393224 | tf_op jit(solution)/shard_map/ppermute | solution.py:29
  37.9 8.1 %collective-permute-start.14 = (bf16[2,16,16,128]{3,2,1,0:T(8,128)(2,1)S(1)}, bf16[2,16,16,128]{3,2,1,0:T(8,128)(2,1)S(1)}, u32[]{:S(2)}, u32[]{:S(2)}) collective-permute-start(bf16[2,16,16,128]{3,2,1,0:T(8,128)(2,1)S(1)} %collective-permute-done.9.refs_3_), channel_id=1, source_target_pairs={{0,8},{4,12},{8,0},{12,4},{16,24},{20,28},{24,16},{28,20},{1,9},{5... | collective-permute-start | bytes 393224 | tf_op jit(solution)/shard_map/ppermute | solution.py:29
  39.2 6.9 %collective-permute-start.17 = (bf16[2,16,16,128]{3,2,1,0:T(8,128)(2,1)S(1)}, bf16[2,16,16,128]{3,2,1,0:T(8,128)(2,1)S(1)}, u32[]{:S(2)}, u32[]{:S(2)}) collective-permute-start(bf16[2,16,16,128]{3,2,1,0:T(8,128)(2,1)S(1)} %collective-permute-done.13.refs_12_), channel_id=1, source_target_pairs={{0,4},{4,0},{8,12},{12,8},{16,20},{20,16},{24,28},{28,24},{1,5},{5... | collective-permute-start | bytes 393224 | tf_op jit(solution)/shard_map/ppermute | solution.py:29
  40.7 5.4 %collective-permute-start.18 = (bf16[2,16,16,128]{3,2,1,0:T(8,128)(2,1)S(1)}, bf16[2,16,16,128]{3,2,1,0:T(8,128)(2,1)S(1)}, u32[]{:S(2)}, u32[]{:S(2)}) collective-permute-start(bf16[2,16,16,128]{3,2,1,0:T(8,128)(2,1)S(1)} %collective-permute-done.7.refs_13_), channel_id=1, source_target_pairs={{0,4},{4,0},{8,12},{12,8},{16,20},{20,16},{24,28},{28,24},{1,5},{5... | collective-permute-start | bytes 393224 | tf_op jit(solution)/shard_map/ppermute | solution.py:29
  49.0 2.0 %collective-permute-start.19 = (bf16[128,2176]{1,0:T(8,128)(2,1)S(1)}, bf16[128,2176]{1,0:T(8,128)(2,1)S(1)}, u32[]{:S(2)}, u32[]{:S(2)}) collective-permute-start(bf16[128,2176]{1,0:T(8,128)(2,1)S(1)} %get-tuple-element.59), channel_id=1, source_target_pairs={{0,1},{1,0},{2,3},{3,2},{4,5},{5,4},{6,7},{7,6},{8,9},{9,8},{10,11... | collective-permute-start | bytes 1671176 | tf_op jit(solution)/shard_map/ppermute | solution.py:29
  51.2 14.7 %collective-permute-start.22 = (bf16[128,2176]{1,0:T(8,128)(2,1)S(1)}, bf16[128,2176]{1,0:T(8,128)(2,1)S(1)}, u32[]{:S(2)}, u32[]{:S(2)}) collective-permute-start(bf16[128,2176]{1,0:T(8,128)(2,1)S(1)} %join.1), channel_id=1, source_target_pairs={{0,2},{1,3},{2,0},{3,1},{4,6},{5,7},{6,4},{7,5},{8,10},{9,11},{10,... | collective-permute-start | bytes 1671176 | tf_op jit(solution)/shard_map/ppermute | solution.py:29
  55.6 1.6 %collective-permute-start.20 = (bf16[64,2176]{1,0:T(8,128)(2,1)S(1)}, bf16[64,2176]{1,0:T(8,128)(2,1)S(1)}, u32[]{:S(2)}, u32[]{:S(2)}) collective-permute-start(bf16[64,2176]{1,0:T(8,128)(2,1)S(1)} %get-tuple-element.62), channel_id=1, source_target_pairs={{0,1},{1,0},{2,3},{3,2},{4,5},{5,4},{6,7},{7,6},{8,9},{9,8},{10,11... | collective-permute-start | bytes 835592 | tf_op jit(solution)/shard_map/ppermute | solution.py:29
  55.7 1.9 %collective-permute-start.21 = (bf16[64,2176]{1,0:T(8,128)(2,1)S(1)}, bf16[64,2176]{1,0:T(8,128)(2,1)S(1)}, u32[]{:S(2)}, u32[]{:S(2)}) collective-permute-start(bf16[64,2176]{1,0:T(8,128)(2,1)S(1)} %get-tuple-element.63), channel_id=1, source_target_pairs={{0,1},{1,0},{2,3},{3,2},{4,5},{5,4},{6,7},{7,6},{8,9},{9,8},{10,11... | collective-permute-start | bytes 835592 | tf_op jit(solution)/shard_map/ppermute | solution.py:29

commit v8 on v7

--- a/solution.py
+++ b/solution.py
@@ -40,11 +40,11 @@
         far = [exchange(first, "wide", 4)]
         above = [exchange(first, "wide", 2)]
         beside = [exchange(first, "wide", 1)]
-        second = after(second, far[0])
+        waiting, second = second, after(second, far[0])
         far.append(exchange(second, "wide", 4))
         across = [exchange(far[0], "wide", 2)]
         far_beside = [exchange(after(far[0], beside[0], above[0]), "wide", 1)]
-        beside.append(exchange(second, "wide", 1))
+        beside.append(exchange(after(waiting, beside[0]), "wide", 1))
         above.append(exchange(second, "wide", 2))
         across.append(exchange(far[1], "wide", 2))
         far_beside.append(exchange(after(far[1], beside[1], above[1]), "wide", 1))

time: 67.3 us -> 67.3 us (level)
  transfers between devices with their start and end apart: 23 -> 23, of which waited for: 13 -> 12; matrix products, arithmetic and copies ran while one was open for 2% -> 2% of each run, Pallas kernels for 20% -> 20%
where the time goes in v8:
time: 67.3 us; the launch traced here: 67.1 us
  starting transfers between devices  23.6 us (35%)
  Pallas kernels  21.4 us (32%)
  waiting for transfers between devices  20.7 us (31%)
  local copies, waits for them, and re-layouts  1.01 us (2%)
    ppermute x23, starting transfers between devices, exchange(): return lax.ppermute(array, axis, [(i, i ^ bit) for i in range(count)])  23.6 us
    ppermute x23, waiting for transfers between devices, exchange(): return lax.ppermute(array, axis, [(i, i ^ bit) for i in range(count)])  20.7 us
    pallas_call x2, Pallas kernels, partial_scores(): pl.pallas_call(functools.partial(score_kernel, len(pieces), far), in_spec...  5.83 us
    pallas_call x1, Pallas kernels, column_squares(): pl.pallas_call(square_kernel, in_specs=[pl.BlockSpec(memory_space=pltpu.H...  3.77 us
    pallas_call x1, Pallas kernels, project_send(): pl.pallas_call(project_send_kernel, in_specs=[pl.BlockSpec(memory_space=p...  3.74 us
    pallas_call x1, Pallas kernels, stage(): pl.pallas_call(stage_kernel, in_specs=[pl.BlockSpec(memory_space=pltpu.HB...  3.39 us
    pallas_call x2, Pallas kernels, make_features(): pl.pallas_call(functools.partial(feature_kernel, first, core_programs, pr...  1.63 us
    pallas_call x1, Pallas kernels, project_keep(): pl.pallas_call(project_keep_kernel, in_specs=[vmem] * 5, out_specs=vmem,...  1.56 us
  transfers between devices with their start and end apart: 23, of which 12 were waited for; matrix products, arithmetic and copies ran while one was open for 2% of the time, Pallas kernels for 20%

profile of v8, /device:TPU:0, one launch (start us, length us, event | category | flops | bytes accessed | tf_op | source)
XLA Modules:
  0.0 67.1 jit_solution(16202395388071839115)
XLA Ops:
  0.0 3.7 %project_send.1 = (bf16[1536,128]{1,0:T(8,128)(2,1)S(1)}, bf16[1024,1024]{1,0:T(8,128)(2,1)S(1)}, bf16[1024,1024]{1,0:T(8,128)(2,1)S(1)}, bf16[1024,128]{1,0:T(8,128)(2,1)S(1)}, bf16[1024,128]{1,0:T(8,128)(2,1)S(1)}) custom-call(bf16[2048,1024]{1,0:T(8,128)(2,1)} %x_hbm.1, bf16[2048,1024]{1,0:T(8,128)(2,1)} %g_hbm.1, bf16[1024,128]{1,0:T(8,128)(2,1)} %w_hbm.1, ...), custom_call_target="tpu_custom_call" | custom-call | flops 536870912 | bytes 8388608 | tf_op jit(solution)/shard_map/project_send/pallas_call | solution.py:144
  3.7 0.5 collective-permute-start
  4.3 1.6 %project_keep.1.keep_ref = f32[1536,128]{1,0:T(8,128)S(1)} custom-call(bf16[1024,1024]{1,0:T(8,128)(2,1)S(1)} %get-tuple-element.36.x, bf16[1024,1024]{1,0:T(8,128)(2,1)S(1)} %get-tuple-element.37.g, bf16[1024,128]{1,0:T(8,128)(2,1)S(1)} %get-tuple-element.38.w, bf16[1024,128]{1,0:T(8,128)(2,1)S(1)} %get-tuple-element.39.up, bf16[64,128]{1,0:T(8,128)(2,1)S(1)} %bitcast.8), custom_call_target="tpu_custom_call" | custom-call | flops 536870912 | bytes 4194304 | tf_op jit(solution)/shard_map/project_keep/pallas_call | solution.py:171
  5.9 2.7 %collective-permute-start.1 = (bf16[640,128]{1,0:T(8,128)(2,1)S(1)}, bf16[640,128]{1,0:T(8,128)(2,1)S(1)}, u32[]{:S(2)}, u32[]{:S(2)}) collective-permute-start(bf16[640,128]{1,0:T(8,128)(2,1)S(1)} %get-tuple-element.42), channel_id=1, source_target_pairs={{0,2},{1,3},{2,0},{3,1},{4,6},{5,7},{6,4},{7,5},{8,10},{9,11},{10,... | collective-permute-start | bytes 491528 | tf_op jit(solution)/shard_map/ppermute | solution.py:29
  8.6 3.8 %squares.1.squares_ref = f32[128,128]{1,0:T(8,128)S(1)} custom-call(bf16[2048,2048]{1,0:T(8,128)(2,1)} %targets_hbm.1), custom_call_target="tpu_custom_call" | custom-call | flops 8388608 | bytes 8388608 | tf_op jit(solution)/shard_map/squares/pallas_call | solution.py:206
  12.4 0.1 collective-permute-start.3
  12.5 0.8 %collective-permute-done.1.came_ref = bf16[640,128]{1,0:T(8,128)(2,1)S(1)} collective-permute-done((bf16[640,128]{1,0:T(8,128)(2,1)S(1)}, bf16[640,128]{1,0:T(8,128)(2,1)S(1)}, u32[]{:S(2)}, u32[]{:S(2)}) %collective-permute-start.1) | collective-permute-done | bytes 163872 | tf_op jit(solution)/shard_map/ppermute | solution.py:29
  13.4 0.8 %features.2 = (bf16[16,16,128]{2,1,0:T(8,128)(2,1)S(1)}, bf16[16,16,128]{2,1,0:T(8,128)(2,1)S(1)}) custom-call(s32[64]{0:T(128)S(1)} %copy-done.1, f32[640,128]{1,0:T(8,128)S(1)} %get-tuple-element.46.left_ref, bf16[640,128]{1,0:T(8,128)(2,1)S(1)} %collective-permute-done.1.came_ref), custom_call_target="tpu_custom_call" | custom-call | flops 100000000 | bytes 655360 | tf_op jit(solution)/shard_map/features/pallas_call | solution.py:311
  14.3 1.2 %collective-permute-done.2 = bf16[16,16,128]{2,1,0:T(8,128)(2,1)S(1)} collective-permute-done((bf16[16,16,128]{2,1,0:T(8,128)(2,1)S(1)}, bf16[16,16,128]{2,1,0:T(8,128)(2,1)S(1)}, u32[]{:S(2)}, u32[]{:S(2)}) %collective-permute-start.2) | collective-permute-done | bytes 65568 | tf_op jit(solution)/shard_map/ppermute | solution.py:29
  15.5 2.9 %collective-permute-start.5 = (bf16[2,16,16,128]{3,2,1,0:T(8,128)(2,1)S(1)}, bf16[2,16,16,128]{3,2,1,0:T(8,128)(2,1)S(1)}, u32[]{:S(2)}, u32[]{:S(2)}) collective-permute-start(bf16[2,16,16,128]{3,2,1,0:T(8,128)(2,1)S(1)} %pad_maximum_fusion.refs_0_), channel_id=1, source_target_pairs={{0,16},{4,20},{8,24},{12,28},{16,0},{20,4},{24,8},{28,12},{1,17},{... | collective-permute-start | bytes 393224 | tf_op jit(solution)/shard_map/ppermute | solution.py:29
  18.4 0.3 collective-permute-done.3.came_ref
  18.7 0.8 %features.3 = (bf16[16,16,128]{2,1,0:T(8,128)(2,1)S(1)}, bf16[16,16,128]{2,1,0:T(8,128)(2,1)S(1)}) custom-call(s32[64]{0:T(128)S(1)} %copy-done.1, f32[640,128]{1,0:T(8,128)S(1)} %get-tuple-element.49.left_ref, bf16[640,128]{1,0:T(8,128)(2,1)S(1)} %collective-permute-done.3.came_ref), custom_call_target="tpu_custom_call" | custom-call | flops 100000000 | bytes 655360 | tf_op jit(solution)/shard_map/features/pallas_call | solution.py:311
  19.6 0.1 reshape.33
  19.7 0.6 gather_fusion
  20.3 1.6 %collective-permute-start.10 = (bf16[2,16,16,128]{3,2,1,0:T(8,128)(2,1)S(1)}, bf16[2,16,16,128]{3,2,1,0:T(8,128)(2,1)S(1)}, u32[]{:S(2)}, u32[]{:S(2)}) collective-permute-start(bf16[2,16,16,128]{3,2,1,0:T(8,128)(2,1)S(1)} %pad_maximum_fusion.refs_0_), channel_id=1, source_target_pairs={{0,8},{4,12},{8,0},{12,4},{16,24},{20,28},{24,16},{28,20},{1,9},{5... | collective-permute-start | bytes 393224 | tf_op jit(solution)/shard_map/ppermute | solution.py:29
  21.9 1.5 %collective-permute-start.8 = (bf16[2,16,16,128]{3,2,1,0:T(8,128)(2,1)S(1)}, bf16[2,16,16,128]{3,2,1,0:T(8,128)(2,1)S(1)}, u32[]{:S(2)}, u32[]{:S(2)}) collective-permute-start(bf16[2,16,16,128]{3,2,1,0:T(8,128)(2,1)S(1)} %pad_maximum_fusion.refs_0_), channel_id=1, source_target_pairs={{0,4},{4,0},{8,12},{12,8},{16,20},{20,16},{24,28},{28,24},{1,5},{5... | collective-permute-start | bytes 393224 | tf_op jit(solution)/shard_map/ppermute | solution.py:29
  23.5 1.7 %collective-permute-done.5.refs_8_ = bf16[2,16,16,128]{3,2,1,0:T(8,128)(2,1)S(1)} collective-permute-done((bf16[2,16,16,128]{3,2,1,0:T(8,128)(2,1)S(1)}, bf16[2,16,16,128]{3,2,1,0:T(8,128)(2,1)S(1)}, u32[]{:S(2)}, u32[]{:S(2)}) %collective-permute-start.5) | collective-permute-done | bytes 131104 | tf_op jit(solution)/shard_map/ppermute | solution.py:29
  25.1 1.0 %collective-permute-start.6 = (bf16[2,16,16,128]{3,2,1,0:T(8,128)(2,1)S(1)}, bf16[2,16,16,128]{3,2,1,0:T(8,128)(2,1)S(1)}, u32[]{:S(2)}, u32[]{:S(2)}) collective-permute-start(bf16[2,16,16,128]{3,2,1,0:T(8,128)(2,1)S(1)} %pad_maximum_fusion.1.refs_1_), channel_id=1, source_target_pairs={{0,16},{4,20},{8,24},{12,28},{16,0},{20,4},{24,8},{28,12},{1,17},{... | collective-permute-start | bytes 393224 | tf_op jit(solution)/shard_map/ppermute | solution.py:29
  26.2 3.2 %collective-permute-start.11 = (bf16[2,16,16,128]{3,2,1,0:T(8,128)(2,1)S(1)}, bf16[2,16,16,128]{3,2,1,0:T(8,128)(2,1)S(1)}, u32[]{:S(2)}, u32[]{:S(2)}) collective-permute-start(bf16[2,16,16,128]{3,2,1,0:T(8,128)(2,1)S(1)} %pad_maximum_fusion.1.refs_1_), channel_id=1, source_target_pairs={{0,8},{4,12},{8,0},{12,4},{16,24},{20,28},{24,16},{28,20},{1,9},{5... | collective-permute-start | bytes 393224 | tf_op jit(solution)/shard_map/ppermute | solution.py:29
  29.4 1.5 %collective-permute-start.9 = (bf16[2,16,16,128]{3,2,1,0:T(8,128)(2,1)S(1)}, bf16[2,16,16,128]{3,2,1,0:T(8,128)(2,1)S(1)}, u32[]{:S(2)}, u32[]{:S(2)}) collective-permute-start(bf16[2,16,16,128]{3,2,1,0:T(8,128)(2,1)S(1)} %pad_maximum_fusion.1.refs_1_), channel_id=1, source_target_pairs={{0,4},{4,0},{8,12},{12,8},{16,20},{20,16},{24,28},{28,24},{1,5},{5... | collective-permute-start | bytes 393224 | tf_op jit(solution)/shard_map/ppermute | solution.py:29
  31.0 0.5 collective-permute-start.15
  31.5 0.1 collective-permute-start.13
  31.5 2.3 %collective-permute-done.6.refs_9_ = bf16[2,16,16,128]{3,2,1,0:T(8,128)(2,1)S(1)} collective-permute-done((bf16[2,16,16,128]{3,2,1,0:T(8,128)(2,1)S(1)}, bf16[2,16,16,128]{3,2,1,0:T(8,128)(2,1)S(1)}, u32[]{:S(2)}, u32[]{:S(2)}) %collective-permute-start.6) | collective-permute-done | bytes 131104 | tf_op jit(solution)/shard_map/ppermute | solution.py:29
  33.8 0.1 broadcast_select_fusion.1
  33.9 1.7 %collective-permute-done.9.refs_3_ = bf16[2,16,16,128]{3,2,1,0:T(8,128)(2,1)S(1)} collective-permute-done((bf16[2,16,16,128]{3,2,1,0:T(8,128)(2,1)S(1)}, bf16[2,16,16,128]{3,2,1,0:T(8,128)(2,1)S(1)}, u32[]{:S(2)}, u32[]{:S(2)}) %collective-permute-start.9) | collective-permute-done | bytes 131104 | tf_op jit(solution)/shard_map/ppermute | solution.py:29
  35.6 0.4 collective-permute-start.12
  36.0 1.5 %collective-permute-start.16 = (bf16[2,16,16,128]{3,2,1,0:T(8,128)(2,1)S(1)}, bf16[2,16,16,128]{3,2,1,0:T(8,128)(2,1)S(1)}, u32[]{:S(2)}, u32[]{:S(2)}) collective-permute-start(bf16[2,16,16,128]{3,2,1,0:T(8,128)(2,1)S(1)} %collective-permute-done.6.refs_9_), channel_id=1, source_target_pairs={{0,4},{4,0},{8,12},{12,8},{16,20},{20,16},{24,28},{28,24},{1,5},{5... | collective-permute-start | bytes 393224 | tf_op jit(solution)/shard_map/ppermute | solution.py:29
  37.5 0.4 collective-permute-done.13.refs_12_
  37.9 1.3 %collective-permute-start.14 = (bf16[2,16,16,128]{3,2,1,0:T(8,128)(2,1)S(1)}, bf16[2,16,16,128]{3,2,1,0:T(8,128)(2,1)S(1)}, u32[]{:S(2)}, u32[]{:S(2)}) collective-permute-start(bf16[2,16,16,128]{3,2,1,0:T(8,128)(2,1)S(1)} %collective-permute-done.9.refs_3_), channel_id=1, source_target_pairs={{0,8},{4,12},{8,0},{12,4},{16,24},{20,28},{24,16},{28,20},{1,9},{5... | collective-permute-start | bytes 393224 | tf_op jit(solution)/shard_map/ppermute | solution.py:29
  39.2 0.9 %collective-permute-start.17 = (bf16[2,16,16,128]{3,2,1,0:T(8,128)(2,1)S(1)}, bf16[2,16,16,128]{3,2,1,0:T(8,128)(2,1)S(1)}, u32[]{:S(2)}, u32[]{:S(2)}) collective-permute-start(bf16[2,16,16,128]{3,2,1,0:T(8,128)(2,1)S(1)} %collective-permute-done.13.refs_12_), channel_id=1, source_target_pairs={{0,4},{4,0},{8,12},{12,8},{16,20},{20,16},{24,28},{28,24},{1,5},{5... | collective-permute-start | bytes 393224 | tf_op jit(solution)/shard_map/ppermute | solution.py:29
  40.1 0.6 collective-permute-done.7.refs_13_
  40.7 1.5 %collective-permute-start.18 = (bf16[2,16,16,128]{3,2,1,0:T(8,128)(2,1)S(1)}, bf16[2,16,16,128]{3,2,1,0:T(8,128)(2,1)S(1)}, u32[]{:S(2)}, u32[]{:S(2)}) collective-permute-start(bf16[2,16,16,128]{3,2,1,0:T(8,128)(2,1)S(1)} %collective-permute-done.7.refs_13_), channel_id=1, source_target_pairs={{0,4},{4,0},{8,12},{12,8},{16,20},{20,16},{24,28},{28,24},{1,5},{5... | collective-permute-start | bytes 393224 | tf_op jit(solution)/shard_map/ppermute | solution.py:29
  42.2 0.1 fusion.1
  42.3 0.1 reshape.34
  42.4 0.1 reshape.35
  42.5 0.1 pad_add_fusion
  42.5 0.1 reshape.36.order_ref
  42.6 3.4 %stage.1.targets_ref = bf16[2048,2048]{1,0:T(8,128)(2,1)S(1)} custom-call(bf16[2048,2048]{1,0:T(8,128)(2,1)} %targets_hbm.1), custom_call_target="tpu_custom_call" | custom-call | bytes 8388608 | tf_op jit(solution)/shard_map/stage/pallas_call | solution.py:228
  46.1 2.9 %scores_far.1 = (bf16[128,2176]{1,0:T(8,128)(2,1)S(1)}, bf16[128,2176]{1,0:T(8,128)(2,1)S(1)}) custom-call(s32[1,512]{1,0:T(1,128)S(1)} %reshape.36.order_ref, f32[128,128]{1,0:T(8,128)S(1)} %squares.1.squares_ref, bf16[2048,2048]{1,0:T(8,128)(2,1)S(1)} %stage.1.targets_ref, bf16[2,16,16,128]{3,2,1,0:T(8,128)(2,1)S(1)} %pad_maximum_fusion.refs_0_, ...), custom_call_target="tpu_custom_call" | custom-call | flops 2147483648 | bytes 8388608 | tf_op jit(solution)/shard_map/scores_far/pallas_call | solution.py:375
  49.1 1.9 %collective-permute-done.19.came_ref = bf16[128,2176]{1,0:T(8,128)(2,1)S(1)} collective-permute-done((bf16[128,2176]{1,0:T(8,128)(2,1)S(1)}, bf16[128,2176]{1,0:T(8,128)(2,1)S(1)}, u32[]{:S(2)}, u32[]{:S(2)}) %collective-permute-start.19) | collective-permute-done | bytes 557088 | tf_op jit(solution)/shard_map/ppermute | solution.py:29
  51.0 0.1 join.1
  51.1 1.6 %collective-permute-start.22 = (bf16[128,2176]{1,0:T(8,128)(2,1)S(1)}, bf16[128,2176]{1,0:T(8,128)(2,1)S(1)}, u32[]{:S(2)}, u32[]{:S(2)}) collective-permute-start(bf16[128,2176]{1,0:T(8,128)(2,1)S(1)} %join.1), channel_id=1, source_target_pairs={{0,2},{1,3},{2,0},{3,1},{4,6},{5,7},{6,4},{7,5},{8,10},{9,11},{10,... | collective-permute-start | bytes 1671176 | tf_op jit(solution)/shard_map/ppermute | solution.py:29
  52.7 2.9 %scores_near.1 = (bf16[64,2176]{1,0:T(8,128)(2,1)S(1)}, bf16[64,2176]{1,0:T(8,128)(2,1)S(1)}, bf16[128,2176]{1,0:T(8,128)(2,1)S(1)}) custom-call(s32[1,512]{1,0:T(1,128)S(1)} %reshape.36.order_ref, f32[128,128]{1,0:T(8,128)S(1)} %squares.1.squares_ref, bf16[2048,2048]{1,0:T(8,128)(2,1)S(1)} %stage.1.targets_ref, ...), custom_call_target="tpu_custom_call" | custom-call | flops 2147483648 | bytes 8388608 | tf_op jit(solution)/shard_map/scores_near/pallas_call | solution.py:375
  55.7 0.5 collective-permute-start.21
  56.2 1.0 %collective-permute-done.20.low_ref = bf16[64,2176]{1,0:T(8,128)(2,1)S(1)} collective-permute-done((bf16[64,2176]{1,0:T(8,128)(2,1)S(1)}, bf16[64,2176]{1,0:T(8,128)(2,1)S(1)}, u32[]{:S(2)}, u32[]{:S(2)}) %collective-permute-start.20) | collective-permute-done | bytes 278560 | tf_op jit(solution)/shard_map/ppermute | solution.py:29
  57.3 0.4 collective-permute-done.21.high_ref
  57.7 8.2 %collective-permute-done.22.far_ref = bf16[128,2176]{1,0:T(8,128)(2,1)S(1)} collective-permute-done((bf16[128,2176]{1,0:T(8,128)(2,1)S(1)}, bf16[128,2176]{1,0:T(8,128)(2,1)S(1)}, u32[]{:S(2)}, u32[]{:S(2)}) %collective-permute-start.22) | collective-permute-done | bytes 557088 | tf_op jit(solution)/shard_map/ppermute | solution.py:29
  65.9 1.2 %finish.1 = f32[128,2048]{1,0:T(8,128)} custom-call(bf16[128,2176]{1,0:T(8,128)(2,1)S(1)} %get-tuple-element.63.keep_ref, bf16[64,2176]{1,0:T(8,128)(2,1)S(1)} %collective-permute-done.20.low_ref, bf16[64,2176]{1,0:T(8,128)(2,1)S(1)} %collective-permute-done.21.high_ref, bf16[128,2176]{1,0:T(8,128)(2,1)S(1)} %collective-permute-done.22.far_ref), custom_call_target="tpu_custom_call" | custom-call | flops 1048576 | bytes 2621440 | tf_op jit(solution)/shard_map/finish/pallas_call | solution.py:426
  (30 shorter events, 0.6 us)
Async XLA Ops:
  0.0 4.3 %copy-start = (bf16[128,64]{0,1:T(8,128)(2,1)S(1)}, bf16[128,64]{0,1:T(8,128)(2,1)}, u32[]{:S(2)}) copy-start(bf16[128,64]{0,1:T(8,128)(2,1)} %param.12) | copy-start | bytes 49156
  3.7 2.1 %collective-permute-start = (bf16[1536,128]{1,0:T(8,128)(2,1)S(1)}, bf16[1536,128]{1,0:T(8,128)(2,1)S(1)}, u32[]{:S(2)}, u32[]{:S(2)}) collective-permute-start(bf16[1536,128]{1,0:T(8,128)(2,1)S(1)} %get-tuple-element.40), channel_id=1, source_target_pairs={{0,1},{1,0},{2,3},{3,2},{4,5},{5,4},{6,7},{7,6},{8,9},{9,8},{10,11... | collective-permute-start | bytes 1179656 | tf_op jit(solution)/shard_map/ppermute | solution.py:29
  5.9 7.4 %collective-permute-start.1 = (bf16[640,128]{1,0:T(8,128)(2,1)S(1)}, bf16[640,128]{1,0:T(8,128)(2,1)S(1)}, u32[]{:S(2)}, u32[]{:S(2)}) collective-permute-start(bf16[640,128]{1,0:T(8,128)(2,1)S(1)} %get-tuple-element.42), channel_id=1, source_target_pairs={{0,2},{1,3},{2,0},{3,1},{4,6},{5,7},{6,4},{7,5},{8,10},{9,11},{10,... | collective-permute-start | bytes 491528 | tf_op jit(solution)/shard_map/ppermute | solution.py:29
  8.6 4.7 %copy-start.1 = (s32[64]{0:T(128)S(1)}, s32[64]{0:T(128)}, u32[]{:S(2)}) copy-start(s32[64]{0:T(128)} %lengths.3) | copy-start | bytes 772
  8.6 11.0 %copy-start.2 = (s32[512]{0:T(512)S(1)}, s32[512]{0:T(512)}, u32[]{:S(2)}) copy-start(s32[512]{0:T(512)} %param.14) | copy-start | bytes 6148
  12.4 6.2 %collective-permute-start.3 = (bf16[640,128]{1,0:T(8,128)(2,1)S(1)}, bf16[640,128]{1,0:T(8,128)(2,1)S(1)}, u32[]{:S(2)}, u32[]{:S(2)}) collective-permute-start(bf16[640,128]{1,0:T(8,128)(2,1)S(1)} %get-tuple-element.50), channel_id=1, source_target_pairs={{0,2},{1,3},{2,0},{3,1},{4,6},{5,7},{6,4},{7,5},{8,10},{9,11},{10,... | collective-permute-start | bytes 491528 | tf_op jit(solution)/shard_map/ppermute | solution.py:29
  14.2 1.3 %collective-permute-start.2 = (bf16[16,16,128]{2,1,0:T(8,128)(2,1)S(1)}, bf16[16,16,128]{2,1,0:T(8,128)(2,1)S(1)}, u32[]{:S(2)}, u32[]{:S(2)}) collective-permute-start(bf16[16,16,128]{2,1,0:T(8,128)(2,1)S(1)} %get-tuple-element.48), channel_id=1, source_target_pairs={{0,1},{1,0},{2,3},{3,2},{4,5},{5,4},{6,7},{7,6},{8,9},{9,8},{10,11... | collective-permute-start | bytes 196616 | tf_op jit(solution)/shard_map/ppermute | solution.py:29
  15.5 9.6 %collective-permute-start.5 = (bf16[2,16,16,128]{3,2,1,0:T(8,128)(2,1)S(1)}, bf16[2,16,16,128]{3,2,1,0:T(8,128)(2,1)S(1)}, u32[]{:S(2)}, u32[]{:S(2)}) collective-permute-start(bf16[2,16,16,128]{3,2,1,0:T(8,128)(2,1)S(1)} %pad_maximum_fusion.refs_0_), channel_id=1, source_target_pairs={{0,16},{4,20},{8,24},{12,28},{16,0},{20,4},{24,8},{28,12},{1,17},{... | collective-permute-start | bytes 393224 | tf_op jit(solution)/shard_map/ppermute | solution.py:29
  19.5 3.9 %collective-permute-start.4 = (bf16[16,16,128]{2,1,0:T(8,128)(2,1)S(1)}, bf16[16,16,128]{2,1,0:T(8,128)(2,1)S(1)}, u32[]{:S(2)}, u32[]{:S(2)}) collective-permute-start(bf16[16,16,128]{2,1,0:T(8,128)(2,1)S(1)} %get-tuple-element.52), channel_id=1, source_target_pairs={{0,1},{1,0},{2,3},{3,2},{4,5},{5,4},{6,7},{7,6},{8,9},{9,8},{10,11... | collective-permute-start | bytes 196616 | tf_op jit(solution)/shard_map/ppermute | solution.py:29
  20.3 10.7 %collective-permute-start.10 = (bf16[2,16,16,128]{3,2,1,0:T(8,128)(2,1)S(1)}, bf16[2,16,16,128]{3,2,1,0:T(8,128)(2,1)S(1)}, u32[]{:S(2)}, u32[]{:S(2)}) collective-permute-start(bf16[2,16,16,128]{3,2,1,0:T(8,128)(2,1)S(1)} %pad_maximum_fusion.refs_0_), channel_id=1, source_target_pairs={{0,8},{4,12},{8,0},{12,4},{16,24},{20,28},{24,16},{28,20},{1,9},{5... | collective-permute-start | bytes 393224 | tf_op jit(solution)/shard_map/ppermute | solution.py:29
  21.9 7.5 %collective-permute-start.8 = (bf16[2,16,16,128]{3,2,1,0:T(8,128)(2,1)S(1)}, bf16[2,16,16,128]{3,2,1,0:T(8,128)(2,1)S(1)}, u32[]{:S(2)}, u32[]{:S(2)}) collective-permute-start(bf16[2,16,16,128]{3,2,1,0:T(8,128)(2,1)S(1)} %pad_maximum_fusion.refs_0_), channel_id=1, source_target_pairs={{0,4},{4,0},{8,12},{12,8},{16,20},{20,16},{24,28},{28,24},{1,5},{5... | collective-permute-start | bytes 393224 | tf_op jit(solution)/shard_map/ppermute | solution.py:29
  25.1 8.7 %collective-permute-start.6 = (bf16[2,16,16,128]{3,2,1,0:T(8,128)(2,1)S(1)}, bf16[2,16,16,128]{3,2,1,0:T(8,128)(2,1)S(1)}, u32[]{:S(2)}, u32[]{:S(2)}) collective-permute-start(bf16[2,16,16,128]{3,2,1,0:T(8,128)(2,1)S(1)} %pad_maximum_fusion.1.refs_1_), channel_id=1, source_target_pairs={{0,16},{4,20},{8,24},{12,28},{16,0},{20,4},{24,8},{28,12},{1,17},{... | collective-permute-start | bytes 393224 | tf_op jit(solution)/shard_map/ppermute | solution.py:29
  26.2 9.4 %collective-permute-start.11 = (bf16[2,16,16,128]{3,2,1,0:T(8,128)(2,1)S(1)}, bf16[2,16,16,128]{3,2,1,0:T(8,128)(2,1)S(1)}, u32[]{:S(2)}, u32[]{:S(2)}) collective-permute-start(bf16[2,16,16,128]{3,2,1,0:T(8,128)(2,1)S(1)} %pad_maximum_fusion.1.refs_1_), channel_id=1, source_target_pairs={{0,8},{4,12},{8,0},{12,4},{16,24},{20,28},{24,16},{28,20},{1,9},{5... | collective-permute-start | bytes 393224 | tf_op jit(solution)/shard_map/ppermute | solution.py:29
  29.4 6.2 %collective-permute-start.9 = (bf16[2,16,16,128]{3,2,1,0:T(8,128)(2,1)S(1)}, bf16[2,16,16,128]{3,2,1,0:T(8,128)(2,1)S(1)}, u32[]{:S(2)}, u32[]{:S(2)}) collective-permute-start(bf16[2,16,16,128]{3,2,1,0:T(8,128)(2,1)S(1)} %pad_maximum_fusion.1.refs_1_), channel_id=1, source_target_pairs={{0,4},{4,0},{8,12},{12,8},{16,20},{20,16},{24,28},{28,24},{1,5},{5... | collective-permute-start | bytes 393224 | tf_op jit(solution)/shard_map/ppermute | solution.py:29
  31.0 8.2 %collective-permute-start.15 = (bf16[2,16,16,128]{3,2,1,0:T(8,128)(2,1)S(1)}, bf16[2,16,16,128]{3,2,1,0:T(8,128)(2,1)S(1)}, u32[]{:S(2)}, u32[]{:S(2)}) collective-permute-start(bf16[2,16,16,128]{3,2,1,0:T(8,128)(2,1)S(1)} %collective-permute-done.5.refs_8_), channel_id=1, source_target_pairs={{0,4},{4,0},{8,12},{12,8},{16,20},{20,16},{24,28},{28,24},{1,5},{5... | collective-permute-start | bytes 393224 | tf_op jit(solution)/shard_map/ppermute | solution.py:29
  31.5 6.4 %collective-permute-start.13 = (bf16[2,16,16,128]{3,2,1,0:T(8,128)(2,1)S(1)}, bf16[2,16,16,128]{3,2,1,0:T(8,128)(2,1)S(1)}, u32[]{:S(2)}, u32[]{:S(2)}) collective-permute-start(bf16[2,16,16,128]{3,2,1,0:T(8,128)(2,1)S(1)} %collective-permute-done.5.refs_8_), channel_id=1, source_target_pairs={{0,8},{4,12},{8,0},{12,4},{16,24},{20,28},{24,16},{28,20},{1,9},{5... | collective-permute-start | bytes 393224 | tf_op jit(solution)/shard_map/ppermute | solution.py:29
  33.8 6.9 %collective-permute-start.7 = (bf16[2,16,16,128]{3,2,1,0:T(8,128)(2,1)S(1)}, bf16[2,16,16,128]{3,2,1,0:T(8,128)(2,1)S(1)}, u32[]{:S(2)}, u32[]{:S(2)}) collective-permute-start(bf16[2,16,16,128]{3,2,1,0:T(8,128)(2,1)S(1)} %collective-permute-done.6.refs_9_), channel_id=1, source_target_pairs={{0,8},{4,12},{8,0},{12,4},{16,24},{20,28},{24,16},{28,20},{1,9},{5... | collective-permute-start | bytes 393224 | tf_op jit(solution)/shard_map/ppermute | solution.py:29
  35.6 10.4 %collective-permute-start.12 = (bf16[2,16,16,128]{3,2,1,0:T(8,128)(2,1)S(1)}, bf16[2,16,16,128]{3,2,1,0:T(8,128)(2,1)S(1)}, u32[]{:S(2)}, u32[]{:S(2)}) collective-permute-start(bf16[2,16,16,128]{3,2,1,0:T(8,128)(2,1)S(1)} %collective-permute-done.8.refs_2_), channel_id=1, source_target_pairs={{0,8},{4,12},{8,0},{12,4},{16,24},{20,28},{24,16},{28,20},{1,9},{5... | collective-permute-start | bytes 393224 | tf_op jit(solution)/shard_map/ppermute | solution.py:29
  36.0 10.0 %collective-permute-start.16 = (bf16[2,16,16,128]{3,2,1,0:T(8,128)(2,1)S(1)}, bf16[2,16,16,128]{3,2,1,0:T(8,128)(2,1)S(1)}, u32[]{:S(2)}, u32[]{:S(2)}) collective-permute-start(bf16[2,16,16,128]{3,2,1,0:T(8,128)(2,1)S(1)} %collective-permute-done.6.refs_9_), channel_id=1, source_target_pairs={{0,4},{4,0},{8,12},{12,8},{16,20},{20,16},{24,28},{28,24},{1,5},{5... | collective-permute-start | bytes 393224 | tf_op jit(solution)/shard_map/ppermute | solution.py:29
  37.9 8.1 %collective-permute-start.14 = (bf16[2,16,16,128]{3,2,1,0:T(8,128)(2,1)S(1)}, bf16[2,16,16,128]{3,2,1,0:T(8,128)(2,1)S(1)}, u32[]{:S(2)}, u32[]{:S(2)}) collective-permute-start(bf16[2,16,16,128]{3,2,1,0:T(8,128)(2,1)S(1)} %collective-permute-done.9.refs_3_), channel_id=1, source_target_pairs={{0,8},{4,12},{8,0},{12,4},{16,24},{20,28},{24,16},{28,20},{1,9},{5... | collective-permute-start | bytes 393224 | tf_op jit(solution)/shard_map/ppermute | solution.py:29
  39.2 6.9 %collective-permute-start.17 = (bf16[2,16,16,128]{3,2,1,0:T(8,128)(2,1)S(1)}, bf16[2,16,16,128]{3,2,1,0:T(8,128)(2,1)S(1)}, u32[]{:S(2)}, u32[]{:S(2)}) collective-permute-start(bf16[2,16,16,128]{3,2,1,0:T(8,128)(2,1)S(1)} %collective-permute-done.13.refs_12_), channel_id=1, source_target_pairs={{0,4},{4,0},{8,12},{12,8},{16,20},{20,16},{24,28},{28,24},{1,5},{5... | collective-permute-start | bytes 393224 | tf_op jit(solution)/shard_map/ppermute | solution.py:29
  40.7 5.3 %collective-permute-start.18 = (bf16[2,16,16,128]{3,2,1,0:T(8,128)(2,1)S(1)}, bf16[2,16,16,128]{3,2,1,0:T(8,128)(2,1)S(1)}, u32[]{:S(2)}, u32[]{:S(2)}) collective-permute-start(bf16[2,16,16,128]{3,2,1,0:T(8,128)(2,1)S(1)} %collective-permute-done.7.refs_13_), channel_id=1, source_target_pairs={{0,4},{4,0},{8,12},{12,8},{16,20},{20,16},{24,28},{28,24},{1,5},{5... | collective-permute-start | bytes 393224 | tf_op jit(solution)/shard_map/ppermute | solution.py:29
  49.0 2.0 %collective-permute-start.19 = (bf16[128,2176]{1,0:T(8,128)(2,1)S(1)}, bf16[128,2176]{1,0:T(8,128)(2,1)S(1)}, u32[]{:S(2)}, u32[]{:S(2)}) collective-permute-start(bf16[128,2176]{1,0:T(8,128)(2,1)S(1)} %get-tuple-element.61), channel_id=1, source_target_pairs={{0,1},{1,0},{2,3},{3,2},{4,5},{5,4},{6,7},{7,6},{8,9},{9,8},{10,11... | collective-permute-start | bytes 1671176 | tf_op jit(solution)/shard_map/ppermute | solution.py:29
  51.1 14.7 %collective-permute-start.22 = (bf16[128,2176]{1,0:T(8,128)(2,1)S(1)}, bf16[128,2176]{1,0:T(8,128)(2,1)S(1)}, u32[]{:S(2)}, u32[]{:S(2)}) collective-permute-start(bf16[128,2176]{1,0:T(8,128)(2,1)S(1)} %join.1), channel_id=1, source_target_pairs={{0,2},{1,3},{2,0},{3,1},{4,6},{5,7},{6,4},{7,5},{8,10},{9,11},{10,... | collective-permute-start | bytes 1671176 | tf_op jit(solution)/shard_map/ppermute | solution.py:29
  55.6 1.6 %collective-permute-start.20 = (bf16[64,2176]{1,0:T(8,128)(2,1)S(1)}, bf16[64,2176]{1,0:T(8,128)(2,1)S(1)}, u32[]{:S(2)}, u32[]{:S(2)}) collective-permute-start(bf16[64,2176]{1,0:T(8,128)(2,1)S(1)} %get-tuple-element.64), channel_id=1, source_target_pairs={{0,1},{1,0},{2,3},{3,2},{4,5},{5,4},{6,7},{7,6},{8,9},{9,8},{10,11... | collective-permute-start | bytes 835592 | tf_op jit(solution)/shard_map/ppermute | solution.py:29
  55.7 1.9 %collective-permute-start.21 = (bf16[64,2176]{1,0:T(8,128)(2,1)S(1)}, bf16[64,2176]{1,0:T(8,128)(2,1)S(1)}, u32[]{:S(2)}, u32[]{:S(2)}) collective-permute-start(bf16[64,2176]{1,0:T(8,128)(2,1)S(1)} %get-tuple-element.65), channel_id=1, source_target_pairs={{0,1},{1,0},{2,3},{3,2},{4,5},{5,4},{6,7},{7,6},{8,9},{9,8},{10,11... | collective-permute-start | bytes 835592 | tf_op jit(solution)/shard_map/ppermute | solution.py:29
